TPU v7x, 32 devices: a whole 2x2x4 slice. The times are simulated.
32 devices in a mesh: dp: 4 (over y, core), fsdp: 8 (over z, x).
Axes of the slice: x: 2, y: 2, z: 4, core: 2. Of those that a mesh axis runs over, the one named last changes fastest.
Arguments:
- x_source: bfloat16 [2, 16384, 1024], P(None, ('dp', 'fsdp')), may hold values from -8 to 8
- skip_source: bfloat16 [2, 16384, 1024], P(None, ('dp', 'fsdp')), may hold values from -8 to 8
- out_cotangent: bfloat16 [2, 8192, 1024], P(None, ('dp', 'fsdp')), may hold values from -6 to 6
- item_length: int32 [8, 2, 4, 4], P('fsdp'), may hold values from 1 to 128, as said below
- item_pack: int32 [8, 2, 4, 4], P('fsdp'), may hold values from 0 to 3, as said below
- item_offset: int32 [8, 2, 4, 4], P('fsdp'), may hold values from 0 to 255, as said below
- item_count: int32 [8, 2, 4, 4], P('fsdp'), may hold values from 1 to 128, as said below
- gains: float32 [2, 1024], P(None, 'fsdp'), may hold values from 0.3 to 2.4
- w_skip: float32 [2048, 1024], P('fsdp'), may hold values from -0.125 to 0.125
- w_qkv: float32 [1024, 3072], P('fsdp'), may hold values from -0.1875 to 0.1875
- w_out: float32 [1024, 1024], P('fsdp'), may hold values from -0.75 to 0.75
- w_up: float32 [1024, 4096], P('fsdp'), may hold values from -0.1875 to 0.1875
- w_down: float32 [4096, 1024], P('fsdp'), may hold values from -0.09375 to 0.09375
- gains_first: float32 [2, 1024], P(None, 'fsdp'), may hold values from -0.12 to 0.12
- first_skip: float32 [2048, 1024], P('fsdp'), may hold values from -0.12 to 0.12
- first_qkv: float32 [1024, 3072], P('fsdp'), may hold values from -0.12 to 0.12
- first_out: float32 [1024, 1024], P('fsdp'), may hold values from -0.12 to 0.12
- first_up: float32 [1024, 4096], P('fsdp'), may hold values from -0.12 to 0.12
- first_down: float32 [4096, 1024], P('fsdp'), may hold values from -0.12 to 0.12
- gains_second: float32 [2, 1024], P(None, 'fsdp'), may hold values from 0.0004 to 0.0016
- second_skip: float32 [2048, 1024], P('fsdp'), may hold values from 0.0004 to 0.0016
- second_qkv: float32 [1024, 3072], P('fsdp'), may hold values from 0.0004 to 0.0016
- second_out: float32 [1024, 1024], P('fsdp'), may hold values from 3e-05 to 0.00012
- second_up: float32 [1024, 4096], P('fsdp'), may hold values from 3e-05 to 0.00012
- second_down: float32 [4096, 1024], P('fsdp'), may hold values from 0.0004 to 0.0016
Outputs:
- out_frames: bfloat16 [2, 8192, 1024], P(None, ('dp', 'fsdp'))
- input_gradient: bfloat16 [2, 16384, 1024], P(None, ('dp', 'fsdp'))
- skip_gradient: bfloat16 [2, 16384, 1024], P(None, ('dp', 'fsdp'))
- gradient_norm: float32 [1], replicated
- gains_new: float32 [2, 1024], P(None, 'fsdp')
- gains_first_new: float32 [2, 1024], P(None, 'fsdp')
- gains_second_new: float32 [2, 1024], P(None, 'fsdp')
- skip_new: float32 [2048, 1024], P('fsdp')
- skip_first_new: float32 [2048, 1024], P('fsdp')
- skip_second_new: float32 [2048, 1024], P('fsdp')
- skip_copy: bfloat16 [2048, 1024], P('fsdp')
- qkv_new: float32 [1024, 3072], P('fsdp')
- qkv_first_new: float32 [1024, 3072], P('fsdp')
- qkv_second_new: float32 [1024, 3072], P('fsdp')
- qkv_copy: bfloat16 [1024, 3072], P('fsdp')
- out_new: float32 [1024, 1024], P('fsdp')
- out_first_new: float32 [1024, 1024], P('fsdp')
- out_second_new: float32 [1024, 1024], P('fsdp')
- out_copy: bfloat16 [1024, 1024], P('fsdp')
- up_new: float32 [1024, 4096], P('fsdp')
- up_first_new: float32 [1024, 4096], P('fsdp')
- up_second_new: float32 [1024, 4096], P('fsdp')
- up_copy: bfloat16 [1024, 4096], P('fsdp')
- down_new: float32 [4096, 1024], P('fsdp')
- down_first_new: float32 [4096, 1024], P('fsdp')
- down_second_new: float32 [4096, 1024], P('fsdp')
- down_copy: bfloat16 [4096, 1024], P('fsdp')
Inputs may be any that keep to these rules, and one draw needn't show every extreme that they name: `item_length`: each source shard holds its utterances in slot order from its first row; in every group and micro-batch one source shard holds exactly 512 frames, every pack receives exactly 256 frames, and the longest utterance has exactly 128 frames. `item_pack`: each source shard sends exactly one utterance to each pack of its group. `item_offset`: the utterances of a pack tile its 256 rows without gaps. `item_count`: at most the utterance's length; in group 0 and micro-batch 0 every utterance of 128 frames has all 128 frames counted.
All inputs are finite; a program needn't handle non-finite values.
Results may differ from a plain program's by a relative error of at most 0.025.
Values may be sent and summed in bfloat16 or wider, within the bound.
A program may use at most 320 MiB of HBM per device.

v0:
```python
from functools import partial
import math

import jax
import jax.numpy as jnp
from jax import lax
from jax.sharding import PartitionSpec as P

D = 1024
HEADS = 16
HD = 64
FF = 4096
STEP = 5


BETA_FIRST = 0.5
BETA_SECOND = 0.5
ADAM_EPSILON = 1e-08
WEIGHT_DECAY = 0.01
NORM_EPSILON = 1e-05


def norm_rows(hidden, gain_row):
    centre = hidden - jnp.mean(hidden, axis=-1, keepdims=True)
    spread = jnp.mean(centre * centre, axis=-1, keepdims=True)
    return centre * lax.rsqrt(spread + NORM_EPSILON) * gain_row


def alibi_bias(length):
    position = jnp.arange(length, dtype=jnp.float32)
    distance = jnp.abs(position[:, None] - position[None, :])
    slopes = jnp.exp2(-8.0 * (jnp.arange(HEADS, dtype=jnp.float32) + 1.0) / HEADS)
    return -slopes[:, None, None] * distance[None]


def dot_rows(left, right):
    return jnp.dot(left, right, preferred_element_type=jnp.float32)


def dot_left(left, right):
    return lax.dot_general(
        left, right, (((0,), (0,)), ((), ())), preferred_element_type=jnp.float32
    )


def dot_right(left, right):
    return lax.dot_general(
        left, right, (((1,), (1,)), ((), ())), preferred_element_type=jnp.float32
    )


def masked_scores(queries, keys_all, alibi_terms, same_item):
    scores = (
        jnp.einsum("qhe,khe->hqk", queries, keys_all, preferred_element_type=jnp.float32)
        * HD ** (-0.5)
        + alibi_terms
    )
    return jnp.where(same_item[None], scores, -1e30)


def gather_rows(table, indices, filled, out_shape):
    picked = jnp.take(table, indices, axis=0)
    return jnp.where(filled, picked, jnp.zeros_like(picked)).reshape(out_shape)


def send_plan(lengths, packs, dp_count, capacity):
    starts = jnp.cumsum(lengths) - lengths
    matches = packs[None, :] == jnp.arange(dp_count, dtype=jnp.int32)[:, None]
    length_to = jnp.sum(jnp.where(matches, lengths[None, :], 0), axis=1)
    start_to = jnp.sum(jnp.where(matches, starts[None, :], 0), axis=1)
    slot_index = jnp.arange(capacity, dtype=jnp.int32)
    filled = slot_index[None, :] < length_to[:, None]
    indices = jnp.where(filled, start_to[:, None] + slot_index[None, :], 0)
    return (indices.reshape(-1), filled.reshape(-1, 1))


def pack_plan(lengths, packs, offsets, counts, own_index, dp_count, capacity, row_count):
    matches = packs == own_index

    def chosen(values):
        return jnp.sum(jnp.where(matches, values, 0), axis=1)

    length_from, offset_from, count_from = (chosen(lengths), chosen(offsets), chosen(counts))
    position = jnp.arange(row_count, dtype=jnp.int32)
    inside = (position[:, None] >= offset_from[None, :]) & (
        position[:, None] < (offset_from + length_from)[None, :]
    )

    def select(values):
        return jnp.sum(jnp.where(inside, values[None, :], 0), axis=1)

    source = select(jnp.arange(dp_count, dtype=jnp.int32))
    indices = source * capacity + position - select(offset_from)
    weight = select(count_from).astype(jnp.float32) / select(length_from).astype(jnp.float32)
    slot_index = jnp.arange(capacity, dtype=jnp.int32)
    back_filled = slot_index[None, :] < length_from[:, None]
    back_indices = jnp.where(back_filled, offset_from[:, None] + slot_index[None, :], 0)
    return (source, indices, weight, back_indices.reshape(-1), back_filled.reshape(-1, 1))


def return_plan(lengths, packs, capacity, source_rows):
    starts = jnp.cumsum(lengths) - lengths
    position = jnp.arange(source_rows, dtype=jnp.int32)
    inside = (position[:, None] >= starts[None, :]) & (
        position[:, None] < (starts + lengths)[None, :]
    )
    pack_of = jnp.sum(jnp.where(inside, packs[None, :], 0), axis=1)
    first_row = jnp.sum(jnp.where(inside, starts[None, :], 0), axis=1)
    filled = jnp.any(inside, axis=1)
    indices = jnp.where(filled, pack_of * capacity + position - first_row, 0)
    return (indices, filled[:, None])


def micro_step(weights, x_rows, skip_rows, cotangent, lengths, packs, offsets, counts):
    used_skip, used_qkv, used_out, used_up, used_down, used_gains = weights
    dp_count = lax.axis_size("dp")
    own_index = lax.axis_index("dp")
    source_rows = x_rows.shape[0]
    capacity = source_rows // dp_count
    row_count = cotangent.shape[0]
    width = cotangent.shape[1]
    own_lengths = lengths[own_index]
    own_packs = packs[own_index]
    send_indices, send_filled = send_plan(own_lengths, own_packs, dp_count, capacity)
    buffer_shape = (dp_count, capacity, width)
    x_outgoing = gather_rows(x_rows, send_indices, send_filled, buffer_shape)
    skip_outgoing = gather_rows(skip_rows, send_indices, send_filled, buffer_shape)
    x_arrived, skip_arrived = (
        lax.all_to_all(x_outgoing, "dp", split_axis=0, concat_axis=0, tiled=True),
        lax.all_to_all(skip_outgoing, "dp", split_axis=0, concat_axis=0, tiled=True),
    )
    source, pack_indices, frame_weight, back_indices, back_filled = pack_plan(
        lengths, packs, offsets, counts, own_index, dp_count, capacity, row_count
    )
    packed = jnp.concatenate(
        [
            jnp.take(x_arrived.reshape(-1, width), pack_indices, axis=0),
            jnp.take(skip_arrived.reshape(-1, width), pack_indices, axis=0),
        ],
        axis=1,
    )
    gain_one = used_gains[0].astype(jnp.float32)
    gain_two = used_gains[1].astype(jnp.float32)
    base_rows = dot_rows(packed, used_skip)
    normed_one, norm_one_back = jax.vjp(norm_rows, base_rows, gain_one)
    normed_one = normed_one.astype(jnp.bfloat16)
    qkv_rows = dot_rows(normed_one, used_qkv).astype(jnp.bfloat16)
    heads_shape = (row_count, HEADS, HD)
    queries = qkv_rows[:, :width].reshape(heads_shape)
    keys_all = qkv_rows[:, width : 2 * width].reshape(heads_shape)
    values_all = qkv_rows[:, 2 * width :].reshape(heads_shape)
    alibi_terms = alibi_bias(row_count)
    same_item = source[:, None] == source[None, :]
    scores = masked_scores(queries, keys_all, alibi_terms, same_item)
    row_peak = jnp.max(scores, axis=-1, keepdims=True)
    log_total = row_peak + jnp.log(jnp.sum(jnp.exp(scores - row_peak), axis=-1, keepdims=True))
    probs_low = jnp.exp(scores - log_total).astype(jnp.bfloat16)
    mixed_heads = jnp.einsum(
        "hqk,khe->qhe", probs_low, values_all, preferred_element_type=jnp.float32
    )
    mixed_heads = mixed_heads.reshape(row_count, width).astype(jnp.bfloat16)
    after_attn = base_rows + dot_rows(mixed_heads, used_out)
    normed_two, norm_two_back = jax.vjp(norm_rows, after_attn, gain_two)
    normed_two = normed_two.astype(jnp.bfloat16)
    up_rows = dot_rows(normed_two, used_up)
    activated, gelu_back = jax.vjp(partial(jax.nn.gelu, approximate=True), up_rows)
    activated = activated.astype(jnp.bfloat16)
    out_frames = (after_attn + dot_rows(activated, used_down)).astype(jnp.bfloat16)
    d_out = frame_weight[:, None] * cotangent.astype(jnp.float32)
    d_out_low = d_out.astype(jnp.bfloat16)
    grad_down = dot_left(activated, d_out_low)
    d_activated = dot_right(d_out_low, used_down)
    d_up = gelu_back(d_activated)[0].astype(jnp.bfloat16)
    grad_up = dot_left(normed_two, d_up)
    d_normed_two = dot_right(d_up, used_up)
    d_after_norm, grad_gain_two = norm_two_back(d_normed_two)
    d_after = d_out + d_after_norm
    d_after_low = d_after.astype(jnp.bfloat16)
    grad_out = dot_left(mixed_heads, d_after_low)
    d_mixed = dot_right(d_after_low, used_out).astype(jnp.bfloat16).reshape(heads_shape)
    scores = masked_scores(queries, keys_all, alibi_terms, same_item)
    probs = jnp.exp(scores - log_total)
    probs_low = probs.astype(jnp.bfloat16)
    d_probs = jnp.einsum("qhe,khe->hqk", d_mixed, values_all, preferred_element_type=jnp.float32)
    d_values = jnp.einsum("hqk,qhe->khe", probs_low, d_mixed, preferred_element_type=jnp.float32)
    d_scores = (probs * (d_probs - jnp.sum(probs * d_probs, axis=-1, keepdims=True))).astype(
        jnp.bfloat16
    )
    d_queries = jnp.einsum(
        "hqk,khe->qhe", d_scores, keys_all, preferred_element_type=jnp.float32
    ) * HD ** (-0.5)
    d_keys = jnp.einsum(
        "hqk,qhe->khe", d_scores, queries, preferred_element_type=jnp.float32
    ) * HD ** (-0.5)
    d_qkv = jnp.concatenate(
        [
            d_queries.reshape(row_count, width),
            d_keys.reshape(row_count, width),
            d_values.reshape(row_count, width),
        ],
        axis=1,
    ).astype(jnp.bfloat16)
    grad_qkv = dot_left(normed_one, d_qkv)
    d_normed_one = dot_right(d_qkv, used_qkv)
    d_base_norm, grad_gain_one = norm_one_back(d_normed_one)
    d_base_low = (d_after + d_base_norm).astype(jnp.bfloat16)
    grad_skip = dot_left(packed, d_base_low)
    d_packed = dot_right(d_base_low, used_skip).astype(jnp.bfloat16)
    gradients = (
        grad_skip,
        grad_qkv,
        grad_out,
        grad_up,
        grad_down,
        jnp.stack([grad_gain_one, grad_gain_two]),
    )
    dx_outgoing = gather_rows(d_packed[:, :width], back_indices, back_filled, buffer_shape)
    dskip_outgoing = gather_rows(d_packed[:, width:], back_indices, back_filled, buffer_shape)
    dx_arrived, dskip_arrived = (
        lax.all_to_all(dx_outgoing, "dp", split_axis=0, concat_axis=0, tiled=True),
        lax.all_to_all(dskip_outgoing, "dp", split_axis=0, concat_axis=0, tiled=True),
    )
    return_indices, return_filled = return_plan(own_lengths, own_packs, capacity, source_rows)
    input_grad = gather_rows(
        dx_arrived.reshape(-1, width), return_indices, return_filled, (source_rows, width)
    )
    skip_grad = gather_rows(
        dskip_arrived.reshape(-1, width), return_indices, return_filled, (source_rows, width)
    )
    return (out_frames, input_grad, skip_grad, gradients)


def adam_update(master, first, second, gradient, rate, decay):
    first_new = BETA_FIRST * first + (1.0 - BETA_FIRST) * gradient
    second_new = BETA_SECOND * second + (1.0 - BETA_SECOND) * gradient * gradient
    first_hat = first_new / (1.0 - BETA_FIRST**STEP)
    second_hat = second_new / (1.0 - BETA_SECOND**STEP)
    master_new = master - rate * (
        first_hat / (jnp.sqrt(second_hat) + ADAM_EPSILON) + decay * master
    )
    return (master_new, first_new, second_new)


def on_device(
    x_source,
    skip_source,
    out_cotangent,
    item_length,
    item_pack,
    item_offset,
    item_count,
    gains,
    w_skip,
    w_qkv,
    w_out,
    w_up,
    w_down,
    gains_first,
    first_skip,
    first_qkv,
    first_out,
    first_up,
    first_down,
    gains_second,
    second_skip,
    second_qkv,
    second_out,
    second_up,
    second_down,
):
    low_skip = w_skip.astype(jnp.bfloat16)
    low_qkv = w_qkv.astype(jnp.bfloat16)
    low_out = w_out.astype(jnp.bfloat16)
    low_up = w_up.astype(jnp.bfloat16)
    low_down = w_down.astype(jnp.bfloat16)
    low_gains = gains.astype(jnp.bfloat16)
    micro_count = x_source.shape[0]
    frame_list = []
    input_list = []
    skip_list = []
    summed = None
    for micro_index in range(micro_count):
        weights = (
            lax.all_gather(low_skip, "fsdp", axis=0, tiled=True),
            lax.all_gather(low_qkv, "fsdp", axis=0, tiled=True),
            lax.all_gather(low_out, "fsdp", axis=0, tiled=True),
            lax.all_gather(low_up, "fsdp", axis=0, tiled=True),
            lax.all_gather(low_down, "fsdp", axis=0, tiled=True),
            lax.all_gather(low_gains, "fsdp", axis=1, tiled=True),
        )
        out_frames, input_grad, skip_grad, gradients = micro_step(
            weights,
            x_source[micro_index],
            skip_source[micro_index],
            out_cotangent[micro_index],
            item_length[0, micro_index],
            item_pack[0, micro_index],
            item_offset[0, micro_index],
            item_count[0, micro_index],
        )
        frame_list.append(out_frames)
        input_list.append(input_grad)
        skip_list.append(skip_grad)
        summed = gradients if micro_index == 0 else jax.tree.map(jnp.add, summed, gradients)
    summed = (
        lax.psum_scatter(
            summed[0].astype(jnp.bfloat16), "fsdp", scatter_dimension=0, tiled=True
        ).astype(jnp.float32),
        lax.psum_scatter(
            summed[1].astype(jnp.bfloat16), "fsdp", scatter_dimension=0, tiled=True
        ).astype(jnp.float32),
        lax.psum_scatter(
            summed[2].astype(jnp.bfloat16), "fsdp", scatter_dimension=0, tiled=True
        ).astype(jnp.float32),
        lax.psum_scatter(
            summed[3].astype(jnp.bfloat16), "fsdp", scatter_dimension=0, tiled=True
        ).astype(jnp.float32),
        lax.psum_scatter(
            summed[4].astype(jnp.bfloat16), "fsdp", scatter_dimension=0, tiled=True
        ).astype(jnp.float32),
        lax.psum_scatter(
            summed[5].astype(jnp.bfloat16), "fsdp", scatter_dimension=1, tiled=True
        ).astype(jnp.float32),
    )
    reduced = (
        lax.psum(summed[0].astype(jnp.bfloat16), "dp").astype(jnp.float32),
        lax.psum(summed[1].astype(jnp.bfloat16), "dp").astype(jnp.float32),
        lax.psum(summed[2].astype(jnp.bfloat16), "dp").astype(jnp.float32),
        lax.psum(summed[3].astype(jnp.bfloat16), "dp").astype(jnp.float32),
        lax.psum(summed[4].astype(jnp.bfloat16), "dp").astype(jnp.float32),
        lax.psum(summed[5].astype(jnp.bfloat16), "dp").astype(jnp.float32),
    )
    local_squares = jnp.float32(0.0)
    for gradient in reduced:
        local_squares = local_squares + jnp.sum(gradient * gradient)
    total_squares = lax.psum(local_squares, "fsdp")
    gradient_norm = jnp.sqrt(total_squares)
    param_count = 6 * D * D + 2 * D * FF + 2 * D
    clip = jnp.minimum(1.0, 0.02 * math.sqrt(param_count) / gradient_norm)
    grad_skip, grad_qkv, grad_out, grad_up, grad_down, grad_gains = [
        clip * gradient for gradient in reduced
    ]
    gains_new, gains_first_new, gains_second_new = adam_update(
        gains, gains_first, gains_second, grad_gains, 0.3, 0.0
    )
    skip_new, skip_first_new, skip_second_new = adam_update(
        w_skip, first_skip, second_skip, grad_skip, 0.5 / math.sqrt(2 * D), WEIGHT_DECAY
    )
    qkv_new, qkv_first_new, qkv_second_new = adam_update(
        w_qkv, first_qkv, second_qkv, grad_qkv, 0.5 / math.sqrt(D), WEIGHT_DECAY
    )
    out_new, out_first_new, out_second_new = adam_update(
        w_out, first_out, second_out, grad_out, 0.5 / math.sqrt(D // 16), WEIGHT_DECAY
    )
    up_new, up_first_new, up_second_new = adam_update(
        w_up, first_up, second_up, grad_up, 0.5 / math.sqrt(D), WEIGHT_DECAY
    )
    down_new, down_first_new, down_second_new = adam_update(
        w_down, first_down, second_down, grad_down, 0.5 / math.sqrt(FF), WEIGHT_DECAY
    )
    return (
        jnp.stack(frame_list),
        jnp.stack(input_list),
        jnp.stack(skip_list),
        gradient_norm.reshape(1),
        gains_new,
        gains_first_new,
        gains_second_new,
        skip_new,
        skip_first_new,
        skip_second_new,
        skip_new.astype(jnp.bfloat16),
        qkv_new,
        qkv_first_new,
        qkv_second_new,
        qkv_new.astype(jnp.bfloat16),
        out_new,
        out_first_new,
        out_second_new,
        out_new.astype(jnp.bfloat16),
        up_new,
        up_first_new,
        up_second_new,
        up_new.astype(jnp.bfloat16),
        down_new,
        down_first_new,
        down_second_new,
        down_new.astype(jnp.bfloat16),
    )


def solution(mesh):
    return jax.shard_map(
        on_device,
        mesh=mesh,
        in_specs=(
            P(None, ("dp", "fsdp"), None),
            P(None, ("dp", "fsdp"), None),
            P(None, ("dp", "fsdp"), None),
            P("fsdp", None, None, None),
            P("fsdp", None, None, None),
            P("fsdp", None, None, None),
            P("fsdp", None, None, None),
            P(None, "fsdp"),
            P("fsdp", None),
            P("fsdp", None),
            P("fsdp", None),
            P("fsdp", None),
            P("fsdp", None),
            P(None, "fsdp"),
            P("fsdp", None),
            P("fsdp", None),
            P("fsdp", None),
            P("fsdp", None),
            P("fsdp", None),
            P(None, "fsdp"),
            P("fsdp", None),
            P("fsdp", None),
            P("fsdp", None),
            P("fsdp", None),
            P("fsdp", None),
        ),
        out_specs=(
            P(None, ("dp", "fsdp"), None),
            P(None, ("dp", "fsdp"), None),
            P(None, ("dp", "fsdp"), None),
            P(),
            P(None, "fsdp"),
            P(None, "fsdp"),
            P(None, "fsdp"),
            P("fsdp", None),
            P("fsdp", None),
            P("fsdp", None),
            P("fsdp", None),
            P("fsdp", None),
            P("fsdp", None),
            P("fsdp", None),
            P("fsdp", None),
            P("fsdp", None),
            P("fsdp", None),
            P("fsdp", None),
            P("fsdp", None),
            P("fsdp", None),
            P("fsdp", None),
            P("fsdp", None),
            P("fsdp", None),
            P("fsdp", None),
            P("fsdp", None),
            P("fsdp", None),
            P("fsdp", None),
        ),
        check_vma=False,
    )
```

profile of v0, /device:TPU:0, one launch (start us, length us, event | category | flops | bytes accessed | tf_op | source)
XLA Modules:
  0.0 1349.1 jit_solution(16953486046960237119)
XLA Ops:
  36.1 13.5 %all-to-all-done.1 = bf16[4,128,1024]{2,1,0:T(8,128)(2,1)S(1)} async-done(((bf16[4,128,1024]{2,1,0:T(8,128)(2,1)}), bf16[4,128,1024]{2,1,0:T(8,128)(2,1)S(1)}, u32[]{:S(2)}, u32[]{:S(2)}) %all-to-all-start.1) | async-done | bytes 1048608 | tf_op jit(solution)/shard_map/all_to_all | solution.py:130
  59.5 21.4 %all_gather.25 = bf16[2,1024]{1,0:T(2,128)(2,1)S(1)} all-gather(bf16[2,128]{1,0:T(2,128)(2,1)S(1)} %convert_element_type.228), channel_id=1, replica_groups=mesh['dp'=4,'fsdp'=8] {'fsdp'}, dimensions={1}, use_global_device_ids=true | all-gather | bytes 4608 | tf_op jit(solution)/shard_map/all_gather | solution.py:289
  87.5 14.3 %all-to-all-done.3 = bf16[4,128,1024]{2,1,0:T(8,128)(2,1)S(1)} async-done(((bf16[4,128,1024]{2,1,0:T(8,128)(2,1)}), bf16[4,128,1024]{2,1,0:T(8,128)(2,1)S(1)}, u32[]{:S(2)}, u32[]{:S(2)}) %all-to-all-start.3) | async-done | bytes 1048608 | tf_op jit(solution)/shard_map/all_to_all | solution.py:130
  128.1 58.9 %all-gather.8.cloned.1.call-done = bf16[1024,3072]{1,0:T(8,128)(2,1)} async-done(((bf16[128,3072]{1,0:T(8,128)(2,1)}), bf16[1024,3072]{1,0:T(8,128)(2,1)}) %all-gather.8.cloned.1.call-update) | async-done | bytes 6291472 | tf_op jit(solution)/shard_map/all_gather | solution.py:285
  212.1 25.2 %all-gather.10.cloned.1.call-done = bf16[1024,1024]{1,0:T(8,128)(2,1)} async-done(((bf16[128,1024]{1,0:T(8,128)(2,1)}), bf16[1024,1024]{1,0:T(8,128)(2,1)}) %all-gather.10.cloned.1.call-update) | async-done | bytes 2097168 | tf_op jit(solution)/shard_map/all_gather | solution.py:286
  245.8 117.4 %all-gather.12.cloned.1.call-done = bf16[1024,4096]{1,0:T(8,128)(2,1)} async-done(((bf16[128,4096]{1,0:T(8,128)(2,1)}), bf16[1024,4096]{1,0:T(8,128)(2,1)}) %all-gather.12.cloned.1.call-update) | async-done | bytes 8388624 | tf_op jit(solution)/shard_map/all_gather | solution.py:287
  363.2 7.9 fusion.99
  375.6 113.4 %all-gather.14.cloned.1.call-done = bf16[4096,1024]{1,0:T(8,128)(2,1)} async-done(((bf16[512,1024]{1,0:T(8,128)(2,1)}), bf16[4096,1024]{1,0:T(8,128)(2,1)}) %all-gather.14.cloned.1.call-update) | async-done | bytes 8388624 | tf_op jit(solution)/shard_map/all_gather | solution.py:288
  488.9 9.6 fusion.15
  505.8 8.1 fusion.8
  586.2 10.8 fusion.56
  597.0 14.0 %add_convert_fusion = bf16[4096,1024]{1,0:T(8,128)(2,1)} fusion(f32[4096,1024]{1,0:T(8,128)} %fusion.56, f32[256]{0:T(256)S(1)} %convert_divide_fusion, bf16[2,256,1024]{2,1,0:T(8,128)(2,1)S(1)} %copy-done.12, f32[256,4096]{1,0:T(8,128)} %fusion.100), kind=kOutput, calls=%fused_computation.16 | convolution fusion | flops 2166095872 | bytes 29885440 | tf_op jit(solution)/shard_map/dot_general | solution.py:41
  611.3 10.0 fusion.98
  621.4 11.6 add_convert_fusion.1
  647.4 14.2 %all-to-all-done.4 = bf16[4,128,1024]{2,1,0:T(8,128)(2,1)S(1)} async-done(((bf16[4,128,1024]{2,1,0:T(8,128)(2,1)}), bf16[4,128,1024]{2,1,0:T(8,128)(2,1)S(1)}, u32[]{:S(2)}, u32[]{:S(2)}) %all-to-all-start.4) | async-done | bytes 1048608 | tf_op jit(solution)/shard_map/all_to_all | solution.py:220
  684.4 8.3 fusion.31
  692.7 16.7 %reduce-scatter.9.cloned.1.call-done = bf16[256,1024]{1,0:T(8,128)(2,1)} async-done(((bf16[2048,1024]{1,0:T(8,128)(2,1)}), bf16[256,1024]{1,0:T(8,128)(2,1)}) %reduce-scatter.9.cloned.1.call-update) | async-done | bytes 524304 | tf_op jit(solution)/shard_map/reduce_scatter | solution.py:306
  709.4 121.8 %reduce-scatter.11.cloned.1.call-done = bf16[128,3072]{1,0:T(8,128)(2,1)} async-done(((bf16[1024,3072]{1,0:T(8,128)(2,1)}), bf16[128,3072]{1,0:T(8,128)(2,1)}) %reduce-scatter.11.cloned.1.call-update) | async-done | bytes 786448 | tf_op jit(solution)/shard_map/reduce_scatter | solution.py:309
  831.2 152.3 %reduce-scatter.17.cloned.1.call-done = bf16[512,1024]{1,0:T(8,128)(2,1)} async-done(((bf16[4096,1024]{1,0:T(8,128)(2,1)}), bf16[512,1024]{1,0:T(8,128)(2,1)}) %reduce-scatter.17.cloned.1.call-update) | async-done | bytes 1048592 | tf_op jit(solution)/shard_map/reduce_scatter | solution.py:318
  983.5 151.5 %reduce-scatter.15.cloned.1.call-done = bf16[128,4096]{1,0:T(8,128)(2,1)} async-done(((bf16[1024,4096]{1,0:T(8,128)(2,1)}), bf16[128,4096]{1,0:T(8,128)(2,1)}) %reduce-scatter.15.cloned.1.call-update) | async-done | bytes 1048592 | tf_op jit(solution)/shard_map/reduce_scatter | solution.py:315
  1139.3 7.6 fusion.30
  1148.0 51.5 %reduce-scatter.19.cloned.1.call-done = bf16[128,2]{1,0:T(8,128)(2,1)} async-done(((bf16[1024,2]{1,0:T(8,128)(2,1)}), bf16[128,2]{1,0:T(8,128)(2,1)}) %reduce-scatter.19.cloned.1.call-update) | async-done | bytes 528
  1222.4 56.7 %all-reduce.3.cloned.1.call-done = (bf16[256,1024]{1,0:T(8,128)(2,1)}, bf16[128,3072]{1,0:T(8,128)(2,1)}, bf16[128,1024]{1,0:T(8,128)(2,1)}, bf16[128,4096]{1,0:T(8,128)(2,1)}, bf16[512,1024]{1,0:T(8,128)(2,1)}) async-done(((bf16[256,1024]{1,0:T(8,128)(2,1)}, bf16[128,3072]{1,0:T(8,128)(2,1)}, bf16[128,1024]{1,0:T(8,128)(2,1)}, bf16[128,4096]{1,0:T(8,128)(2,1)}, bf16[512,1024]{1,0:T(8,128)(2,1)}), ...) | async-done | bytes 3670032 | tf_op jit(solution)/shard_map/psum | solution.py:326
  1295.1 22.2 %psum.55 = f32[]{:T(128)} all-reduce(f32[]{:T(128)S(6)} %add.423), channel_id=1, replica_groups=mesh['dp'=4,'fsdp'=8] {'fsdp'}, use_global_device_ids=true, to_apply=%region_70.74 | all-reduce | flops 1 | bytes 8 | tf_op jit(solution)/shard_map/psum | solution.py:336
  (457 shorter events, 287.8 us)
Async XLA Ops:
  7.2 115.0 %all-gather.6.cloned.1.call-start = ((), (), s32[]{:S(2)}) async-start(), calls=%async_computation.14 | async-start | bytes 4718592 | tf_op jit(solution)/shard_map/all_gather | solution.py:284
  9.4 177.6 %all-gather.8.cloned.1.call-start = ((), (), s32[]{:S(2)}) async-start(), calls=%async_computation.15 | async-start | bytes 7077888 | tf_op jit(solution)/shard_map/all_gather | solution.py:285
  12.0 225.2 %all-gather.10.cloned.1.call-start = ((), (), s32[]{:S(2)}) async-start(), calls=%async_computation.16 | async-start | bytes 2359296 | tf_op jit(solution)/shard_map/all_gather | solution.py:286
  12.9 350.3 %all-gather.12.cloned.1.call-start = ((), (), s32[]{:S(2)}) async-start(), calls=%async_computation.17 | async-start | bytes 9437184 | tf_op jit(solution)/shard_map/all_gather | solution.py:287
  15.7 473.3 %all-gather.14.cloned.1.call-start = ((), (), s32[]{:S(2)}) async-start(), calls=%async_computation.18 | async-start | bytes 9437184 | tf_op jit(solution)/shard_map/all_gather | solution.py:288
  30.8 18.8 %all-to-all-start.1 = ((bf16[4,128,1024]{2,1,0:T(8,128)(2,1)}), bf16[4,128,1024]{2,1,0:T(8,128)(2,1)S(1)}, u32[]{:S(2)}, u32[]{:S(2)}) async-start(bf16[4,128,1024]{2,1,0:T(8,128)(2,1)} %bitcast.232), calls=%async_computation.1 | async-start | bytes 2097152 | tf_op jit(solution)/shard_map/all_to_all | solution.py:130
  49.6 34.2 %all-to-all-start = ((bf16[4,128,1024]{2,1,0:T(8,128)(2,1)}), bf16[4,128,1024]{2,1,0:T(8,128)(2,1)}, u32[]{:S(2)}, u32[]{:S(2)}) async-start(bf16[4,128,1024]{2,1,0:T(8,128)(2,1)} %bitcast.228), calls=%async_computation | async-start | bytes 2097152 | tf_op jit(solution)/shard_map/all_to_all | solution.py:129
  83.8 18.0 %all-to-all-start.3 = ((bf16[4,128,1024]{2,1,0:T(8,128)(2,1)}), bf16[4,128,1024]{2,1,0:T(8,128)(2,1)S(1)}, u32[]{:S(2)}, u32[]{:S(2)}) async-start(bf16[4,128,1024]{2,1,0:T(8,128)(2,1)} %bitcast.30), calls=%async_computation.3 | async-start | bytes 2097152 | tf_op jit(solution)/shard_map/all_to_all | solution.py:130
  101.8 18.0 %all-to-all-start.2 = ((bf16[4,128,1024]{2,1,0:T(8,128)(2,1)}), bf16[4,128,1024]{2,1,0:T(8,128)(2,1)S(1)}, u32[]{:S(2)}, u32[]{:S(2)}) async-start(bf16[4,128,1024]{2,1,0:T(8,128)(2,1)} %bitcast.230), calls=%async_computation.2 | async-start | bytes 2097152 | tf_op jit(solution)/shard_map/all_to_all | solution.py:129
  105.3 587.4 %reduce-scatter.13.cloned.1.call-start = ((), (), s32[]{:S(2)}) async-start(), calls=%async_computation.21 | async-start | bytes 2359296 | tf_op jit(solution)/shard_map/reduce_scatter | solution.py:312
  105.5 100.4 %copy-start.120 = (f32[16]{0:T(128)}, f32[16]{0:T(128)S(1)}, u32[]{:S(2)}) copy-start(f32[16]{0:T(128)S(1)} %exponential_negate_fusion) | copy-start | bytes 196
  245.5 365.8 %copy-start.5 = (f32[256,1024]{1,0:T(8,128)}, f32[256,1024]{1,0:T(8,128)S(1)}, u32[]{:S(2)}) copy-start(f32[256,1024]{1,0:T(8,128)S(1)} %get-tuple-element.181) | copy-start | bytes 3145732
  552.6 156.8 %reduce-scatter.9.cloned.1.call-start = ((), (), s32[]{:S(2)}) async-start(), calls=%async_computation.19 | async-start | bytes 4718592 | tf_op jit(solution)/shard_map/reduce_scatter | solution.py:306
  574.1 257.1 %reduce-scatter.11.cloned.1.call-start = ((), (), s32[]{:S(2)}) async-start(), calls=%async_computation.20 | async-start | bytes 7077888 | tf_op jit(solution)/shard_map/reduce_scatter | solution.py:309
  585.0 398.5 %reduce-scatter.17.cloned.1.call-start = ((), (), s32[]{:S(2)}) async-start(), calls=%async_computation.23 | async-start | bytes 9437184 | tf_op jit(solution)/shard_map/reduce_scatter | solution.py:318
  611.1 523.9 %reduce-scatter.15.cloned.1.call-start = ((), (), s32[]{:S(2)}) async-start(), calls=%async_computation.22 | async-start | bytes 9437184 | tf_op jit(solution)/shard_map/reduce_scatter | solution.py:315
  643.5 18.1 %all-to-all-start.4 = ((bf16[4,128,1024]{2,1,0:T(8,128)(2,1)}), bf16[4,128,1024]{2,1,0:T(8,128)(2,1)S(1)}, u32[]{:S(2)}, u32[]{:S(2)}) async-start(bf16[4,128,1024]{2,1,0:T(8,128)(2,1)} %bitcast.233), calls=%async_computation.4 | async-start | bytes 2097152 | tf_op jit(solution)/shard_map/all_to_all | solution.py:220
  661.5 19.0 %all-to-all-start.6 = ((bf16[4,128,1024]{2,1,0:T(8,128)(2,1)}), bf16[4,128,1024]{2,1,0:T(8,128)(2,1)S(1)}, u32[]{:S(2)}, u32[]{:S(2)}) async-start(bf16[4,128,1024]{2,1,0:T(8,128)(2,1)} %bitcast.229), calls=%async_computation.6 | async-start | bytes 2097152 | tf_op jit(solution)/shard_map/all_to_all | solution.py:221
  665.1 534.4 %reduce-scatter.19.cloned.1.call-start = ((), (), s32[]{:S(2)}) async-start(), calls=%async_computation.24 | async-start | bytes 294912
  680.6 454.4 %all-to-all-start.5 = ((bf16[4,128,1024]{2,1,0:T(8,128)(2,1)}), bf16[4,128,1024]{2,1,0:T(8,128)(2,1)S(1)}, u32[]{:S(2)}, u32[]{:S(2)}) async-start(bf16[4,128,1024]{2,1,0:T(8,128)(2,1)} %bitcast.231), calls=%async_computation.5 | async-start | bytes 2097152 | tf_op jit(solution)/shard_map/all_to_all | solution.py:220
  684.1 595.0 %all-reduce.3.cloned.1.call-start = ((), (), s32[]{:S(2)}) async-start(), calls=%async_computation.25 | async-start | bytes 7340032 | tf_op jit(solution)/shard_map/psum | solution.py:326
  1135.0 79.1 %all-to-all-start.7 = ((bf16[4,128,1024]{2,1,0:T(8,128)(2,1)}), bf16[4,128,1024]{2,1,0:T(8,128)(2,1)}, u32[]{:S(2)}, u32[]{:S(2)}) async-start(bf16[4,128,1024]{2,1,0:T(8,128)(2,1)} %bitcast.227), calls=%async_computation.7 | async-start | bytes 2097152 | tf_op jit(solution)/shard_map/all_to_all | solution.py:221
  1222.4 95.7 %copy-start.116 = (f32[2,128]{1,0:T(2,128)S(1)}, f32[2,128]{1,0:T(2,128)}, u32[]{:S(2)}) copy-start(f32[2,128]{1,0:T(2,128)} %param.44) | copy-start | bytes 3076
  1222.4 95.7 %copy-start.117 = (f32[2,128]{1,0:T(2,128)S(1)}, f32[2,128]{1,0:T(2,128)}, u32[]{:S(2)}) copy-start(f32[2,128]{1,0:T(2,128)} %param.50) | copy-start | bytes 3076
  (120 other events, 880.2 us)
Sparse Core Ops, SparseCore 0:
  10.7 76.1 all-gather.5
  89.7 97.2 all-gather.7
  189.7 47.4 all-gather.9
  239.8 123.4 all-gather.11
  365.8 123.1 all-gather.13
  552.7 65.7 reduce-scatter.12
  622.2 87.1 reduce-scatter.8
  713.4 117.7 reduce-scatter.10
  835.3 148.1 reduce-scatter.16
  987.0 147.9 reduce-scatter.14
  1139.3 60.1 reduce-scatter.18
  1202.3 76.7 all-reduce.2
where the time goes:
time: 1360 us; the launch traced here: 1350 us
  waiting for transfers between devices  914 us (67%)
  matrix products  184 us (14%)
  local copies, waits for them, and re-layouts  74.6 us (5%)
  other arithmetic  72.3 us (5%)
  blocking collectives  49.3 us (4%)
  starting transfers between devices  32.3 us (2%)
  between operations  22.2 us (2%)
    reduce_scatter x1, waiting for transfers between devices, on_device(): lax.psum_scatter(summed[4].astype(jnp.bfloat16), 'fsdp', scatter_dimensio...  152 us
    reduce_scatter x1, waiting for transfers between devices, on_device(): lax.psum_scatter(summed[3].astype(jnp.bfloat16), 'fsdp', scatter_dimensio...  152 us
    reduce_scatter x1, waiting for transfers between devices, on_device(): lax.psum_scatter(summed[1].astype(jnp.bfloat16), 'fsdp', scatter_dimensio...  122 us
    all_gather x1, waiting for transfers between devices, on_device(): lax.all_gather(low_up, 'fsdp', axis=0, tiled=True)  117 us
    all_gather x1, waiting for transfers between devices, on_device(): lax.all_gather(low_down, 'fsdp', axis=0, tiled=True)  113 us
    dot_general x10, matrix products, dot_left(): lax.dot_general(left, right, (((0,), (0,)), ((), ())), preferred_element_...  66.3 us
    all_gather x1, waiting for transfers between devices, on_device(): lax.all_gather(low_qkv, 'fsdp', axis=0, tiled=True)  58.9 us
    psum x1, waiting for transfers between devices, on_device(): lax.psum(summed[0].astype(jnp.bfloat16), 'dp').astype(jnp.float32)  56.7 us
  transfers between devices with their start and end apart: 20, of which 14 were waited for; matrix products, arithmetic and copies ran while one was open for 17% of the time, Pallas kernels for 0%

commit v1 on v0

v1 whole, which is shorter than its diff:
```python
from functools import partial
import math

import jax
import jax.numpy as jnp
from jax import lax
from jax.experimental import pallas as pl
from jax.experimental.pallas import tpu as pltpu
from jax.sharding import PartitionSpec as P

D = 1024
HEADS = 16
HD = 64
FF = 4096
STEP = 5
CORES = 2
OUTER = 4

BETA_FIRST = 0.5
BETA_SECOND = 0.5
ADAM_EPSILON = 1e-08
WEIGHT_DECAY = 0.01
NORM_EPSILON = 1e-05

BF16 = jnp.bfloat16
F32 = jnp.float32
MESH = pl.DeviceIdType.MESH

GATHER_UNITS = ((0, 0, 1, False), (1, 0, 1, True), (2, 0, 1, False), (3, 0, 1, True), (4, 0, 2, False), (4, 1, 2, False))


def sizes():
    n_dp, n_fsdp = lax.axis_size("dp"), lax.axis_size("fsdp")
    return n_dp // CORES, CORES, OUTER, n_fsdp // OUTER


def place():
    rows, cores, outer, inner = sizes()
    dp, fsdp = lax.axis_index("dp"), lax.axis_index("fsdp")
    return dp // cores, lax.rem(dp, cores), fsdp // inner, lax.rem(fsdp, inner)


def gather_kernel(dims, *refs):
    n_y, n_c, n_a, n_b = dims
    count = 5
    shards, payload, gains = refs[:count], refs[count], refs[count + 1]
    outs = refs[count + 2 : 2 * count + 4]
    fulls, arrived, gains_full = outs[:count], outs[count], outs[count + 1]
    send_sem, recv_sem, local_sem = refs[2 * count + 4 :]
    dp, fsdp = lax.axis_index("dp"), lax.axis_index("fsdp")
    y, c, a, b = dp // n_c, lax.rem(dp, n_c), fsdp // n_b, lax.rem(fsdp, n_b)
    n_dp, n_fsdp = n_y * n_c, n_a * n_b
    used = [0, 0]
    sent = []

    def remote(src, dst, landing, device):
        index = used[0]
        used[0] += 1
        copy = pltpu.make_async_remote_copy(
            src_ref=src, dst_ref=dst, send_sem=send_sem.at[index], recv_sem=recv_sem.at[index],
            device_id=device, device_id_type=MESH,
        )
        copy.start()
        sent.append(copy)
        return pltpu.make_async_remote_copy(
            src_ref=src, dst_ref=landing, send_sem=send_sem.at[index], recv_sem=recv_sem.at[index],
            device_id=device, device_id_type=MESH,
        )

    def local(src, dst):
        index = used[1]
        used[1] += 1
        copy = pltpu.make_async_copy(src, dst, local_sem.at[index])
        copy.start()
        return copy

    def turn(value, step, size):
        return lax.rem(value + (step + size) % size, size)

    frames = []
    for k in range(1, n_dp):
        to, back = turn(dp, k, n_dp), turn(dp, -k, n_dp)
        frames.append(remote(payload.at[:, to], arrived.at[:, dp], arrived.at[:, back], (to, fsdp)))
    own_frames = local(payload.at[:, dp], arrived.at[:, dp])
    gain_copies = []
    for k in range(1, n_fsdp):
        to, back = turn(fsdp, k, n_fsdp), turn(fsdp, -k, n_fsdp)
        gain_copies.append(remote(gains, gains_full.at[fsdp], gains_full.at[back], (dp, to)))
    own_gains = local(gains, gains_full.at[fsdp])

    units = []
    for matrix, part, parts, shared in GATHER_UNITS:
        width = shards[matrix].shape[1] // parts
        units.append((matrix, part * width, width, shared))
    state = [{} for _ in units]

    def columns(unit, of_y):
        matrix, first, width, shared = unit
        if shared:
            step = width // (n_c * n_y)
            return pl.ds(pl.multiple_of(first + (c * n_y + of_y) * step, 128), step)
        step = width // n_c
        return pl.ds(pl.multiple_of(first + c * step, 128), step)

    def stage_outer(index):
        matrix, first, width, shared = units[index]
        cols, full, shard = columns(units[index], y), fulls[matrix], shards[matrix]
        state[index]["outer"] = [
            remote(
                shard.at[:, cols], full.at[a, b, :, cols], full.at[turn(a, -k, n_a), b, :, cols],
                (dp, turn(a, k, n_a) * n_b + b),
            )
            for k in range(1, n_a)
        ]
        whole = pl.ds(first, width)
        state[index]["own"] = local(shard.at[:, whole], full.at[a, b, :, whole])

    def spread(index, block, of_y, kinds):
        matrix, first, width, shared = units[index]
        full, cols = fulls[matrix], columns(units[index], of_y)
        view = full.at[block[0], block[1], :, cols]
        if "y" in kinds and shared:
            for k in range(1, n_y):
                source = turn(y, -k, n_y)
                landing = full.at[block[0], block[1], :, columns(units[index], source)]
                copy = remote(view, view, landing, (turn(y, k, n_y) * n_c + c, fsdp))
                state[index].setdefault("y", []).append((copy, block, source))
        if "c" in kinds:
            step = width // (n_c * n_y) if shared else width // n_c
            other = (
                first + ((1 - c) * n_y + of_y) * step if shared else first + (1 - c) * step
            )
            landing = full.at[block[0], block[1], :, pl.ds(pl.multiple_of(other, 128), step)]
            copy = remote(view, view, landing, (y * n_c + 1 - c, fsdp))
            state[index].setdefault("c", []).append(copy)

    def stage_inner(index):
        matrix, first, width, shared = units[index]
        cols, full = columns(units[index], y), fulls[matrix]
        state[index]["own"].wait()
        for copy in state[index]["outer"]:
            copy.wait_recv()
        state[index]["inner"] = [
            remote(
                full.at[:, b, :, cols], full.at[:, b, :, cols], full.at[:, turn(b, -k, n_b), :, cols],
                (dp, a * n_b + turn(b, k, n_b)),
            )
            for k in range(1, n_b)
        ]
        for k in range(1, n_a):
            spread(index, (turn(a, -k, n_a), b), y, "yc")

    def stage_y(index):
        for k, copy in zip(range(1, n_b), state[index]["inner"]):
            copy.wait_recv()
            spread(index, (slice(None), turn(b, -k, n_b)), y, "yc")

    def stage_c(index):
        for copy, block, source in state[index].get("y", []):
            copy.wait_recv()
            spread(index, block, source, "c")

    count_units = len(units)
    for step in range(count_units + 3):
        if step < count_units:
            stage_outer(step)
        if 0 <= step - 1 < count_units:
            stage_inner(step - 1)
        if 0 <= step - 2 < count_units:
            stage_y(step - 2)
        if 0 <= step - 3 < count_units:
            stage_c(step - 3)
    for copy in frames + gain_copies:
        copy.wait_recv()
    for index in range(count_units):
        for copy in state[index].get("c", []):
            copy.wait_recv()
    for copy in sent:
        copy.wait_send()
    own_frames.wait()
    own_gains.wait()


def gather_all(shards, payload, gains):
    dims = sizes()
    n_y, n_c, n_a, n_b = dims
    total = n_y * n_c - 1 + n_a * n_b - 1
    for _, _, _, shared in GATHER_UNITS:
        groups = n_a - 1 + n_b - 1
        total += groups + ((n_y - 1) * groups + n_y * groups if shared else groups)
    anywhere = pl.BlockSpec(memory_space=pl.ANY)
    out_shape = [
        jax.ShapeDtypeStruct((n_a, n_b) + shard.shape, shard.dtype) for shard in shards
    ] + [
        jax.ShapeDtypeStruct(payload.shape, payload.dtype),
        jax.ShapeDtypeStruct((n_a * n_b,) + gains.shape, gains.dtype),
    ]
    results = pl.pallas_call(
        partial(gather_kernel, dims),
        out_shape=out_shape,
        in_specs=[anywhere] * (len(shards) + 2),
        out_specs=[anywhere] * len(out_shape),
        scratch_shapes=[
            pltpu.SemaphoreType.DMA((total,)),
            pltpu.SemaphoreType.DMA((total,)),
            pltpu.SemaphoreType.DMA((len(GATHER_UNITS) + 2,)),
        ],
        compiler_params=pltpu.CompilerParams(has_side_effects=True),
        name="gather_weights",
    )(*shards, payload, gains)
    fulls = [
        full.reshape(n_a * n_b * shard.shape[0], shard.shape[1])
        for full, shard in zip(results, shards)
    ]
    return fulls, results[-2], results[-1]


def move(value, axis, shift):
    n_y, n_c, n_a, n_b = sizes()
    dims = {"y": n_y, "c": n_c, "a": n_a, "b": n_b}
    pairs = []
    for source in range(n_y * n_c * n_a * n_b):
        at = {
            "y": source // (n_c * n_a * n_b),
            "c": source // (n_a * n_b) % n_c,
            "a": source // n_b % n_a,
            "b": source % n_b,
        }
        at[axis] = (at[axis] + shift) % dims[axis]
        target = ((at["y"] * n_c + at["c"]) * n_a + at["a"]) * n_b + at["b"]
        pairs.append((source, target))
    return lax.ppermute(value, ("dp", "fsdp"), pairs)


def swap(value, axis, mask):
    n_y, n_c, n_a, n_b = sizes()
    pairs = []
    for source in range(n_y * n_c * n_a * n_b):
        at = {
            "y": source // (n_c * n_a * n_b),
            "c": source // (n_a * n_b) % n_c,
            "a": source // n_b % n_a,
            "b": source % n_b,
        }
        at[axis] = at[axis] ^ mask
        target = ((at["y"] * n_c + at["c"]) * n_a + at["a"]) * n_b + at["b"]
        pairs.append((source, target))
    return lax.ppermute(value, ("dp", "fsdp"), pairs)


def pick(value, index, axis):
    return lax.dynamic_index_in_dim(value, index, axis, keepdims=False)


def add_all(values):
    total = values[0].astype(F32)
    for value in values[1:]:
        total = total + value.astype(F32)
    return total.astype(BF16)


def both_cores(value):
    return jnp.concatenate([value, move(value, "c", 1)], axis=0)


def weight_gradient(left, right, shared):
    n_y, n_c, n_a, n_b = sizes()
    y, c, a, b = place()
    width = right.shape[1] // n_c
    halves = right.reshape(right.shape[0], n_c, width)
    mine, other = pick(halves, c, 1), pick(halves, 1 - c, 1)
    left_all = both_cores(left)
    right_all = jnp.concatenate([mine, move(other, "c", 1)], axis=0)
    partial_sum = lax.dot_general(
        left_all, right_all, (((0,), (0,)), ((), ())), preferred_element_type=F32
    ).astype(BF16)
    rows = left.shape[1] // (n_a * n_b)
    blocks = partial_sum.reshape(n_a, n_b, rows, width)
    if shared:
        step = width // n_y
        pieces = blocks.reshape(n_a, n_b, rows, n_y, step)
        got = [
            move(pick(pieces, (y + k) % n_y, 3), "y", k) for k in range(1, n_y)
        ]
        blocks = add_all([pick(pieces, y, 3)] + got)
    got = [move(pick(blocks, (b + k) % n_b, 1), "b", k) for k in range(1, n_b)]
    blocks = add_all([pick(blocks, b, 1)] + got)
    got = [move(pick(blocks, (a + k) % n_a, 0), "a", k) for k in range(1, n_a)]
    own = add_all([pick(blocks, a, 0)] + got)
    if shared:
        full = jnp.zeros((n_y, rows, step), BF16)
        full = lax.dynamic_update_index_in_dim(full, own, y, 0)
        for k in range(1, n_y):
            full = lax.dynamic_update_index_in_dim(full, move(own, "y", k), (y - k) % n_y, 0)
        own = jnp.moveaxis(full, 0, 1).reshape(rows, width)
    else:
        mask = 1
        while mask < n_y:
            own = add_all([own, swap(own, "y", mask)])
            mask *= 2
    other = move(own, "c", 1)
    return jnp.where(
        c == 0, jnp.concatenate([own, other], axis=1), jnp.concatenate([other, own], axis=1)
    ).astype(F32)


def sum_over(value, axis, count):
    mask = 1
    while mask < count:
        value = value + swap(value, axis, mask)
        mask *= 2
    return value


def dot_rows(left, right):
    return jnp.dot(left, right, preferred_element_type=F32)


def dot_right(left, right):
    return lax.dot_general(left, right, (((1,), (1,)), ((), ())), preferred_element_type=F32)


def norm_parts(hidden):
    centre = hidden - jnp.mean(hidden, axis=-1, keepdims=True)
    spread = jnp.mean(centre * centre, axis=-1, keepdims=True)
    scale = lax.rsqrt(spread + NORM_EPSILON)
    return centre * scale, scale


def norm_back(normal, scale, gain_row, gradient):
    scaled = gradient * gain_row
    grad_gain = jnp.sum(gradient * normal, axis=0)
    back = scale * (
        scaled
        - jnp.mean(scaled, axis=-1, keepdims=True)
        - normal * jnp.mean(scaled * normal, axis=-1, keepdims=True)
    )
    return back, grad_gain


def alibi_bias(length):
    position = jnp.arange(length, dtype=F32)
    distance = jnp.abs(position[:, None] - position[None, :])
    slopes = jnp.exp2(-8.0 * (jnp.arange(HEADS, dtype=F32) + 1.0) / HEADS)
    return -slopes[:, None, None] * distance[None]


def attention_scores(queries, keys_all, alibi_terms, same_item):
    scores = (
        jnp.einsum("nqhe,nkhe->nhqk", queries, keys_all, preferred_element_type=F32) * HD ** (-0.5)
        + alibi_terms[None]
    )
    return jnp.where(same_item[:, None], scores, -1e30)


def adam_update(master, first, second, gradient, rate, decay):
    first_new = BETA_FIRST * first + (1.0 - BETA_FIRST) * gradient
    second_new = BETA_SECOND * second + (1.0 - BETA_SECOND) * gradient * gradient
    first_hat = first_new / (1.0 - BETA_FIRST**STEP)
    second_hat = second_new / (1.0 - BETA_SECOND**STEP)
    master_new = master - rate * (
        first_hat / (jnp.sqrt(second_hat) + ADAM_EPSILON) + decay * master
    )
    return (master_new, first_new, second_new)


def one_hot(indices, filled, size):
    hit = indices[..., None] == jnp.arange(size, dtype=jnp.int32)
    return (hit & filled[..., None]).astype(BF16)


def frame_plans(lengths, packs, offsets, counts, source_rows, row_count, capacity):
    n_dp = lax.axis_size("dp")
    own = lax.axis_index("dp")
    slot = jnp.arange(capacity, dtype=jnp.int32)
    ids = jnp.arange(n_dp, dtype=jnp.int32)
    own_lengths, own_packs = pick(lengths, own, 1), pick(packs, own, 1)
    starts = jnp.cumsum(own_lengths, axis=1) - own_lengths
    matches = own_packs[:, None, :] == ids[None, :, None]
    length_to = jnp.sum(jnp.where(matches, own_lengths[:, None, :], 0), axis=2)
    start_to = jnp.sum(jnp.where(matches, starts[:, None, :], 0), axis=2)
    filled = slot < length_to[..., None]
    send = one_hot(start_to[..., None] + slot, filled, source_rows)
    here = packs == own

    def chosen(values):
        return jnp.sum(jnp.where(here, values, 0), axis=2)

    length_from, offset_from, count_from = chosen(lengths), chosen(offsets), chosen(counts)
    filled = slot < length_from[..., None]
    back = one_hot(offset_from[..., None] + slot, filled, row_count)
    position = jnp.arange(row_count, dtype=jnp.int32)
    inside = (position[None, :, None] >= offset_from[:, None, :]) & (
        position[None, :, None] < (offset_from + length_from)[:, None, :]
    )

    def select(values):
        return jnp.sum(jnp.where(inside, values[:, None, :], 0), axis=2)

    source = select(jnp.broadcast_to(ids, offset_from.shape))
    weight = select(count_from).astype(F32) / select(length_from).astype(F32)
    return send, back, source, weight


def on_device(
    x_source, skip_source, out_cotangent, item_length, item_pack, item_offset, item_count,
    gains, w_skip, w_qkv, w_out, w_up, w_down,
    gains_first, first_skip, first_qkv, first_out, first_up, first_down,
    gains_second, second_skip, second_qkv, second_out, second_up, second_down,
):
    n_y, n_c, n_a, n_b = sizes()
    n_dp, n_fsdp = n_y * n_c, n_a * n_b
    y, c, a, b = place()
    dp, fsdp = lax.axis_index("dp"), lax.axis_index("fsdp")
    micro, source_rows, width = x_source.shape
    row_count = out_cotangent.shape[1]
    capacity = source_rows // n_dp
    rows = micro * row_count

    send, back, source, weight = frame_plans(
        item_length[0], item_pack[0], item_offset[0], item_count[0], source_rows, row_count, capacity
    )

    def to_packs(values):
        return jnp.einsum("bpsr,brw->bpsw", send, values, preferred_element_type=F32).astype(BF16)

    payload = jnp.concatenate([to_packs(x_source), to_packs(skip_source)], axis=-1)
    shards = [w.astype(BF16) for w in (w_skip, w_qkv, w_out, w_up, w_down)]
    own_gains = gains.shape[1]
    low_gains = jnp.zeros((8, 128), F32).at[:2, :own_gains].set(gains.astype(BF16).astype(F32))
    (used_skip, used_qkv, used_out, used_up, used_down), arrived, gains_all = gather_all(
        shards, payload, low_gains
    )
    used_gains = jnp.moveaxis(gains_all[:, :2, :own_gains], 0, 1).reshape(2, width)

    packed = jnp.einsum("bpst,bpsw->btw", back, arrived, preferred_element_type=F32)
    packed = packed.astype(BF16).reshape(rows, 2 * width)
    base_rows = dot_rows(packed, used_skip)
    normal_one, scale_one = norm_parts(base_rows)
    normed_one = (normal_one * used_gains[0]).astype(BF16)
    qkv_rows = dot_rows(normed_one, used_qkv).astype(BF16)
    heads_shape = (micro, row_count, HEADS, HD)
    queries = qkv_rows[:, :width].reshape(heads_shape)
    keys_all = qkv_rows[:, width : 2 * width].reshape(heads_shape)
    values_all = qkv_rows[:, 2 * width :].reshape(heads_shape)
    alibi_terms = alibi_bias(row_count)
    same_item = source[:, :, None] == source[:, None, :]
    scores = attention_scores(queries, keys_all, alibi_terms, same_item)
    row_peak = jnp.max(scores, axis=-1, keepdims=True)
    log_total = row_peak + jnp.log(jnp.sum(jnp.exp(scores - row_peak), axis=-1, keepdims=True))
    probs_low = jnp.exp(scores - log_total).astype(BF16)
    mixed = jnp.einsum("nhqk,nkhe->nqhe", probs_low, values_all, preferred_element_type=F32)
    mixed = mixed.reshape(rows, width).astype(BF16)
    after_attn = base_rows + dot_rows(mixed, used_out)
    normal_two, scale_two = norm_parts(after_attn)
    normed_two = (normal_two * used_gains[1]).astype(BF16)
    up_rows = dot_rows(normed_two, used_up)
    activated, gelu_back = jax.vjp(partial(jax.nn.gelu, approximate=True), up_rows)
    activated = activated.astype(BF16)
    out_frames = (after_attn + dot_rows(activated, used_down)).astype(BF16)

    d_out = weight.reshape(rows, 1) * out_cotangent.reshape(rows, width).astype(F32)
    d_out_low = d_out.astype(BF16)
    grad_down = weight_gradient(activated, d_out_low, False)
    d_up = gelu_back(dot_right(d_out_low, used_down))[0].astype(BF16)
    grad_up = weight_gradient(normed_two, d_up, True)
    d_after_norm, grad_gain_two = norm_back(
        normal_two, scale_two, used_gains[1], dot_right(d_up, used_up)
    )
    d_after = d_out + d_after_norm
    d_after_low = d_after.astype(BF16)
    grad_out = weight_gradient(mixed, d_after_low, False)
    d_mixed = dot_right(d_after_low, used_out).astype(BF16).reshape(heads_shape)
    scores = attention_scores(queries, keys_all, alibi_terms, same_item)
    probs = jnp.exp(scores - log_total)
    probs_low = probs.astype(BF16)
    d_probs = jnp.einsum("nqhe,nkhe->nhqk", d_mixed, values_all, preferred_element_type=F32)
    d_values = jnp.einsum("nhqk,nqhe->nkhe", probs_low, d_mixed, preferred_element_type=F32)
    d_scores = (probs * (d_probs - jnp.sum(probs * d_probs, axis=-1, keepdims=True))).astype(BF16)
    d_queries = jnp.einsum("nhqk,nkhe->nqhe", d_scores, keys_all, preferred_element_type=F32)
    d_keys = jnp.einsum("nhqk,nqhe->nkhe", d_scores, queries, preferred_element_type=F32)
    d_qkv = jnp.concatenate(
        [
            (d_queries * HD ** (-0.5)).reshape(rows, width),
            (d_keys * HD ** (-0.5)).reshape(rows, width),
            d_values.reshape(rows, width),
        ],
        axis=1,
    ).astype(BF16)
    grad_qkv = weight_gradient(normed_one, d_qkv, True)
    d_base_norm, grad_gain_one = norm_back(
        normal_one, scale_one, used_gains[0], dot_right(d_qkv, used_qkv)
    )
    d_base_low = (d_after + d_base_norm).astype(BF16)
    d_packed = dot_right(d_base_low, used_skip).astype(BF16).reshape(micro, row_count, 2 * width)
    returning = jnp.einsum("bpst,btw->bpsw", back, d_packed, preferred_element_type=F32).astype(BF16)
    returned = jnp.zeros_like(returning)
    returned = lax.dynamic_update_index_in_dim(returned, pick(returning, dp, 1), dp, 1)
    for k in range(1, n_dp):
        pairs = [
            (s * n_fsdp + f, (s + k) % n_dp * n_fsdp + f) for s in range(n_dp) for f in range(n_fsdp)
        ]
        got = lax.ppermute(pick(returning, (dp + k) % n_dp, 1), ("dp", "fsdp"), pairs)
        returned = lax.dynamic_update_index_in_dim(returned, got, (dp - k) % n_dp, 1)
    grad_skip = weight_gradient(packed, d_base_low, False)
    in_gradient = jnp.einsum("bpsr,bpsw->brw", send, returned, preferred_element_type=F32)
    in_gradient = in_gradient.astype(BF16)
    input_gradient, skip_gradient = in_gradient[..., :width], in_gradient[..., width:]

    grad_gains = lax.psum(jnp.stack([grad_gain_one, grad_gain_two]), ("dp", "fsdp"))
    grad_gains = pick(grad_gains.reshape(2, n_fsdp, own_gains), fsdp, 1)

    gradients = (grad_skip, grad_qkv, grad_out, grad_up, grad_down, grad_gains)
    squares = jnp.float32(0.0)
    for gradient in gradients:
        squares = squares + jnp.sum(gradient * gradient)
    squares = sum_over(sum_over(jnp.full((8, 128), squares), "b", n_b), "a", n_a)
    gradient_norm = jnp.sqrt(squares[0, 0])
    param_count = 6 * D * D + 2 * D * FF + 2 * D
    clip = jnp.minimum(1.0, 0.02 * math.sqrt(param_count) / gradient_norm)
    grad_skip, grad_qkv, grad_out, grad_up, grad_down, grad_gains = [clip * g for g in gradients]
    results = [out_frames.reshape(micro, row_count, width), input_gradient, skip_gradient]
    results.append(gradient_norm.reshape(1))
    results.extend(adam_update(gains, gains_first, gains_second, grad_gains, 0.3, 0.0))
    for master, first, second, gradient, fan_in in (
        (w_skip, first_skip, second_skip, grad_skip, 2 * D),
        (w_qkv, first_qkv, second_qkv, grad_qkv, D),
        (w_out, first_out, second_out, grad_out, D // 16),
        (w_up, first_up, second_up, grad_up, D),
        (w_down, first_down, second_down, grad_down, FF),
    ):
        new = adam_update(master, first, second, gradient, 0.5 / math.sqrt(fan_in), WEIGHT_DECAY)
        results.extend(new)
        results.append(new[0].astype(BF16))
    return tuple(results)


def solution(mesh):
    frames = P(None, ("dp", "fsdp"), None)
    plan = P("fsdp", None, None, None)
    gain, weight = P(None, "fsdp"), P("fsdp", None)
    return jax.shard_map(
        on_device,
        mesh=mesh,
        in_specs=(frames,) * 3 + (plan,) * 4 + ((gain,) + (weight,) * 5) * 3,
        out_specs=(frames,) * 3 + (P(),) + (gain,) * 3 + (weight,) * 20,
        check_vma=False,
    )
```

time: 1360 us -> 806 us (0.59)
  waiting for transfers between devices: 914 us -> 135 us
  Pallas kernels: 0 us -> 194 us
  local copies, waits for them, and re-layouts: 74.6 us -> 170 us
  matrix products: 184 us -> 141 us
  starting transfers between devices: 32.3 us -> 55.8 us
  between operations: 22.2 us -> 8.45 us
    reduce_scatter x5 -> x0, waiting for transfers between devices: 442 us -> none  [the longest x1 152 us: on_device(): lax.psum_scatter(summed[4].astype(jnp.bfloat16), 'fsdp', scatter_dimensio...]
    all_gather x5 -> x0, waiting for transfers between devices: 315 us -> none  [the longest x1 117 us: on_device(): lax.all_gather(low_up, 'fsdp', axis=0, tiled=True)]
    pallas_call x0 -> x1, Pallas kernels: none -> 194 us  [gather_all(): pl.pallas_call(partial(gather_kernel, dims), out_shape=out_shape, in_spec...]
    ppermute x0 -> x48, waiting for transfers between devices: none -> 135 us  [the longest x39 134 us: move(): return lax.ppermute(value, ('dp', 'fsdp'), pairs)]
    psum x1 -> x0, waiting for transfers between devices: 56.7 us -> none  [on_device(): lax.psum(summed[0].astype(jnp.bfloat16), 'dp').astype(jnp.float32)]
    ppermute x0 -> x48, starting transfers between devices: none -> 55.8 us  [the longest x39 47.2 us: move(): return lax.ppermute(value, ('dp', 'fsdp'), pairs)]
    unnamed x13 -> x0, waiting for transfers between devices: 51.7 us -> none
    all_to_all x8 -> x0, waiting for transfers between devices: 48.4 us -> none  [the longest x2 27.8 us: micro_step(): lax.all_to_all(skip_outgoing, 'dp', split_axis=0, concat_axis=0, tiled=True)]
  transfers between devices with their start and end apart: 20 -> 48, of which waited for: 14 -> 10; matrix products, arithmetic and copies ran while one was open for 17% -> 40% of each run, Pallas kernels for 0% -> 0%
where the time goes in v1:
time: 806 us; the launch traced here: 803 us
  Pallas kernels  194 us (24%)
  local copies, waits for them, and re-layouts  170 us (21%)
  matrix products  141 us (17%)
  waiting for transfers between devices  135 us (17%)
  other arithmetic  58.9 us (7%)
  starting transfers between devices  55.8 us (7%)
  blocking collectives  39.6 us (5%)
  between operations  8.45 us (1%)
    pallas_call x1, Pallas kernels, gather_all(): pl.pallas_call(partial(gather_kernel, dims), out_shape=out_shape, in_spec...  194 us
    ppermute x39, waiting for transfers between devices, move(): return lax.ppermute(value, ('dp', 'fsdp'), pairs)  134 us
    dot_general x5, matrix products, dot_rows(): return jnp.dot(left, right, preferred_element_type=F32)  51.5 us
    ppermute x39, starting transfers between devices, move(): return lax.ppermute(value, ('dp', 'fsdp'), pairs)  47.2 us
    dynamic_slice x8, local copies, waits for them, and re-layouts, pick(): return lax.dynamic_index_in_dim(value, index, axis, keepdims=False)  45.3 us
    psum x1, blocking collectives, on_device(): lax.psum(jnp.stack([grad_gain_one, grad_gain_two]), ('dp', 'fsdp'))  39.6 us
    unnamed x217, local copies, waits for them, and re-layouts  39.2 us
    dot_general x5, matrix products, weight_gradient(): lax.dot_general(left_all, right_all, (((0,), (0,)), ((), ())), preferred_...  30.6 us
  transfers between devices with their start and end apart: 48, of which 10 were waited for; matrix products, arithmetic and copies ran while one was open for 40% of the time, Pallas kernels for 0%

profile of v1, /device:TPU:0, one launch (start us, length us, event | category | flops | bytes accessed | tf_op | source)
XLA Modules:
  0.0 803.0 jit_solution(16604567083543694041)
XLA Ops:
  13.7 194.1 %gather_weights.1 = (bf16[4,2,256,1024]{3,2,1,0:T(8,128)(2,1)}, bf16[4,2,128,3072]{3,2,1,0:T(8,128)(2,1)}, bf16[4,2,128,1024]{3,2,1,0:T(8,128)(2,1)}, bf16[4,2,1...) custom-call(bf16[256,1024]{1,0:T(8,128)(2,1)} %convert_element_type., ...), custom_call_target="tpu_custom_call" | custom-call | tf_op jit(solution)/shard_map/gather_weights/pallas_call | solution.py:198
  257.5 6.8 fusion.149
  264.7 28.0 %fusion.6 = (bf16[512,4096]{1,0:T(8,128)(2,1)S(1)}, bf16[512,4096]{1,0:T(8,128)(2,1)}) fusion(f32[512,4096]{1,0:T(8,128)} %fusion.149, bf16[512,1024]{1,0:T(8,128)(2,1)S(1)} %multiply_convert_fusion.4, bf16[1024,4096]{1,0:T(8,128)(2,1)} %bitcast.322), kind=kOutput, calls=%fused_computation.8 | convolution fusion | flops 4341104640 | bytes 26214400 | tf_op jit(solution)/shard_map/dot_general | solution.py:316
  310.7 6.2 convolution_bitcast_fusion
  316.9 5.6 multiply_reduce_fusion
  335.4 7.3 multiply_reduce_fusion.2
  366.2 7.8 reshape.376
  374.0 10.3 %add_convert_fusion.1 = bf16[512,1024]{1,0:T(8,128)(2,1)} fusion(f32[512,1024]{1,0:T(8,128)S(1)} %get-tuple-element.143, bf16[512,4096]{1,0:T(8,128)(2,1)} %get-tuple-element.97, bf16[4096,1024]{1,0:T(8,128)(2,1)} %bitcast.318), kind=kOutput, calls=%fused_computation.98 | convolution fusion | flops 4296015872 | bytes 15728640 | tf_op jit(solution)/shard_map/dot_general | solution.py:316
  384.3 9.9 %constant_dynamic-slice_fusion.5 = (bf16[512,1,2048]{2,1,0:T(2,128)(2,1)}, bf16[512,1,2048]{2,1,0:T(2,128)(2,1)}) fusion(bf16[512,2,2048]{2,1,0:T(2,128)(2,1)S(1)} %copy-done.3, s32[]{:T(128)S(6)} %select_n.315, s32[]{:T(128)S(6)} %select_n.316), kind=kLoop, calls=%fused_computation.234 | loop fusion | bytes 8388616 | tf_op jit(solution)/shard_map/jit(dynamic_index_in_dim)/dynamic_slice | solution.py:252
  435.9 39.6 %psum.7 = f32[2,8,128]{2,0,1:T(2,128)S(1)} all-reduce(f32[2,8,128]{2,0,1:T(2,128)S(1)} %maximum_bitcast_fusion), channel_id=1, replica_groups=mesh['dp'=4,'fsdp'=8] {'dp','fsdp'}, use_global_device_ids=true, to_apply=%region_27.28 | all-reduce | flops 2048 | bytes 16384 | tf_op jit(solution)/shard_map/psum | solution.py:510
  485.0 7.2 convolution_convert_fusion.2
  492.2 7.7 reshape_reshape.6
  500.6 11.0 %constant_dynamic-slice_fusion.9 = (bf16[4,2,128,1,768]{4,3,2,1,0:T(2,128)(2,1)}, bf16[4,2,128,1,768]{4,3,2,1,0:T(2,128)(2,1)S(1)}) fusion(bf16[4,2,128,2,768]{4,3,2,1,0:T(2,128)(2,1)} %reshape_reshape.6, s32[]{:T(128)S(6)} %select_n.331, s32[]{:T(128)S(6)} %select_n.333), kind=kLoop, calls=%fused_computation.238 | loop fusion | bytes 6291464 | tf_op jit(solution)/shard_map/jit(dynamic_index_in_dim)/dynamic_slice | solution.py:252
  525.5 8.9 %fusion.25 = bf16[1024,2048]{1,0:T(8,128)(2,1)} fusion(bf16[512,2048]{1,0:T(8,128)(2,1)} %collective-permute-done.29, bf16[512,2048]{1,0:T(8,128)(2,1)S(1)} %bitcast.286, bf16[512,1024]{1,0:T(8,128)(2,1)} %collective-permute-done.28, bf16[512,1024]{1,0:T(8,128)(2,1)S(1)} %copy-done.62), kind=kOutput, calls=%fused_computation.38 | convolution fusion | flops 4309647360 | bytes 10485760 | tf_op jit(solution)/shard_map/dot_general | solution.py:274
  534.4 7.8 reshape_reshape.7
  542.2 10.3 %constant_dynamic-slice_fusion.3 = (bf16[4,2,128,1,1024]{4,3,2,1,0:T(2,128)(2,1)S(1)}, bf16[4,2,128,1,1024]{4,3,2,1,0:T(2,128)(2,1)S(1)}) fusion(bf16[4,2,128,2,1024]{4,3,2,1,0:T(2,128)(2,1)} %reshape_reshape.7, s32[]{:T(128)S(6)} %select_n.331, s32[]{:T(128)S(6)} %select_n.333), kind=kLoop, calls=%fused_computation.232 | loop fusion | bytes 8388616 | tf_op jit(solution)/shard_map/jit(dynamic_index_in_dim)/dynamic_slice | solution.py:252
  554.8 6.9 fusion.12
  570.9 29.6 %collective-permute-done.30 = bf16[4,2,128,1024]{3,2,1,0:T(8,128)(2,1)S(1)} collective-permute-done((bf16[4,2,128,1024]{3,2,1,0:T(8,128)(2,1)S(1)}, bf16[4,2,128,1024]{3,2,1,0:T(8,128)(2,1)S(1)}, u32[]{:S(2)}, u32[]{:S(2)}) %collective-permute-start.30) | collective-permute-done | bytes 2097184 | tf_op jit(solution)/shard_map/ppermute | solution.py:232
  609.4 18.1 %collective-permute-done.14 = bf16[4,128,768]{2,1,0:T(8,128)(2,1)S(1)} collective-permute-done((bf16[4,128,768]{2,1,0:T(8,128)(2,1)S(1)}, bf16[4,128,768]{2,1,0:T(8,128)(2,1)S(1)}, u32[]{:S(2)}, u32[]{:S(2)}) %collective-permute-start.14) | collective-permute-done | bytes 786464 | tf_op jit(solution)/shard_map/ppermute | solution.py:232
  633.7 14.8 %collective-permute-done.31 = bf16[4,128,1024]{2,1,0:T(8,128)(2,1)S(1)} collective-permute-done((bf16[4,128,1024]{2,1,0:T(8,128)(2,1)S(1)}, bf16[4,128,1024]{2,1,0:T(8,128)(2,1)S(1)}, u32[]{:S(2)}, u32[]{:S(2)}) %collective-permute-start.31) | collective-permute-done | bytes 1048608 | tf_op jit(solution)/shard_map/ppermute | solution.py:232
  653.6 33.0 %collective-permute-done.41 = bf16[512,512]{1,0:T(8,128)(2,1)S(1)} collective-permute-done((bf16[512,512]{1,0:T(8,128)(2,1)S(1)}, bf16[512,512]{1,0:T(8,128)(2,1)S(1)}, u32[]{:S(2)}, u32[]{:S(2)}) %collective-permute-start.41) | collective-permute-done | bytes 524320 | tf_op jit(solution)/shard_map/ppermute | solution.py:232
  689.2 11.7 %collective-permute-start.16 = (bf16[128,768]{1,0:T(8,128)(2,1)S(1)}, bf16[128,768]{1,0:T(8,128)(2,1)S(1)}, u32[]{:S(2)}, u32[]{:S(2)}) collective-permute-start(bf16[128,768]{1,0:T(8,128)(2,1)S(1)} %get-tuple-element.132), channel_id=1, source_target_pairs={{0,4},{1,5},{2,6},{3,7},{4,0},{5,1},{6,2},{7,3},{8,12},{9,13},{10,... | collective-permute-start | bytes 589832 | tf_op jit(solution)/shard_map/ppermute | solution.py:232
  700.9 9.0 %collective-permute-done.33 = bf16[128,1024]{1,0:T(8,128)(2,1)S(1)} collective-permute-done((bf16[128,1024]{1,0:T(8,128)(2,1)S(1)}, bf16[128,1024]{1,0:T(8,128)(2,1)S(1)}, u32[]{:S(2)}, u32[]{:S(2)}) %collective-permute-start.33) | collective-permute-done | bytes 262176 | tf_op jit(solution)/shard_map/ppermute | solution.py:232
  720.1 20.0 %collective-permute-done.18 = bf16[128,768]{1,0:T(8,128)(2,1)S(1)} collective-permute-done((bf16[128,768]{1,0:T(8,128)(2,1)S(1)}, bf16[128,768]{1,0:T(8,128)(2,1)S(1)}, u32[]{:S(2)}, u32[]{:S(2)}) %collective-permute-start.18) | collective-permute-done | bytes 196640 | tf_op jit(solution)/shard_map/ppermute | solution.py:232
  (450 shorter events, 282.9 us)
Async XLA Ops:
  212.9 301.3 %collective-permute-start.3 = (bf16[512,2048]{1,0:T(8,128)(2,1)}, bf16[512,2048]{1,0:T(8,128)(2,1)}, u32[]{:S(2)}, u32[]{:S(2)}) collective-permute-start(bf16[512,2048]{1,0:T(8,128)(2,1)} %bitcast.8), channel_id=1, source_target_pairs={{0,8},{1,9},{2,10},{3,11},{4,12},{5,13},{6,14},{7,15},{8,0},{9,1},... | collective-permute-start | bytes 6291464 | tf_op jit(solution)/shard_map/ppermute | solution.py:232
  221.2 256.7 %collective-permute-start.11 = (bf16[512,1024]{1,0:T(8,128)(2,1)}, bf16[512,1024]{1,0:T(8,128)(2,1)}, u32[]{:S(2)}, u32[]{:S(2)}) collective-permute-start(bf16[512,1024]{1,0:T(8,128)(2,1)} %multiply_convert_fusion.5), channel_id=1, source_target_pairs={{0,8},{1,9},{2,10},{3,11},{4,12},{5,13},{6,14},{7,15},{8,0},{9,1},... | collective-permute-start | bytes 3145736 | tf_op jit(solution)/shard_map/ppermute | solution.py:232
  252.8 156.2 %collective-permute-start.20 = (bf16[512,1024]{0,1:T(8,128)(2,1)}, bf16[512,1024]{0,1:T(8,128)(2,1)}, u32[]{:S(2)}, u32[]{:S(2)}) collective-permute-start(bf16[512,1024]{0,1:T(8,128)(2,1)} %bitcast.121), channel_id=1, source_target_pairs={{0,8},{1,9},{2,10},{3,11},{4,12},{5,13},{6,14},{7,15},{8,0},{9,1},... | collective-permute-start | bytes 3145736 | tf_op jit(solution)/shard_map/ppermute | solution.py:232
  356.4 121.1 %collective-permute-start = (bf16[2,128,2048]{2,1,0:T(8,128)(2,1)}, bf16[2,128,2048]{2,1,0:T(8,128)(2,1)}, u32[]{:S(2)}, u32[]{:S(2)}) collective-permute-start(bf16[2,128,2048]{2,1,0:T(8,128)(2,1)} %get-tuple-element.106), channel_id=1, source_target_pairs={{0,8},{1,9},{2,10},{3,11},{4,12},{5,13},{6,14},{7,15},{8,16},{9,17... | collective-permute-start | bytes 3145736 | tf_op jit(solution)/shard_map/ppermute | solution.py:503
  365.2 43.9 %collective-permute-start.21 = (bf16[512,512]{1,0:T(8,128)(2,1)}, bf16[512,512]{1,0:T(8,128)(2,1)}, u32[]{:S(2)}, u32[]{:S(2)}) collective-permute-start(bf16[512,512]{1,0:T(8,128)(2,1)} %bitcast.259), channel_id=1, source_target_pairs={{0,8},{1,9},{2,10},{3,11},{4,12},{5,13},{6,14},{7,15},{8,0},{9,1},... | collective-permute-start | bytes 1572872 | tf_op jit(solution)/shard_map/ppermute | solution.py:232
  409.0 73.5 %collective-permute-start.12 = (bf16[512,1536]{1,0:T(8,128)(2,1)}, bf16[512,1536]{1,0:T(8,128)(2,1)}, u32[]{:S(2)}, u32[]{:S(2)}) collective-permute-start(bf16[512,1536]{1,0:T(8,128)(2,1)} %bitcast.46), channel_id=1, source_target_pairs={{0,8},{1,9},{2,10},{3,11},{4,12},{5,13},{6,14},{7,15},{8,0},{9,1},... | collective-permute-start | bytes 4718600 | tf_op jit(solution)/shard_map/ppermute | solution.py:232
  412.9 63.2 %collective-permute-start.22 = (bf16[4,128,512]{2,1,0:T(8,128)(2,1)}, bf16[4,128,512]{2,1,0:T(8,128)(2,1)}, u32[]{:S(2)}, u32[]{:S(2)}) collective-permute-start(bf16[4,128,512]{2,1,0:T(8,128)(2,1)} %dynamic-slice_bitcast_fusion.10), channel_id=1, source_target_pairs={{0,1},{1,0},{2,3},{3,2},{4,5},{5,4},{6,7},{7,6},{8,9},{9,8},{10,11... | collective-permute-start | bytes 1572872 | tf_op jit(solution)/shard_map/ppermute | solution.py:232
  476.1 78.5 %collective-permute-start.37 = (bf16[512,4096]{1,0:T(8,128)(2,1)}, bf16[512,4096]{1,0:T(8,128)(2,1)}, u32[]{:S(2)}, u32[]{:S(2)}) collective-permute-start(bf16[512,4096]{1,0:T(8,128)(2,1)} %get-tuple-element.97), channel_id=1, source_target_pairs={{0,8},{1,9},{2,10},{3,11},{4,12},{5,13},{6,14},{7,15},{8,0},{9,1},... | collective-permute-start | bytes 12582920 | tf_op jit(solution)/shard_map/ppermute | solution.py:232
  477.5 46.0 %collective-permute-start.29 = (bf16[512,2048]{1,0:T(8,128)(2,1)}, bf16[512,2048]{1,0:T(8,128)(2,1)}, u32[]{:S(2)}, u32[]{:S(2)}) collective-permute-start(bf16[512,2048]{1,0:T(8,128)(2,1)} %bitcast.287), channel_id=1, source_target_pairs={{0,8},{1,9},{2,10},{3,11},{4,12},{5,13},{6,14},{7,15},{8,0},{9,1},... | collective-permute-start | bytes 6291464 | tf_op jit(solution)/shard_map/ppermute | solution.py:232
  514.0 39.3 %collective-permute-start.38 = (bf16[512,512]{1,0:T(8,128)(2,1)}, bf16[512,512]{1,0:T(8,128)(2,1)}, u32[]{:S(2)}, u32[]{:S(2)}) collective-permute-start(bf16[512,512]{1,0:T(8,128)(2,1)} %bitcast.263), channel_id=1, source_target_pairs={{0,8},{1,9},{2,10},{3,11},{4,12},{5,13},{6,14},{7,15},{8,0},{9,1},... | collective-permute-start | bytes 1572872 | tf_op jit(solution)/shard_map/ppermute | solution.py:232
  514.2 50.7 %collective-permute-start.13 = (bf16[4,2,128,768]{3,2,1,0:T(8,128)(2,1)}, bf16[4,2,128,768]{3,2,1,0:T(8,128)(2,1)}, u32[]{:S(2)}, u32[]{:S(2)}) collective-permute-start(bf16[4,2,128,768]{3,2,1,0:T(8,128)(2,1)} %bitcast.258), channel_id=1, source_target_pairs={{0,16},{1,17},{2,18},{3,19},{4,20},{5,21},{6,22},{7,23},{8,24},{9,... | collective-permute-start | bytes 4718600 | tf_op jit(solution)/shard_map/ppermute | solution.py:232
  523.4 39.2 %collective-permute-start.26 = (bf16[128,512]{1,0:T(8,128)(2,1)S(1)}, bf16[128,512]{1,0:T(8,128)(2,1)S(1)}, u32[]{:S(2)}, u32[]{:S(2)}) collective-permute-start(bf16[128,512]{1,0:T(8,128)(2,1)S(1)} %fusion.120), channel_id=1, source_target_pairs={{0,16},{1,17},{2,18},{3,19},{4,20},{5,21},{6,22},{7,23},{8,24},{9,... | collective-permute-start | bytes 393224 | tf_op jit(solution)/shard_map/ppermute | solution.py:248
  523.5 39.2 %collective-permute-start.5 = (bf16[4,256,512]{2,1,0:T(8,128)(2,1)}, bf16[4,256,512]{2,1,0:T(8,128)(2,1)}, u32[]{:S(2)}, u32[]{:S(2)}) collective-permute-start(bf16[4,256,512]{2,1,0:T(8,128)(2,1)} %dynamic-slice_bitcast_fusion.2), channel_id=1, source_target_pairs={{0,1},{1,0},{2,3},{3,2},{4,5},{5,4},{6,7},{7,6},{8,9},{9,8},{10,11... | collective-permute-start | bytes 3145736 | tf_op jit(solution)/shard_map/ppermute | solution.py:232
  553.3 47.2 %collective-permute-start.30 = (bf16[4,2,128,1024]{3,2,1,0:T(8,128)(2,1)S(1)}, bf16[4,2,128,1024]{3,2,1,0:T(8,128)(2,1)S(1)}, u32[]{:S(2)}, u32[]{:S(2)}) collective-permute-start(bf16[4,2,128,1024]{3,2,1,0:T(8,128)(2,1)S(1)} %bitcast.288), channel_id=1, source_target_pairs={{0,16},{1,17},{2,18},{3,19},{4,20},{5,21},{6,22},{7,23},{8,24},{9,... | collective-permute-start | bytes 6291464 | tf_op jit(solution)/shard_map/ppermute | solution.py:232
  562.0 65.7 %collective-permute-start.39 = (bf16[4,512,512]{2,1,0:T(8,128)(2,1)S(1)}, bf16[4,512,512]{2,1,0:T(8,128)(2,1)S(1)}, u32[]{:S(2)}, u32[]{:S(2)}) collective-permute-start(bf16[4,512,512]{2,1,0:T(8,128)(2,1)S(1)} %dynamic-slice_bitcast_fusion), channel_id=1, source_target_pairs={{0,1},{1,0},{2,3},{3,2},{4,5},{5,4},{6,7},{7,6},{8,9},{9,8},{10,11... | collective-permute-start | bytes 6291464 | tf_op jit(solution)/shard_map/ppermute | solution.py:232
  566.8 60.6 %collective-permute-start.14 = (bf16[4,128,768]{2,1,0:T(8,128)(2,1)S(1)}, bf16[4,128,768]{2,1,0:T(8,128)(2,1)S(1)}, u32[]{:S(2)}, u32[]{:S(2)}) collective-permute-start(bf16[4,128,768]{2,1,0:T(8,128)(2,1)S(1)} %dynamic-slice_bitcast_fusion.6), channel_id=1, source_target_pairs={{0,1},{1,0},{2,3},{3,2},{4,5},{5,4},{6,7},{7,6},{8,9},{9,8},{10,11... | collective-permute-start | bytes 2359304 | tf_op jit(solution)/shard_map/ppermute | solution.py:232
  603.7 148.3 %collective-permute-start.1 = (bf16[2,128,2048]{2,1,0:T(8,128)(2,1)}, bf16[2,128,2048]{2,1,0:T(8,128)(2,1)}, u32[]{:S(2)}, u32[]{:S(2)}) collective-permute-start(bf16[2,128,2048]{2,1,0:T(8,128)(2,1)} %get-tuple-element.105), channel_id=1, source_target_pairs={{0,16},{1,17},{2,18},{3,19},{4,20},{5,21},{6,22},{7,23},{8,24},{9,... | collective-permute-start | bytes 3145736 | tf_op jit(solution)/shard_map/ppermute | solution.py:503
  604.8 43.7 %collective-permute-start.31 = (bf16[4,128,1024]{2,1,0:T(8,128)(2,1)S(1)}, bf16[4,128,1024]{2,1,0:T(8,128)(2,1)S(1)}, u32[]{:S(2)}, u32[]{:S(2)}) collective-permute-start(bf16[4,128,1024]{2,1,0:T(8,128)(2,1)S(1)} %dynamic-slice_bitcast_fusion.1), channel_id=1, source_target_pairs={{0,1},{1,0},{2,3},{3,2},{4,5},{5,4},{6,7},{7,6},{8,9},{9,8},{10,11... | collective-permute-start | bytes 3145736 | tf_op jit(solution)/shard_map/ppermute | solution.py:232
  631.0 55.6 %collective-permute-start.41 = (bf16[512,512]{1,0:T(8,128)(2,1)S(1)}, bf16[512,512]{1,0:T(8,128)(2,1)S(1)}, u32[]{:S(2)}, u32[]{:S(2)}) collective-permute-start(bf16[512,512]{1,0:T(8,128)(2,1)S(1)} %get-tuple-element.117), channel_id=1, source_target_pairs={{0,4},{1,5},{2,6},{3,7},{4,0},{5,1},{6,2},{7,3},{8,12},{9,13},{10,... | collective-permute-start | bytes 1572872 | tf_op jit(solution)/shard_map/ppermute | solution.py:232
  631.7 54.9 %collective-permute-start.40 = (bf16[512,512]{1,0:T(8,128)(2,1)S(1)}, bf16[512,512]{1,0:T(8,128)(2,1)S(1)}, u32[]{:S(2)}, u32[]{:S(2)}) collective-permute-start(bf16[512,512]{1,0:T(8,128)(2,1)S(1)} %get-tuple-element.115), channel_id=1, source_target_pairs={{0,2},{1,3},{2,4},{3,5},{4,6},{5,7},{6,0},{7,1},{8,10},{9,11},{10,... | collective-permute-start | bytes 1572872 | tf_op jit(solution)/shard_map/ppermute | solution.py:232
  648.5 39.5 %collective-permute-start.17 = (bf16[128,768]{1,0:T(8,128)(2,1)S(1)}, bf16[128,768]{1,0:T(8,128)(2,1)S(1)}, u32[]{:S(2)}, u32[]{:S(2)}) collective-permute-start(bf16[128,768]{1,0:T(8,128)(2,1)S(1)} %get-tuple-element.131), channel_id=1, source_target_pairs={{0,6},{1,7},{2,0},{3,1},{4,2},{5,3},{6,4},{7,5},{8,14},{9,15},{10,... | collective-permute-start | bytes 589832 | tf_op jit(solution)/shard_map/ppermute | solution.py:232
  651.5 37.7 %collective-permute-start.34 = (bf16[128,1024]{1,0:T(8,128)(2,1)S(1)}, bf16[128,1024]{1,0:T(8,128)(2,1)S(1)}, u32[]{:S(2)}, u32[]{:S(2)}) collective-permute-start(bf16[128,1024]{1,0:T(8,128)(2,1)S(1)} %get-tuple-element.121), channel_id=1, source_target_pairs={{0,6},{1,7},{2,0},{3,1},{4,2},{5,3},{6,4},{7,5},{8,14},{9,15},{10,... | collective-permute-start | bytes 786440 | tf_op jit(solution)/shard_map/ppermute | solution.py:232
  709.9 40.8 %collective-permute-start.43 = (bf16[512,512]{1,0:T(8,128)(2,1)S(1)}, bf16[512,512]{1,0:T(8,128)(2,1)}, u32[]{:S(2)}, u32[]{:S(2)}) collective-permute-start(bf16[512,512]{1,0:T(8,128)(2,1)S(1)} %fusion.92), channel_id=1, source_target_pairs={{0,16},{1,17},{2,18},{3,19},{4,20},{5,21},{6,22},{7,23},{8,24},{9,... | collective-permute-start | bytes 1572872 | tf_op jit(solution)/shard_map/ppermute | solution.py:248
  712.0 53.1 %collective-permute-start.2 = (bf16[2,128,2048]{2,1,0:T(8,128)(2,1)}, bf16[2,128,2048]{2,1,0:T(8,128)(2,1)}, u32[]{:S(2)}, u32[]{:S(2)}) collective-permute-start(bf16[2,128,2048]{2,1,0:T(8,128)(2,1)} %get-tuple-element.104), channel_id=1, source_target_pairs={{0,24},{1,25},{2,26},{3,27},{4,28},{5,29},{6,30},{7,31},{8,0},{9,1... | collective-permute-start | bytes 3145736 | tf_op jit(solution)/shard_map/ppermute | solution.py:503
  (123 other events, 1017.9 us)

commit v2 on v1

v2 whole, which is shorter than its diff:
```python
from functools import partial
import math

import jax
import jax.numpy as jnp
from jax import lax
from jax.experimental import pallas as pl
from jax.experimental.pallas import tpu as pltpu
from jax.sharding import PartitionSpec as P

D = 1024
HEADS = 16
HD = 64
FF = 4096
STEP = 5
CORES = 2
OUTER = 4

BETA_FIRST = 0.5
BETA_SECOND = 0.5
ADAM_EPSILON = 1e-08
WEIGHT_DECAY = 0.01
NORM_EPSILON = 1e-05

BF16 = jnp.bfloat16
F32 = jnp.float32
MESH = pl.DeviceIdType.MESH

GATHER_UNITS = (
    (0, 0, 2, False), (0, 1, 2, False), (1, 0, 2, True), (1, 1, 2, True), (2, 0, 1, False),
    (3, 0, 2, True), (3, 1, 2, True),
    (4, 0, 4, False), (4, 1, 4, False), (4, 2, 4, False), (4, 3, 4, False),
)
VMEM_LIMIT = 63 * 2**20
REDUCE_UNITS = (
    (4, 0, 2, False), (4, 1, 2, False), (3, 0, 2, True), (3, 1, 2, True), (2, 0, 1, False),
    (1, 0, 2, False), (1, 1, 2, False), (0, 0, 2, False), (0, 1, 2, False),
)


def sizes():
    n_dp, n_fsdp = lax.axis_size("dp"), lax.axis_size("fsdp")
    return n_dp // CORES, CORES, OUTER, n_fsdp // OUTER


def place():
    rows, cores, outer, inner = sizes()
    dp, fsdp = lax.axis_index("dp"), lax.axis_index("fsdp")
    return dp // cores, lax.rem(dp, cores), fsdp // inner, lax.rem(fsdp, inner)


def turn(value, step, size):
    return lax.rem(value + (step + size) % size, size)


class Copies:
    def __init__(self, send_sem, recv_sem, local_sem):
        self.send_sem, self.recv_sem, self.local_sem = send_sem, recv_sem, local_sem
        self.remotes, self.locals, self.sent = 0, 0, []

    def remote(self, src, dst, land, device):
        index = self.remotes
        self.remotes += 1
        sems = dict(send_sem=self.send_sem.at[index], recv_sem=self.recv_sem.at[index])
        copy = pltpu.make_async_remote_copy(
            src_ref=src, dst_ref=dst, device_id=device, device_id_type=MESH, **sems
        )
        copy.start()
        self.sent.append(copy)
        return pltpu.make_async_remote_copy(
            src_ref=src, dst_ref=land, device_id=device, device_id_type=MESH, **sems
        )

    def local(self, src, dst):
        index = self.locals
        self.locals += 1
        copy = pltpu.make_async_copy(src, dst, self.local_sem.at[index])
        copy.start()
        return copy


def whole(ref, first=0, width=None):
    n_a, n_b, rows, columns = ref.shape
    width = columns if width is None else width
    return ref[:, :, :, pl.ds(first, width)].reshape(n_a * n_b * rows, width)


def row_loop(rows, chunk, body):
    @pl.loop(0, rows // chunk)
    def _(i):
        body(pl.ds(pl.multiple_of(i * chunk, chunk), chunk))


def norm_into(hidden, gain_row, target):
    def body(at):
        centre = hidden[at, :]
        centre = centre - jnp.mean(centre, axis=-1, keepdims=True)
        spread = jnp.mean(centre * centre, axis=-1, keepdims=True)
        target[at, :] = (centre * lax.rsqrt(spread + NORM_EPSILON) * gain_row).astype(BF16)

    row_loop(hidden.shape[0], 64, body)


GELU_SCALE = math.sqrt(2.0 / math.pi)


def gelu(u):
    return 0.5 * u * (1.0 + jnp.tanh(GELU_SCALE * (u + 0.044715 * (u * u * u))))


def head_probs(queries, keys_all, distance, same, slope):
    scores = lax.dot_general(
        queries, keys_all, (((1,), (1,)), ((), ())), preferred_element_type=F32
    )
    scores = jnp.where(same, scores * HD ** (-0.5) - slope * distance, -1e30)
    weights = jnp.exp(scores - jnp.max(scores, axis=-1, keepdims=True))
    return weights / jnp.sum(weights, axis=-1, keepdims=True)


def pair_mask(rows):
    lane = lax.broadcasted_iota(jnp.int32, (rows, 2 * HD), 1)
    return lane < HD


def forward_kernel(dims, *refs):
    n_y, n_c, n_a, n_b = dims
    masters, payload, gains, pack_hot, ids_down, ids_across, slopes = (
        refs[:5], refs[5], refs[6], refs[7], refs[8], refs[9], refs[10]
    )
    refs = refs[11:]
    fulls_out, refs = refs[:5], refs[5:]
    packed_out, base_out, qkv_out, mixed_out, after_out, up_out, act_out = refs[:7]
    one_out, two_out, frames_out, gains_out = refs[7:11]
    refs = refs[11:]
    fulls, refs = refs[:5], refs[5:]
    stage, arrived, hot, gains_all, packed, base, one, qkv, mixed, after, two, up, out = refs[:13]
    send_sem, recv_sem, local_sem = refs[13:]
    dp, fsdp = lax.axis_index("dp"), lax.axis_index("fsdp")
    y, c, a, b = dp // n_c, lax.rem(dp, n_c), fsdp // n_b, lax.rem(fsdp, n_b)
    n_dp, n_fsdp = n_y * n_c, n_a * n_b
    copies = Copies(send_sem, recv_sem, local_sem)
    remote, local = copies.remote, copies.local
    micro = payload.shape[0]
    slots = payload.shape[2]

    staged = {}

    def load(m):
        rows, columns = masters[m].shape
        view = stage.at[m % 2, pl.ds(0, rows * columns // 1024)]
        if columns == 1024:
            staged[m] = [local(masters[m], view)]
        else:
            parts = columns // 1024
            staged[m] = [
                local(
                    masters[m].at[:, pl.ds(p * 1024, 1024)],
                    stage.at[m % 2, pl.ds(p * rows, rows)],
                )
                for p in range(parts)
            ]

    load(0)
    load(1)
    frames = []
    slab = n_dp * slots

    def slot(group):
        return pl.ds(pl.multiple_of(group * slots, 16), slots)

    gain_copies = []
    own_gains = local(gains, gains_all.at[fsdp])
    hot_copy = local(pack_hot, hot)
    for k in range(1, n_dp):
        to, back = turn(dp, k, n_dp), turn(dp, -k, n_dp)
        for i in range(micro):
            frames.append(
                remote(
                    payload.at[i, to], arrived.at[i, slot(dp)], arrived.at[i, slot(back)], (to, fsdp)
                )
            )
    own_frames = [local(payload.at[i, dp], arrived.at[i, slot(dp)]) for i in range(micro)]

    units = []
    for m, part, parts, shared in GATHER_UNITS:
        width = masters[m].shape[1] // parts
        units.append((m, part * width, width, shared and width // (n_c * n_y) % 128 == 0))
    state = [{"x": [], "y": [], "c": []} for _ in units]

    def columns(u, of_c, of_y):
        m, first, width, shared = units[u]
        if shared:
            step = width // (n_c * n_y)
            return pl.ds(pl.multiple_of(first + (of_c * n_y + of_y) * step, 128), step)
        step = width // n_c
        return pl.ds(pl.multiple_of(first + of_c * step, 128), step)

    def convert(m):
        for copy in staged[m]:
            copy.wait()
        rows, width = masters[m].shape

        def body(at):
            for p in range(width // 1024):
                low = stage[m % 2, pl.ds(at.start + p * rows, at.size), :].astype(BF16)
                fulls[m][a, b, at, pl.ds(p * 1024, 1024)] = low

        row_loop(rows, 32, body)

    def stage_z(u):
        m = units[u][0]
        cols = columns(u, c, y)
        view = fulls[m].at[a, b, :, cols]
        state[u]["z"] = [
            remote(
                view, view, fulls[m].at[turn(a, -k, n_a), b, :, cols],
                (dp, turn(a, k, n_a) * n_b + b),
            )
            for k in range(1, n_a)
        ]

    def spread(u, block_a, block_b, of_y, to_y):
        m, first, width, shared = units[u]
        full = fulls[m]
        view = full.at[block_a, block_b, :, columns(u, c, of_y)]
        if to_y and shared:
            for k in range(1, n_y):
                source = turn(y, -k, n_y)
                landing = full.at[block_a, block_b, :, columns(u, c, source)]
                copy = remote(view, view, landing, (turn(y, k, n_y) * n_c + c, fsdp))
                state[u]["y"].append((copy, block_a, block_b, source))
        landing = full.at[block_a, block_b, :, columns(u, 1 - c, of_y)]
        state[u]["c"].append(remote(view, view, landing, (y * n_c + 1 - c, fsdp)))

    def send_x(u, step):
        m = units[u][0]
        cols, block_a = columns(u, c, y), turn(a, -step, n_a)
        view = fulls[m].at[block_a, b, :, cols]
        for k in range(1, n_b):
            landing = fulls[m].at[block_a, turn(b, -k, n_b), :, cols]
            state[u]["x"].append(remote(view, view, landing, (dp, a * n_b + turn(b, k, n_b))))

    def stage_own(u):
        send_x(u, 0)

    def stage_x(u):
        for k in range(1, n_a):
            state[u]["z"][k - 1].wait_recv()
            send_x(u, k)
            spread(u, turn(a, -k, n_a), b, y, True)

    def stage_s(u):
        for copy in state[u]["x"]:
            copy.wait_recv()
        for k in range(1, n_b):
            spread(u, slice(None), turn(b, -k, n_b), y, True)

    def stage_c(u):
        for copy, block_a, block_b, source in state[u]["y"]:
            copy.wait_recv()
            spread(u, block_a, block_b, source, False)

    outgoing = []

    def finish(u):
        m, first, width, shared = units[u]
        for copy in state[u]["c"]:
            copy.wait_recv()
        cols = pl.ds(first, width)
        outgoing.append(local(fulls[m].at[:, :, :, cols], fulls_out[m].at[:, :, :, cols]))

    for m in range(5):
        convert(m)
        if m + 2 < 5:
            load(m + 2)
        for u in range(len(units)):
            if units[u][0] == m:
                stage_z(u)
        if m == 0:
            stage_own(0)
            stage_own(1)
            for k in range(1, n_fsdp):
                to, back = turn(fsdp, k, n_fsdp), turn(fsdp, -k, n_fsdp)
                gain_copies.append(
                    remote(gains, gains_all.at[fsdp], gains_all.at[back], (dp, to))
                )

    count = len(units)

    def comm(u):
        if u + 2 < count:
            stage_own(u + 2)
        if u < count:
            stage_x(u)
        if u >= 1:
            stage_s(u - 1)

    tokens, width = base.shape
    per_pack = tokens // micro

    def make_packed():
        for copy in frames:
            copy.wait_recv()
        for copy in own_frames:
            copy.wait()
        hot_copy.wait()
        for i in range(micro):
            for half in range(2):
                cols = pl.ds(half * 1024, 1024)
                packed[pl.ds(i * per_pack, per_pack), cols] = jnp.dot(
                    hot[i], arrived[i, :, cols], preferred_element_type=F32
                ).astype(BF16)
        outgoing.append(local(packed, packed_out))

    gain_rows = []

    def make_gains():
        for copy in gain_copies:
            copy.wait_recv()
        own_gains.wait()
        outgoing.append(local(gains_all, gains_out))
        own = D // n_fsdp
        for row in range(2):
            gain_rows.append(
                jnp.concatenate([gains_all[f, pl.ds(row, 1), pl.ds(0, own)] for f in range(n_fsdp)], axis=1)
            )

    def make_base():
        for first in (0, 512):
            base[:, pl.ds(first, 512)] = jnp.dot(
                packed[...], whole(fulls[0], first, 512), preferred_element_type=F32
            )
        norm_into(base, gain_rows[0], one)
        outgoing.append(local(base, base_out))
        outgoing.append(local(one, one_out))

    def make_qkv():
        for first in range(0, 3 * D, 512):
            qkv[:, pl.ds(first, 512)] = jnp.dot(
                one[...], whole(fulls[1], first, 512), preferred_element_type=F32
            ).astype(BF16)
        outgoing.append(local(qkv, qkv_out))

    def attend(i):
        rows = pl.ds(i * per_pack, per_pack)
        position = lax.broadcasted_iota(jnp.int32, (per_pack, per_pack), 0)
        distance = jnp.abs(
            position - lax.broadcasted_iota(jnp.int32, (per_pack, per_pack), 1)
        ).astype(F32)
        first_head = pair_mask(per_pack)

        @pl.loop(0, HEADS // 2)
        def _(pair):
            def cols(part):
                return pl.ds(pl.multiple_of(part * D + pair * 2 * HD, 128), 2 * HD)

            same = ids_down[i] == ids_across[i]
            queries, keys_all, values_all = (qkv[rows, cols(part)] for part in range(3))
            results = []
            for head in range(2):
                mine = first_head if head == 0 else jnp.logical_not(first_head)
                slope = slopes[pl.ds(2 * pair + head, 1), :]
                probs = head_probs(
                    jnp.where(mine, queries, jnp.zeros_like(queries)), keys_all, distance, same, slope
                )
                results.append(
                    jnp.dot(probs.astype(BF16), values_all, preferred_element_type=F32)
                )
            mixed[rows, cols(0)] = jnp.where(first_head, results[0], results[1]).astype(BF16)

    def make_after():
        outgoing.append(local(mixed, mixed_out))
        for first in (0, 512):
            cols = pl.ds(first, 512)
            after[:, cols] = base[:, cols] + jnp.dot(
                mixed[...], whole(fulls[2], first, 512), preferred_element_type=F32
            )
        norm_into(after, gain_rows[1], two)
        outgoing.append(local(after, after_out))
        outgoing.append(local(two, two_out))

    up_copies = [None, None]
    half_ff = FF // 2

    def make_up(j):
        slot_now = j % 2
        if up_copies[slot_now] is not None:
            up_copies[slot_now].wait()
        cols = pl.ds(j * 512, 512)
        up[slot_now] = jnp.dot(
            two[...], whole(fulls[3], j * 512, 512), preferred_element_type=F32
        )
        up_copies[slot_now] = local(up.at[slot_now], up_out.at[:, cols])
        half, within = j * 512 // half_ff, j * 512 % half_ff

        def body(at):
            act = gelu(up[slot_now, at, :]).astype(BF16)
            arrived[half, at, pl.ds(within, 512)] = act

        row_loop(tokens, 64, body)

    def send_act(half):
        outgoing.append(
            local(arrived.at[half], act_out.at[:, pl.ds(half * half_ff, half_ff)])
        )

    def make_out(first, step):
        cols = pl.ds(first, step)
        weight = whole(fulls[4], first, step)
        total = after[:, cols] + jnp.dot(
            arrived[0], weight[:half_ff], preferred_element_type=F32
        )
        total += jnp.dot(arrived[1], weight[half_ff:], preferred_element_type=F32)
        out[:, cols] = total.astype(BF16)

    comm(0)
    comm(1)
    comm(2)
    make_gains()
    comm(3)
    make_packed()
    finish(0)
    finish(1)
    make_base()
    comm(4)
    stage_c(2)
    stage_c(3)
    comm(5)
    finish(2)
    finish(3)
    make_qkv()
    comm(6)
    attend(0)
    comm(7)
    finish(4)
    attend(1)
    make_after()
    stage_c(5)
    comm(8)
    finish(5)
    for j in range(4):
        make_up(j)
    send_act(0)
    stage_c(6)
    comm(9)
    finish(6)
    for j in range(4, 8):
        make_up(j)
    send_act(1)
    comm(10)
    finish(7)
    make_out(0, 256)
    comm(11)
    finish(8)
    make_out(256, 256)
    finish(9)
    make_out(512, 256)
    finish(10)
    make_out(768, 256)
    outgoing.append(local(out, frames_out))
    for copy in outgoing + [c for c in up_copies if c is not None]:
        copy.wait()
    for copy in copies.sent:
        copy.wait_send()


def forward_all(masters, payload, gains, pack_hot, source):
    dims = sizes()
    n_y, n_c, n_a, n_b = dims
    n_fsdp = n_a * n_b
    micro, n_dp, slots, _ = payload.shape
    per_pack = source.shape[1]
    tokens = micro * per_pack
    total = micro * (n_y * n_c - 1) + n_fsdp - 1
    for _, _, _, shared in GATHER_UNITS:
        groups = n_a - 1 + n_b - 1
        total += (n_a - 1) + n_a * (n_b - 1)
        total += (n_y - 1) * groups + n_y * groups if shared else groups
    shape = jax.ShapeDtypeStruct
    full_shapes = [(n_a, n_b) + master.shape for master in masters]
    out_shape = [shape(s, BF16) for s in full_shapes]
    out_shape += [
        shape((tokens, 2 * D), BF16), shape((tokens, D), F32), shape((tokens, 3 * D), BF16),
        shape((tokens, D), BF16), shape((tokens, D), F32), shape((tokens, FF), F32),
        shape((tokens, FF), BF16), shape((tokens, D), BF16), shape((tokens, D), BF16),
        shape((tokens, D), BF16), shape((n_fsdp,) + gains.shape, F32),
    ]
    anywhere = pl.BlockSpec(memory_space=pl.ANY)
    inside = pl.BlockSpec(memory_space=pltpu.VMEM)
    slopes = jnp.exp2(-8.0 * (jnp.arange(HEADS, dtype=F32) + 1.0) / HEADS)
    slopes = jnp.broadcast_to(slopes[:, None], (HEADS, per_pack))
    stage_rows = max(m.shape[0] * m.shape[1] // 1024 for m in masters)
    results = pl.pallas_call(
        partial(forward_kernel, dims),
        out_shape=out_shape,
        in_specs=[anywhere] * 8 + [inside] * 3,
        out_specs=[anywhere] * len(out_shape),
        scratch_shapes=[pltpu.VMEM(s, BF16) for s in full_shapes]
        + [
            pltpu.VMEM((2, stage_rows, 1024), F32),
            pltpu.VMEM((micro, n_dp * slots, 2 * D), BF16),
            pltpu.VMEM((micro, per_pack, n_dp * slots), BF16),
            pltpu.VMEM((n_fsdp,) + gains.shape, F32),
            pltpu.VMEM((tokens, 2 * D), BF16),
            pltpu.VMEM((tokens, D), F32),
            pltpu.VMEM((tokens, D), BF16),
            pltpu.VMEM((tokens, 3 * D), BF16),
            pltpu.VMEM((tokens, D), BF16),
            pltpu.VMEM((tokens, D), F32),
            pltpu.VMEM((tokens, D), BF16),
            pltpu.VMEM((2, tokens, 512), F32),
            pltpu.VMEM((tokens, D), BF16),
            pltpu.SemaphoreType.DMA((total,)),
            pltpu.SemaphoreType.DMA((total,)),
            pltpu.SemaphoreType.DMA((64,)),
        ],
        compiler_params=pltpu.CompilerParams(
            has_side_effects=True, vmem_limit_bytes=VMEM_LIMIT
        ),
        name="gather_and_forward",
    )(
        *masters, payload, gains, pack_hot,
        source[:, :, None], source[:, None, :], slopes,
    )
    return results


def move(value, axis, shift):
    n_y, n_c, n_a, n_b = sizes()
    dims = {"y": n_y, "c": n_c, "a": n_a, "b": n_b}
    pairs = []
    for source in range(n_y * n_c * n_a * n_b):
        at = {
            "y": source // (n_c * n_a * n_b),
            "c": source // (n_a * n_b) % n_c,
            "a": source // n_b % n_a,
            "b": source % n_b,
        }
        at[axis] = (at[axis] + shift) % dims[axis]
        target = ((at["y"] * n_c + at["c"]) * n_a + at["a"]) * n_b + at["b"]
        pairs.append((source, target))
    return lax.ppermute(value, ("dp", "fsdp"), pairs)


def swap(value, axis, mask):
    n_y, n_c, n_a, n_b = sizes()
    pairs = []
    for source in range(n_y * n_c * n_a * n_b):
        at = {
            "y": source // (n_c * n_a * n_b),
            "c": source // (n_a * n_b) % n_c,
            "a": source // n_b % n_a,
            "b": source % n_b,
        }
        at[axis] = at[axis] ^ mask
        target = ((at["y"] * n_c + at["c"]) * n_a + at["a"]) * n_b + at["b"]
        pairs.append((source, target))
    return lax.ppermute(value, ("dp", "fsdp"), pairs)


def pick(value, index, axis):
    return lax.dynamic_index_in_dim(value, index, axis, keepdims=False)


def add_all(values):
    total = values[0].astype(F32)
    for value in values[1:]:
        total = total + value.astype(F32)
    return total.astype(BF16)


def reduce_kernel(dims, shapes, *refs):
    n_y, n_c, n_a, n_b = dims
    count = 5
    lefts, rights, returning = refs[:count], refs[count : 2 * count], refs[2 * count]
    outs = refs[2 * count + 1 : 3 * count + 1]
    returned = refs[3 * count + 1]
    scratch = refs[3 * count + 2 :]
    sums, finals = scratch[:count], scratch[count : 2 * count]
    left_bufs, right_bufs = scratch[2 * count : 2 * count + 3], scratch[2 * count + 3 : 2 * count + 6]
    rest = scratch[2 * count + 6 :]
    landing = rest[: 3 * len(REDUCE_UNITS)]
    send_sem, recv_sem, local_sem, credit = rest[3 * len(REDUCE_UNITS) :]
    dp, fsdp = lax.axis_index("dp"), lax.axis_index("fsdp")
    y, c, a, b = dp // n_c, lax.rem(dp, n_c), fsdp // n_b, lax.rem(fsdp, n_b)
    n_dp = n_y * n_c
    used = [0, 0]
    sent = []
    other_core = (y * n_c + 1 - c, fsdp)
    slot_of = {4: 0, 0: 0, 3: 1, 1: 1, 2: 2}

    def remote(src, dst, land, device):
        index = used[0]
        used[0] += 1
        sems = dict(send_sem=send_sem.at[index], recv_sem=recv_sem.at[index])
        copy = pltpu.make_async_remote_copy(
            src_ref=src, dst_ref=dst, device_id=device, device_id_type=MESH, **sems
        )
        copy.start()
        sent.append(copy)
        return pltpu.make_async_remote_copy(
            src_ref=src, dst_ref=land, device_id=device, device_id_type=MESH, **sems
        )

    def local(src, dst):
        index = used[1]
        used[1] += 1
        copy = pltpu.make_async_copy(src, dst, local_sem.at[index])
        copy.start()
        return copy

    def turn(value, step, size):
        return lax.rem(value + (step + size) % size, size)

    tokens = lefts[0].shape[0]
    acts = {}

    def send_acts(m):
        depth, width = lefts[m].shape[1], rights[m].shape[1] // n_c
        left, right = left_bufs[slot_of[m]], right_bufs[slot_of[m]]
        mine = pl.ds(pl.multiple_of(c * width, 128), width)
        others = pl.ds(pl.multiple_of((1 - c) * width, 128), width)
        low, high = pl.ds(0, tokens), pl.ds(tokens, tokens)
        here = [
            local(rights[m].at[:, mine], right.at[low, pl.ds(0, width)]),
            local(lefts[m], left.at[low, pl.ds(0, depth)]),
        ]
        there = right.at[high, pl.ds(0, width)]
        away = [remote(rights[m].at[:, others], there, there, other_core)]
        there = left.at[high, pl.ds(0, depth)]
        away.append(remote(lefts[m], there, there, other_core))
        acts[m] = (here, away)

    def wait_acts(m):
        here, away = acts[m]
        for copy in here:
            copy.wait()
        for copy in away:
            copy.wait_recv()

    units = []
    for m, part, parts, shared in REDUCE_UNITS:
        width = shapes[m][1] // n_c // parts
        units.append((m, part * width, width, shared))
    state = [{} for _ in units]

    def piece(unit, of_y):
        m, first, width, shared = unit
        if shared:
            step = width // n_y
            return pl.ds(pl.multiple_of(first + of_y * step, 128), step), step
        return pl.ds(first, width), width

    def product(u):
        m, first, width, shared = units[u]
        rows = sums[m].shape[2]
        left, right, total = left_bufs[slot_of[m]], right_bufs[slot_of[m]], sums[m]
        group = max(1, 512 // (n_b * rows))
        tile = group * n_b * rows

        @pl.loop(0, n_a // group)
        def _(i):
            at = pl.ds(pl.multiple_of(i * tile, 128), tile)
            value = lax.dot_general(
                left[:, at], right[:, pl.ds(first, width)], (((0,), (0,)), ((), ())),
                preferred_element_type=F32,
            ).astype(BF16)
            total[pl.ds(i * group, group), :, :, pl.ds(first, width)] = value.reshape(
                group, n_b, rows, width
            )

    def chunks(outer, rows, body):
        chunk = min(64, rows)
        per = rows // chunk

        @pl.loop(0, outer * per)
        def _(i):
            body(i // per, pl.ds(pl.multiple_of(lax.rem(i, per) * chunk, 16), chunk))

    def y_send(u):
        m, first, width, shared = units[u]
        for k in range(1, n_y):
            cols, step = piece(units[u], turn(y, k, n_y))
            there = landing[3 * u].at[k - 1]
            state[u].setdefault("y", []).append(
                remote(sums[m].at[:, :, :, cols], there, there, (turn(y, k, n_y) * n_c + c, fsdp))
            )

    def y_add(u):
        m = units[u][0]
        for copy in state[u]["y"]:
            copy.wait_recv()
        cols, step = piece(units[u], y)

        def body(outer, rows):
            at = (outer // n_b, lax.rem(outer, n_b), rows, cols)
            value = sums[m][at].astype(F32)
            for k in range(1, n_y):
                value += landing[3 * u][k - 1, outer // n_b, lax.rem(outer, n_b), rows, :].astype(F32)
            sums[m][at] = value.astype(BF16)

        chunks(n_a * n_b, sums[m].shape[2], body)

    def x_land(u):
        return landing[3 * u + 1] if units[u][3] else landing[3 * u]

    def z_land(u):
        return landing[3 * u + 2] if units[u][3] else landing[3 * u + 1]

    def x_send(u):
        m = units[u][0]
        cols, step = piece(units[u], y)
        state[u]["x"] = []
        for k in range(1, n_b):
            there = x_land(u).at[k - 1]
            to = turn(b, k, n_b)
            state[u]["x"].append(
                remote(sums[m].at[:, to, :, cols], there, there, (dp, a * n_b + to))
            )

    def x_add(u):
        m = units[u][0]
        for copy in state[u]["x"]:
            copy.wait_recv()
        cols, step = piece(units[u], y)

        def body(outer, rows):
            value = sums[m][outer, b, rows, cols].astype(F32)
            for k in range(1, n_b):
                value += x_land(u)[k - 1, outer, rows, :].astype(F32)
            sums[m][outer, b, rows, cols] = value.astype(BF16)

        chunks(n_a, sums[m].shape[2], body)

    def z_send(u):
        m = units[u][0]
        cols, step = piece(units[u], y)
        state[u]["z"] = []
        for k in range(1, n_a):
            there = z_land(u).at[k - 1]
            to = turn(a, k, n_a)
            state[u]["z"].append(
                remote(sums[m].at[to, b, :, cols], there, there, (dp, to * n_b + b))
            )

    def z_add(u):
        m, first, width, shared = units[u]
        for copy in state[u]["z"]:
            copy.wait_recv()
        cols, step = piece(units[u], y)
        half = shapes[m][1] // n_c

        def body(outer, rows):
            value = sums[m][a, b, rows, cols].astype(F32)
            for k in range(1, n_a):
                value += z_land(u)[k - 1, rows, :].astype(F32)
            if shared:
                at = pl.ds(pl.multiple_of(c * half + first + y * step, 128), step)
                finals[m][rows, at] = value.astype(BF16)
            else:
                landing[3 * u + 2][y, rows, :] = value.astype(BF16)

        chunks(1, sums[m].shape[2], body)

    def last_send(u):
        m, first, width, shared = units[u]
        half = shapes[m][1] // n_c
        state[u]["last"] = []
        for k in range(1, n_y):
            device = (turn(y, k, n_y) * n_c + c, fsdp)
            from_y = turn(y, -k, n_y)
            if shared:
                step = width // n_y
                mine = pl.ds(pl.multiple_of(c * half + first + y * step, 128), step)
                theirs = pl.ds(pl.multiple_of(c * half + first + from_y * step, 128), step)
                view = finals[m].at[:, mine]
                state[u]["last"].append(remote(view, view, finals[m].at[:, theirs], device))
            else:
                view = landing[3 * u + 2].at[y]
                state[u]["last"].append(remote(view, view, landing[3 * u + 2].at[from_y], device))

    def last_add(u):
        m, first, width, shared = units[u]
        half = shapes[m][1] // n_c
        for copy in state[u]["last"]:
            copy.wait_recv()
        at = pl.ds(pl.multiple_of(c * half + first, 128), width)
        if not shared:

            def body(outer, rows):
                value = landing[3 * u + 2][0, rows, :].astype(F32)
                for k in range(1, n_y):
                    value += landing[3 * u + 2][k, rows, :].astype(F32)
                finals[m][rows, at] = value.astype(BF16)

            chunks(1, sums[m].shape[2], body)
        view = finals[m].at[:, at]
        theirs = pl.ds(pl.multiple_of((1 - c) * half + first, 128), width)
        state[u]["core"] = remote(view, view, finals[m].at[:, theirs], other_core)

    def give_credit(index):
        pl.semaphore_signal(credit.at[index], inc=1, device_id=other_core, device_id_type=MESH)

    for m in (4, 3, 2):
        send_acts(m)
    wait_acts(4)
    for u in (0, 1):
        product(u)
        x_send(u)
    give_credit(0)
    wait_acts(3)
    for u in (2, 3):
        product(u)
        y_send(u)
    give_credit(1)
    frames = []
    for k in range(1, n_dp):
        to, back = turn(dp, k, n_dp), turn(dp, -k, n_dp)
        frames.append(
            remote(returning.at[:, to], returned.at[:, dp], returned.at[:, back], (to, fsdp))
        )
    own_frames = local(returning.at[:, dp], returned.at[:, dp])
    wait_acts(2)
    product(4)
    x_send(4)
    pl.semaphore_wait(credit.at[1], 1)
    send_acts(1)
    pl.semaphore_wait(credit.at[0], 1)
    send_acts(0)
    wait_acts(1)
    for u in (5, 6):
        product(u)
        x_send(u)
    x_add(0)
    z_send(0)
    wait_acts(0)
    for u in (7, 8):
        product(u)
        x_send(u)

    def xz(u):
        x_add(u)
        z_send(u)

    def yx(u):
        y_add(u)
        x_send(u)

    def zl(u):
        z_add(u)
        last_send(u)

    for do, u in (
        (yx, 2), (xz, 1), (yx, 3), (zl, 0), (xz, 4), (zl, 1), (xz, 5), (zl, 4), (xz, 6), (zl, 5),
        (xz, 7), (zl, 6), (xz, 8), (zl, 7), (xz, 2), (zl, 8), (xz, 3), (zl, 2), (last_add, 0),
        (last_add, 1), (last_add, 4), (last_add, 5), (last_add, 6), (last_add, 7), (last_add, 8),
        (zl, 3), (last_add, 2), (last_add, 3),
    ):
        do(u)
    for u in range(len(units)):
        state[u]["core"].wait_recv()
    final_copies = [local(finals[m], outs[m]) for m in range(count)]
    for copy in frames:
        copy.wait_recv()
    own_frames.wait()
    for copy in sent:
        copy.wait_send()
    for copy in final_copies:
        copy.wait()


def reduce_all(lefts, rights, returning):
    dims = sizes()
    n_y, n_c, n_a, n_b = dims
    n_fsdp = n_a * n_b
    tokens = lefts[0].shape[0]
    shapes = [(left.shape[1], right.shape[1]) for left, right in zip(lefts, rights)]
    anywhere = pl.BlockSpec(memory_space=pl.ANY)
    scratch = [pltpu.VMEM((n_a, n_b, r // n_fsdp, w // n_c), BF16) for r, w in shapes]
    scratch += [pltpu.VMEM((r // n_fsdp, w), BF16) for r, w in shapes]
    scratch += [
        pltpu.VMEM((2 * tokens, max(shapes[m][0] for m in group)), BF16)
        for group in ((4, 0), (3, 1), (2,))
    ]
    scratch += [
        pltpu.VMEM((2 * tokens, max(shapes[m][1] // n_c for m in group)), BF16)
        for group in ((4, 0), (3, 1), (2,))
    ]
    for m, part, parts, shared in REDUCE_UNITS:
        rows, width = shapes[m][0] // n_fsdp, shapes[m][1] // n_c // parts
        if shared:
            step = width // n_y
            scratch += [
                pltpu.VMEM((n_y - 1, n_a, n_b, rows, step), BF16),
                pltpu.VMEM((n_b - 1, n_a, rows, step), BF16),
                pltpu.VMEM((n_a - 1, rows, step), BF16),
            ]
        else:
            scratch += [
                pltpu.VMEM((n_b - 1, n_a, rows, width), BF16),
                pltpu.VMEM((n_a - 1, rows, width), BF16),
                pltpu.VMEM((n_y, rows, width), BF16),
            ]
    total = 10 + n_y * n_c - 1
    for _, _, _, shared in REDUCE_UNITS:
        total += (n_b - 1) + (n_a - 1) + (n_y - 1) + 1 + (n_y - 1 if shared else 0)
    scratch += [
        pltpu.SemaphoreType.DMA((total,)),
        pltpu.SemaphoreType.DMA((total,)),
        pltpu.SemaphoreType.DMA((16,)),
        pltpu.SemaphoreType.REGULAR((2,)),
    ]
    out_shape = [jax.ShapeDtypeStruct((r // n_fsdp, w), BF16) for r, w in shapes]
    out_shape.append(jax.ShapeDtypeStruct(returning.shape, returning.dtype))
    results = pl.pallas_call(
        partial(reduce_kernel, dims, shapes),
        out_shape=out_shape,
        in_specs=[anywhere] * 11,
        out_specs=[anywhere] * 6,
        scratch_shapes=scratch,
        compiler_params=pltpu.CompilerParams(
            has_side_effects=True, vmem_limit_bytes=60 * 2**20
        ),
        name="reduce_gradients",
    )(*lefts, *rights, returning)
    return results[:5], results[5]


def sum_over(value, axis, count):
    mask = 1
    while mask < count:
        value = value + swap(value, axis, mask)
        mask *= 2
    return value


def dot_rows(left, right):
    return jnp.dot(left, right, preferred_element_type=F32)


def dot_right(left, right):
    return lax.dot_general(left, right, (((1,), (1,)), ((), ())), preferred_element_type=F32)


def norm_parts(hidden):
    centre = hidden - jnp.mean(hidden, axis=-1, keepdims=True)
    spread = jnp.mean(centre * centre, axis=-1, keepdims=True)
    scale = lax.rsqrt(spread + NORM_EPSILON)
    return centre * scale, scale


def norm_back(normal, scale, gain_row, gradient):
    scaled = gradient * gain_row
    grad_gain = jnp.sum(gradient * normal, axis=0)
    back = scale * (
        scaled
        - jnp.mean(scaled, axis=-1, keepdims=True)
        - normal * jnp.mean(scaled * normal, axis=-1, keepdims=True)
    )
    return back, grad_gain


def alibi_bias(length):
    position = jnp.arange(length, dtype=F32)
    distance = jnp.abs(position[:, None] - position[None, :])
    slopes = jnp.exp2(-8.0 * (jnp.arange(HEADS, dtype=F32) + 1.0) / HEADS)
    return -slopes[:, None, None] * distance[None]


def attention_scores(queries, keys_all, alibi_terms, same_item):
    scores = (
        jnp.einsum("nqhe,nkhe->nhqk", queries, keys_all, preferred_element_type=F32) * HD ** (-0.5)
        + alibi_terms[None]
    )
    return jnp.where(same_item[:, None], scores, -1e30)


def adam_update(master, first, second, gradient, rate, decay):
    first_new = BETA_FIRST * first + (1.0 - BETA_FIRST) * gradient
    second_new = BETA_SECOND * second + (1.0 - BETA_SECOND) * gradient * gradient
    first_hat = first_new / (1.0 - BETA_FIRST**STEP)
    second_hat = second_new / (1.0 - BETA_SECOND**STEP)
    master_new = master - rate * (
        first_hat / (jnp.sqrt(second_hat) + ADAM_EPSILON) + decay * master
    )
    return (master_new, first_new, second_new)


def one_hot(indices, filled, size):
    hit = indices[..., None] == jnp.arange(size, dtype=jnp.int32)
    return (hit & filled[..., None]).astype(BF16)


def frame_plans(lengths, packs, offsets, counts, source_rows, row_count, capacity):
    n_dp = lax.axis_size("dp")
    own = lax.axis_index("dp")
    slot = jnp.arange(capacity, dtype=jnp.int32)
    ids = jnp.arange(n_dp, dtype=jnp.int32)
    own_lengths, own_packs = pick(lengths, own, 1), pick(packs, own, 1)
    starts = jnp.cumsum(own_lengths, axis=1) - own_lengths
    matches = own_packs[:, None, :] == ids[None, :, None]
    length_to = jnp.sum(jnp.where(matches, own_lengths[:, None, :], 0), axis=2)
    start_to = jnp.sum(jnp.where(matches, starts[:, None, :], 0), axis=2)
    filled = slot < length_to[..., None]
    send = one_hot(start_to[..., None] + slot, filled, source_rows)
    here = packs == own

    def chosen(values):
        return jnp.sum(jnp.where(here, values, 0), axis=2)

    length_from, offset_from, count_from = chosen(lengths), chosen(offsets), chosen(counts)
    filled = slot < length_from[..., None]
    back = one_hot(offset_from[..., None] + slot, filled, row_count)
    position = jnp.arange(row_count, dtype=jnp.int32)
    inside = (position[None, :, None] >= offset_from[:, None, :]) & (
        position[None, :, None] < (offset_from + length_from)[:, None, :]
    )

    def select(values):
        return jnp.sum(jnp.where(inside, values[:, None, :], 0), axis=2)

    source = select(jnp.broadcast_to(ids, offset_from.shape))
    weight = select(count_from).astype(F32) / select(length_from).astype(F32)
    return send, back, source, weight


def on_device(
    x_source, skip_source, out_cotangent, item_length, item_pack, item_offset, item_count,
    gains, w_skip, w_qkv, w_out, w_up, w_down,
    gains_first, first_skip, first_qkv, first_out, first_up, first_down,
    gains_second, second_skip, second_qkv, second_out, second_up, second_down,
):
    n_y, n_c, n_a, n_b = sizes()
    n_dp, n_fsdp = n_y * n_c, n_a * n_b
    y, c, a, b = place()
    dp, fsdp = lax.axis_index("dp"), lax.axis_index("fsdp")
    micro, source_rows, width = x_source.shape
    row_count = out_cotangent.shape[1]
    capacity = source_rows // n_dp
    rows = micro * row_count

    send, back, source, weight = frame_plans(
        item_length[0], item_pack[0], item_offset[0], item_count[0], source_rows, row_count, capacity
    )

    def to_packs(values):
        return jnp.einsum("bpsr,brw->bpsw", send, values, preferred_element_type=F32).astype(BF16)

    payload = jnp.concatenate([to_packs(x_source), to_packs(skip_source)], axis=-1)
    own_gains = gains.shape[1]
    low_gains = jnp.zeros((8, 128), F32).at[:2, :own_gains].set(gains.astype(BF16).astype(F32))
    results = forward_all(
        (w_skip, w_qkv, w_out, w_up, w_down), payload, low_gains,
        jnp.moveaxis(back.reshape(micro, n_dp * capacity, row_count), 1, 2), source,
    )
    fulls, results = results[:5], results[5:]
    used_skip, used_qkv, used_out, used_up, used_down = (
        full.reshape(-1, full.shape[-1]) for full in fulls
    )
    packed, base_rows, qkv_rows, mixed, after_attn, up_rows, activated = results[:7]
    normed_one, normed_two, out_frames, gains_all = results[7:]
    used_gains = jnp.moveaxis(gains_all[:, :2, :own_gains], 0, 1).reshape(2, width)
    normal_one, scale_one = norm_parts(base_rows)
    normal_two, scale_two = norm_parts(after_attn)
    heads_shape = (micro, row_count, HEADS, HD)
    queries = qkv_rows[:, :width].reshape(heads_shape)
    keys_all = qkv_rows[:, width : 2 * width].reshape(heads_shape)
    values_all = qkv_rows[:, 2 * width :].reshape(heads_shape)
    alibi_terms = alibi_bias(row_count)
    same_item = source[:, :, None] == source[:, None, :]
    gelu_back = jax.vjp(partial(jax.nn.gelu, approximate=True), up_rows)[1]

    d_out = weight.reshape(rows, 1) * out_cotangent.reshape(rows, width).astype(F32)
    d_out_low = d_out.astype(BF16)
    d_up = gelu_back(dot_right(d_out_low, used_down))[0].astype(BF16)
    d_after_norm, grad_gain_two = norm_back(
        normal_two, scale_two, used_gains[1], dot_right(d_up, used_up)
    )
    d_after = d_out + d_after_norm
    d_after_low = d_after.astype(BF16)
    d_mixed = dot_right(d_after_low, used_out).astype(BF16).reshape(heads_shape)
    scores = attention_scores(queries, keys_all, alibi_terms, same_item)
    probs = jax.nn.softmax(scores, axis=-1)
    probs_low = probs.astype(BF16)
    d_probs = jnp.einsum("nqhe,nkhe->nhqk", d_mixed, values_all, preferred_element_type=F32)
    d_values = jnp.einsum("nhqk,nqhe->nkhe", probs_low, d_mixed, preferred_element_type=F32)
    d_scores = (probs * (d_probs - jnp.sum(probs * d_probs, axis=-1, keepdims=True))).astype(BF16)
    d_queries = jnp.einsum("nhqk,nkhe->nqhe", d_scores, keys_all, preferred_element_type=F32)
    d_keys = jnp.einsum("nhqk,nqhe->nkhe", d_scores, queries, preferred_element_type=F32)
    d_qkv = jnp.concatenate(
        [
            (d_queries * HD ** (-0.5)).reshape(rows, width),
            (d_keys * HD ** (-0.5)).reshape(rows, width),
            d_values.reshape(rows, width),
        ],
        axis=1,
    ).astype(BF16)
    d_base_norm, grad_gain_one = norm_back(
        normal_one, scale_one, used_gains[0], dot_right(d_qkv, used_qkv)
    )
    d_base_low = (d_after + d_base_norm).astype(BF16)
    d_packed = dot_right(d_base_low, used_skip).astype(BF16).reshape(micro, row_count, 2 * width)
    returning = jnp.einsum("bpst,btw->bpsw", back, d_packed, preferred_element_type=F32).astype(BF16)
    (grad_skip, grad_qkv, grad_out, grad_up, grad_down), returned = reduce_all(
        (packed, normed_one, mixed, normed_two, activated),
        (d_base_low, d_qkv, d_after_low, d_up, d_out_low),
        returning,
    )
    in_gradient = jnp.einsum("bpsr,bpsw->brw", send, returned, preferred_element_type=F32)
    in_gradient = in_gradient.astype(BF16)
    input_gradient, skip_gradient = in_gradient[..., :width], in_gradient[..., width:]

    grad_gains = lax.psum(jnp.stack([grad_gain_one, grad_gain_two]), ("dp", "fsdp"))
    grad_gains = pick(grad_gains.reshape(2, n_fsdp, own_gains), fsdp, 1)

    gradients = [g.astype(F32) for g in (grad_skip, grad_qkv, grad_out, grad_up, grad_down)]
    gradients.append(grad_gains)
    squares = jnp.float32(0.0)
    for gradient in gradients:
        squares = squares + jnp.sum(gradient * gradient)
    squares = sum_over(sum_over(jnp.full((8, 128), squares), "b", n_b), "a", n_a)
    gradient_norm = jnp.sqrt(squares[0, 0])
    param_count = 6 * D * D + 2 * D * FF + 2 * D
    clip = jnp.minimum(1.0, 0.02 * math.sqrt(param_count) / gradient_norm)
    grad_skip, grad_qkv, grad_out, grad_up, grad_down, grad_gains = [clip * g for g in gradients]
    results = [out_frames.reshape(micro, row_count, width), input_gradient, skip_gradient]
    results.append(gradient_norm.reshape(1))
    results.extend(adam_update(gains, gains_first, gains_second, grad_gains, 0.3, 0.0))
    for master, first, second, gradient, fan_in in (
        (w_skip, first_skip, second_skip, grad_skip, 2 * D),
        (w_qkv, first_qkv, second_qkv, grad_qkv, D),
        (w_out, first_out, second_out, grad_out, D // 16),
        (w_up, first_up, second_up, grad_up, D),
        (w_down, first_down, second_down, grad_down, FF),
    ):
        new = adam_update(master, first, second, gradient, 0.5 / math.sqrt(fan_in), WEIGHT_DECAY)
        results.extend(new)
        results.append(new[0].astype(BF16))
    return tuple(results)


def solution(mesh):
    frames = P(None, ("dp", "fsdp"), None)
    plan = P("fsdp", None, None, None)
    gain, weight = P(None, "fsdp"), P("fsdp", None)
    return jax.shard_map(
        on_device,
        mesh=mesh,
        in_specs=(frames,) * 3 + (plan,) * 4 + ((gain,) + (weight,) * 5) * 3,
        out_specs=(frames,) * 3 + (P(),) + (gain,) * 3 + (weight,) * 20,
        check_vma=False,
    )
```

time: 806 us -> 595 us (0.74)
  Pallas kernels: 194 us -> 358 us
  waiting for transfers between devices: 135 us -> 1.95 us
  local copies, waits for them, and re-layouts: 170 us -> 64.9 us
  matrix products: 141 us -> 64.2 us
  starting transfers between devices: 55.8 us -> 4.52 us
  other arithmetic: 58.9 us -> 48.5 us
    pallas_call x1 -> x2, Pallas kernels: 194 us -> 358 us  [the longest x1 190 us: reduce_all(): pl.pallas_call(partial(reduce_kernel, dims, shapes), out_shape=out_shape,...]
    ppermute x42 -> x0, waiting for transfers between devices: 134 us -> none  [the longest x39 134 us: move(): return lax.ppermute(value, ('dp', 'fsdp'), pairs)]
    dot_general x13 -> x0, matrix products: 91.3 us -> none  [the longest x5 51.5 us: dot_rows(): return jnp.dot(left, right, preferred_element_type=F32)]
    ppermute x42 -> x0, starting transfers between devices: 48.8 us -> none  [the longest x39 47.2 us: move(): return lax.ppermute(value, ('dp', 'fsdp'), pairs)]
    dynamic_slice x8 -> x1, local copies, waits for them, and re-layouts: 45.3 us -> 0.72 us  [pick(): return lax.dynamic_index_in_dim(value, index, axis, keepdims=False)]
    unnamed x217 -> x115, local copies, waits for them, and re-layouts: 39.2 us -> 12.1 us
    convert_element_type x21 -> x1, other arithmetic: 19.7 us -> 0.99 us  [one_hot(): return (hit & filled[..., None]).astype(BF16)]
    another operation x2 -> x0, local copies, waits for them, and re-layouts: 15.5 us -> none  [weight_gradient(): pieces = blocks.reshape(n_a, n_b, rows, n_y, step)]
  transfers between devices with their start and end apart: 48 -> 3, of which waited for: 10 -> 2; matrix products, arithmetic and copies ran while one was open for 40% -> 1% of each run, Pallas kernels for 0% -> 0%
where the time goes in v2:
time: 595 us; the launch traced here: 590 us
  Pallas kernels  358 us (60%)
  local copies, waits for them, and re-layouts  64.9 us (11%)
  matrix products  64.2 us (11%)
  other arithmetic  48.5 us (8%)
  blocking collectives  40.4 us (7%)
  between operations  7.33 us (1%)
    pallas_call x1, Pallas kernels, reduce_all(): pl.pallas_call(partial(reduce_kernel, dims, shapes), out_shape=out_shape,...  190 us
    pallas_call x1, Pallas kernels, forward_all(): pl.pallas_call(partial(forward_kernel, dims), out_shape=out_shape, in_spe...  168 us
    psum x1, blocking collectives, on_device(): lax.psum(jnp.stack([grad_gain_one, grad_gain_two]), ('dp', 'fsdp'))  40.4 us
    dot_general x5, matrix products, dot_right(): lax.dot_general(left, right, (((1,), (1,)), ((), ())), preferred_element_...  31.5 us
    convert_element_type x5, other arithmetic, on_device(): results.append(new[0].astype(BF16))  16.4 us
    unnamed x115, local copies, waits for them, and re-layouts  12.1 us
  transfers between devices with their start and end apart: 3, of which 2 were waited for; matrix products, arithmetic and copies ran while one was open for 1% of the time, Pallas kernels for 0%

profile of v2, /device:TPU:0, one launch (start us, length us, event | category | flops | bytes accessed | tf_op | source)
XLA Modules:
  0.0 589.9 jit_solution(15687811737735921005)
XLA Ops:
  5.0 3.0 fusion.35
  12.2 4.0 pad_maximum_fusion.refs_5_
  17.9 167.8 %gather_and_forward.1 = (bf16[4,2,256,1024]{3,2,1,0:T(8,128)(2,1)}, bf16[4,2,128,3072]{3,2,1,0:T(8,128)(2,1)}, bf16[4,2,128,1024]{3,2,1,0:T(8,128)(2,1)}, bf16[4...) custom-call(f32[256,1024]{1,0:T(8,128)} %refs_0_.1, ...), custom_call_target="tpu_custom_call" | custom-call | tf_op jit(solution)/shard_map/gather_and_forward/pallas_call | solution.py:493
  189.3 13.0 %fusion.7.refs_8_ = bf16[512,4096]{1,0:T(8,128)(2,1)S(1)} fusion(f32[512,4096]{1,0:T(8,128)} %get-tuple-element.69, bf16[512,1024]{1,0:T(8,128)(2,1)S(1)} %bitcast.103, bf16[4096,1024]{1,0:T(8,128)(2,1)} %bitcast.121), kind=kOutput, calls=%fused_computation.9 | convolution fusion | flops 4336910336 | bytes 22020096 | tf_op jit(solution)/shard_map/dot_general | solution.py:942
  202.4 6.7 %multiply_reduce_fusion.1 = (f32[1024]{0:T(1024)}, f32[512]{0:T(512)S(1)}, f32[512]{0:T(512)S(1)}, f32[512,1024]{1,0:T(8,128)}) fusion(f32[512,1024]{1,0:T(8,128)S(1)} %copy-done.1, f32[512]{0:T(512)S(1)} %add_rsqrt_fusion.1, f32[512]{0:T(512)S(1)} %broadcast_multiply_fusion.6, f32[1024]{0:T(1024)S(1)} %bitcast.109, ...), kind=kOutput, calls=%fused_computation.49 | convolution fusion | flops 4299159552 | bytes 16793600 | tf_op jit(solution)/shard_map/dot_general | solution.py:942
  217.6 4.0 reshape.327
  221.6 3.5 copy.118
  225.1 3.9 fusion.84
  232.2 2.9 reshape.328
  237.7 4.2 reshape.322
  244.3 7.2 %fusion.88 = (f32[2,16,256]{2,1,0:T(8,128)S(1)}, f32[2,16,256,256]{2,3,1,0:T(8,128)}) fusion(f32[16,256,256]{1,2,0:T(8,128)} %broadcast_multiply_fusion, pred[2,256,256]{1,2,0:T(8,128)(4,1)S(1)} %broadcast_compare_fusion, bf16[2,256,16,64]{1,3,2,0:T(8,128)(2,1)S(1)} %copy-done.9, bf16[2,256,16,64]{1,3,2,0:T(8,128)(2,1)S(1)} %copy.124), kind=kOutput, calls=%fused_computation.169 | convolution fusion | flops 278921472 | bytes 14843904 | tf_op jit(solution)/shard_map/sub | solution.py:1083
  251.5 5.6 multiply_reduce_fusion
  270.5 3.2 reshape.323
  274.8 3.8 copy.148
  278.6 3.2 reshape.324
  281.9 4.0 copy.149
  285.9 4.1 reshape.325
  292.7 7.2 %multiply_reduce_fusion.2 = (f32[1024]{0:T(1024)S(1)}, f32[512]{0:T(512)S(1)}, f32[512]{0:T(512)S(1)}, f32[512,1024]{1,0:T(8,128)S(1)}) fusion(f32[512,1024]{1,0:T(8,128)S(1)} %copy-done, f32[512]{0:T(512)S(1)} %add_rsqrt_fusion, f32[512]{0:T(512)S(1)} %broadcast_multiply_fusion.3, f32[1024]{0:T(1024)S(1)} %bitcast.107, ...), kind=kOutput, calls=%fused_computation.50 | convolution fusion | flops 3225417728 | bytes 13647872 | tf_op jit(solution)/shard_map/dot_general | solution.py:942
  307.7 190.4 %reduce_gradients.1 = (bf16[256,1024]{1,0:T(8,128)(2,1)}, bf16[128,3072]{1,0:T(8,128)(2,1)}, bf16[128,1024]{1,0:T(8,128)(2,1)}, bf16[128,4096]{1,0:T(8,128)(2,1)...) custom-call(bf16[512,2048]{1,0:T(8,128)(2,1)} %get-tuple-element.62.refs_0_, ...), custom_call_target="tpu_custom_call" | custom-call | tf_op jit(solution)/shard_map/reduce_gradients/pallas_call | solution.py:915
  507.5 40.4 %psum.7 = f32[2,8,128]{2,0,1:T(2,128)S(1)} all-reduce(f32[2,8,128]{2,0,1:T(2,128)S(1)} %maximum_bitcast_fusion), channel_id=1, replica_groups=mesh['dp'=4,'fsdp'=8] {'dp','fsdp'}, use_global_device_ids=true, to_apply=%region_27.28 | all-reduce | flops 2048 | bytes 16384 | tf_op jit(solution)/shard_map/psum | solution.py:1113
  556.8 4.7 bitcast_convert_fusion
  572.0 3.6 fusion.79
  578.4 4.4 fusion.75
  583.3 4.4 fusion.73
  (195 shorter events, 83.4 us)
Async XLA Ops:
  188.2 14.1 %copy-start.37 = (f32[512]{0:T(512)}, f32[512]{0:T(512)S(1)}, u32[]{:S(2)}) copy-start(f32[512]{0:T(512)S(1)} %add_rsqrt_fusion.1) | copy-start | bytes 6148
  189.0 13.3 %copy-start.34 = (f32[1,8,128]{2,0,1:T(1,128)}, f32[1,8,128]{2,0,1:T(1,128)S(1)}, u32[]{:S(2)}) copy-start(f32[1,8,128]{2,0,1:T(1,128)S(1)} %get-tuple-element.129) | copy-start | bytes 12292
  189.1 13.3 %slice-start.2 = ((s8[8388608]{0:T(1024)(128)(4,1)}), s8[4194304]{0:T(1024)(128)(4,1)S(1)}, s32[]{:S(2)}) async-start(s8[8388608]{0:T(1024)(128)(4,1)} %bitcast.118), calls=%async_computation.2 | async-start | bytes 8388608
  189.3 13.0 %slice-start.3 = ((s8[8388608]{0:T(1024)(128)(4,1)}), s8[4194304]{0:T(1024)(128)(4,1)S(1)}, s32[]{:S(2)}) async-start(s8[8388608]{0:T(1024)(128)(4,1)} %bitcast.118), calls=%async_computation.3 | async-start | bytes 8388608
  202.3 6.8 %copy-start.12 = (bf16[512,4096]{1,0:T(8,128)(2,1)}, bf16[512,4096]{1,0:T(8,128)(2,1)S(1)}, u32[]{:S(2)}) copy-start(bf16[512,4096]{1,0:T(8,128)(2,1)S(1)} %fusion.7.refs_8_) | copy-start | bytes 12582916
  202.4 8.5 %copy-start.16 = (bf16[512,3072]{1,0:T(8,128)(2,1)S(1)}, bf16[512,3072]{1,0:T(8,128)(2,1)}, u32[]{:S(2)}) copy-start(bf16[512,3072]{1,0:T(8,128)(2,1)} %get-tuple-element.73) | copy-start | bytes 9437188
  244.3 7.2 %copy-start.26 = (bf16[2,256,16,64]{1,3,2,0:T(8,128)(2,1)S(1)}, bf16[2,256,16,64]{1,3,2,0:T(8,128)(2,1)}, u32[]{:S(2)}) copy-start(bf16[2,256,16,64]{1,3,2,0:T(8,128)(2,1)} %copy.122) | copy-start | bytes 3145732
  251.5 5.6 slice-start
  251.5 6.5 %slice-start.1 = ((s8[8388608]{0:T(1024)(128)(4,1)}), s8[4194304]{0:T(1024)(128)(4,1)S(1)}, s32[]{:S(2)}) async-start(s8[8388608]{0:T(1024)(128)(4,1)} %bitcast.100), calls=%async_computation.1 | async-start | bytes 8388608
  292.7 7.2 %copy-start.4 = (f32[512,1024]{1,0:T(8,128)S(1)}, f32[512,1024]{1,0:T(8,128)}, u32[]{:S(2)}) copy-start(f32[512,1024]{1,0:T(8,128)} %get-tuple-element.121) | copy-start | bytes 6291460
  498.1 8.2 %copy-start.6 = (bf16[512,1024]{1,0:T(8,128)(2,1)S(1)}, bf16[512,1024]{1,0:T(8,128)(2,1)}, u32[]{:S(2)}) copy-start(bf16[512,1024]{1,0:T(8,128)(2,1)} %get-tuple-element.82) | copy-start | bytes 3145732
  498.1 9.4 %copy-start.40 = (f32[1024]{0:T(1024)S(1)}, f32[1024]{0:T(1024)}, u32[]{:S(2)}) copy-start(f32[1024]{0:T(1024)} %get-tuple-element.85) | copy-start | bytes 12292
  498.1 58.6 %copy-start.39 = (s32[2,4,128]{2,1,0:T(4,128)S(1)}, s32[2,4,128]{2,1,0:T(4,128)}, u32[]{:S(2)}) copy-start(s32[2,4,128]{2,1,0:T(4,128)} %copy-done.38) | copy-start | bytes 12292
  498.1 58.6 %copy-start.42 = (pred[2,4,128]{2,1,0:T(4,128)(4,1)S(1)}, pred[2,4,128]{2,1,0:T(4,128)(4,1)}, u32[]{:S(2)}) copy-start(pred[2,4,128]{2,1,0:T(4,128)(4,1)} %copy-done.41) | copy-start | bytes 3076
  552.4 3.9 collective-permute-start
  556.3 5.2 collective-permute-start.1
  561.5 5.9 %copy-start.44 = (f32[2,128]{1,0:T(2,128)S(1)}, f32[2,128]{1,0:T(2,128)}, u32[]{:S(2)}) copy-start(f32[2,128]{1,0:T(2,128)} %param.34) | copy-start | bytes 3076
  561.5 5.9 %copy-start.45 = (f32[2,128]{1,0:T(2,128)S(1)}, f32[2,128]{1,0:T(2,128)}, u32[]{:S(2)}) copy-start(f32[2,128]{1,0:T(2,128)} %param.40) | copy-start | bytes 3076
  561.5 5.9 %copy-start.46 = (f32[2,128]{1,0:T(2,128)S(1)}, f32[2,128]{1,0:T(2,128)}, u32[]{:S(2)}) copy-start(f32[2,128]{1,0:T(2,128)} %param.46) | copy-start | bytes 3076
  561.6 6.5 %copy-start.13 = (f32[256,1024]{1,0:T(8,128)S(1)}, f32[256,1024]{1,0:T(8,128)}, u32[]{:S(2)}) copy-start(f32[256,1024]{1,0:T(8,128)} %refs_0_.1) | copy-start | bytes 3145732
  561.6 6.5 %copy-start.23 = (bf16[256,1024]{1,0:T(8,128)(2,1)S(1)}, bf16[256,1024]{1,0:T(8,128)(2,1)}, u32[]{:S(2)}) copy-start(bf16[256,1024]{1,0:T(8,128)(2,1)} %get-tuple-element.78) | copy-start | bytes 1572868
  561.6 6.5 %copy-start.30 = (f32[256,1024]{1,0:T(8,128)S(1)}, f32[256,1024]{1,0:T(8,128)}, u32[]{:S(2)}) copy-start(f32[256,1024]{1,0:T(8,128)} %param.41) | copy-start | bytes 3145732
  561.6 6.5 %copy-start.31 = (f32[256,1024]{1,0:T(8,128)S(1)}, f32[256,1024]{1,0:T(8,128)}, u32[]{:S(2)}) copy-start(f32[256,1024]{1,0:T(8,128)} %param.47) | copy-start | bytes 3145732
  561.6 4.6 collective-permute-start.2
  (34 other events, 107.9 us)

commit v3 on v2

--- a/solution.py
+++ b/solution.py
@@ -53,23 +53,37 @@
     return lax.rem(value + (step + size) % size, size)
 
 
+class Remote:
+    def __init__(self, src, dst, land, device, **sems):
+        self.given = pltpu.make_async_remote_copy(
+            src_ref=src, dst_ref=dst, device_id=device, device_id_type=MESH, **sems
+        )
+        self.given.start()
+        self.taken = (src, land, device, sems)
+        self.left = False
+
+    def wait_recv(self):
+        src, land, device, sems = self.taken
+        pltpu.make_async_remote_copy(
+            src_ref=src, dst_ref=land, device_id=device, device_id_type=MESH, **sems
+        ).wait_recv()
+
+    def wait_send(self):
+        if not self.left:
+            self.given.wait_send()
+        self.left = True
+
+
 class Copies:
     def __init__(self, send_sem, recv_sem, local_sem):
         self.send_sem, self.recv_sem, self.local_sem = send_sem, recv_sem, local_sem
-        self.remotes, self.locals, self.sent = 0, 0, []
+        self.locals, self.sent = 0, []
 
     def remote(self, src, dst, land, device):
-        index = self.remotes
-        self.remotes += 1
+        index = len(self.sent)
         sems = dict(send_sem=self.send_sem.at[index], recv_sem=self.recv_sem.at[index])
-        copy = pltpu.make_async_remote_copy(
-            src_ref=src, dst_ref=dst, device_id=device, device_id_type=MESH, **sems
-        )
-        copy.start()
-        self.sent.append(copy)
-        return pltpu.make_async_remote_copy(
-            src_ref=src, dst_ref=land, device_id=device, device_id_type=MESH, **sems
-        )
+        self.sent.append(Remote(src, dst, land, device, **sems))
+        return self.sent[-1]
 
     def local(self, src, dst):
         index = self.locals
@@ -91,12 +105,16 @@
         body(pl.ds(pl.multiple_of(i * chunk, chunk), chunk))
 
 
-def norm_into(hidden, gain_row, target):
+def norm_into(hidden, gain_row, target, hat, scales, first):
     def body(at):
         centre = hidden[at, :]
         centre = centre - jnp.mean(centre, axis=-1, keepdims=True)
         spread = jnp.mean(centre * centre, axis=-1, keepdims=True)
-        target[at, :] = (centre * lax.rsqrt(spread + NORM_EPSILON) * gain_row).astype(BF16)
+        scale = lax.rsqrt(spread + NORM_EPSILON)
+        normal = centre * scale
+        target[at, :] = (normal * gain_row).astype(BF16)
+        hat[at, :] = normal.astype(BF16)
+        scales[at, pl.ds(first, 64)] = jnp.broadcast_to(scale, (scale.shape[0], 64))
 
     row_loop(hidden.shape[0], 64, body)
 
@@ -104,8 +122,12 @@
 GELU_SCALE = math.sqrt(2.0 / math.pi)
 
 
-def gelu(u):
-    return 0.5 * u * (1.0 + jnp.tanh(GELU_SCALE * (u + 0.044715 * (u * u * u))))
+def gelu_and_slope(u):
+    square = u * u
+    bent = jnp.tanh(GELU_SCALE * (u + 0.044715 * (square * u)))
+    half = 0.5 * (1.0 + bent)
+    slope = half + (0.5 * GELU_SCALE) * u * (1.0 - bent * bent) * (1.0 + 0.134145 * square)
+    return u * half, slope
 
 
 def head_probs(queries, keys_all, distance, same, slope):
@@ -129,12 +151,13 @@
     )
     refs = refs[11:]
     fulls_out, refs = refs[:5], refs[5:]
-    packed_out, base_out, qkv_out, mixed_out, after_out, up_out, act_out = refs[:7]
-    one_out, two_out, frames_out, gains_out = refs[7:11]
-    refs = refs[11:]
+    packed_out, qkv_out, mixed_out, slope_out, act_out, one_out, two_out = refs[:7]
+    hat_one_out, hat_two_out, scales_out, frames_out, gains_out = refs[7:12]
+    refs = refs[12:]
     fulls, refs = refs[:5], refs[5:]
     stage, arrived, hot, gains_all, packed, base, one, qkv, mixed, after, two, up, out = refs[:13]
-    send_sem, recv_sem, local_sem = refs[13:]
+    hat_one, hat_two, scales, slope_buf = refs[13:17]
+    send_sem, recv_sem, local_sem = refs[17:]
     dp, fsdp = lax.axis_index("dp"), lax.axis_index("fsdp")
     y, c, a, b = dp // n_c, lax.rem(dp, n_c), fsdp // n_b, lax.rem(fsdp, n_b)
     n_dp, n_fsdp = n_y * n_c, n_a * n_b
@@ -330,8 +353,8 @@
             base[:, pl.ds(first, 512)] = jnp.dot(
                 packed[...], whole(fulls[0], first, 512), preferred_element_type=F32
             )
-        norm_into(base, gain_rows[0], one)
-        outgoing.append(local(base, base_out))
+        norm_into(base, gain_rows[0], one, hat_one, scales, 0)
+        outgoing.append(local(hat_one, hat_one_out))
         outgoing.append(local(one, one_out))
 
     def make_qkv():
@@ -375,29 +398,29 @@
             after[:, cols] = base[:, cols] + jnp.dot(
                 mixed[...], whole(fulls[2], first, 512), preferred_element_type=F32
             )
-        norm_into(after, gain_rows[1], two)
-        outgoing.append(local(after, after_out))
+        norm_into(after, gain_rows[1], two, hat_two, scales, 64)
+        outgoing.append(local(hat_two, hat_two_out))
+        outgoing.append(local(scales, scales_out))
         outgoing.append(local(two, two_out))
 
-    up_copies = [None, None]
+    slope_copies = [None, None]
     half_ff = FF // 2
 
     def make_up(j):
         slot_now = j % 2
-        if up_copies[slot_now] is not None:
-            up_copies[slot_now].wait()
         cols = pl.ds(j * 512, 512)
-        up[slot_now] = jnp.dot(
-            two[...], whole(fulls[3], j * 512, 512), preferred_element_type=F32
-        )
-        up_copies[slot_now] = local(up.at[slot_now], up_out.at[:, cols])
+        up[...] = jnp.dot(two[...], whole(fulls[3], j * 512, 512), preferred_element_type=F32)
+        if slope_copies[slot_now] is not None:
+            slope_copies[slot_now].wait()
         half, within = j * 512 // half_ff, j * 512 % half_ff
 
         def body(at):
-            act = gelu(up[slot_now, at, :]).astype(BF16)
-            arrived[half, at, pl.ds(within, 512)] = act
+            value, slope = gelu_and_slope(up[at, :])
+            arrived[half, at, pl.ds(within, 512)] = value.astype(BF16)
+            slope_buf[slot_now, at, :] = slope.astype(BF16)
 
         row_loop(tokens, 64, body)
+        slope_copies[slot_now] = local(slope_buf.at[slot_now], slope_out.at[:, cols])
 
     def send_act(half):
         outgoing.append(
@@ -458,7 +481,7 @@
     finish(10)
     make_out(768, 256)
     outgoing.append(local(out, frames_out))
-    for copy in outgoing + [c for c in up_copies if c is not None]:
+    for copy in outgoing + slope_copies:
         copy.wait()
     for copy in copies.sent:
         copy.wait_send()
@@ -480,9 +503,11 @@
     full_shapes = [(n_a, n_b) + master.shape for master in masters]
     out_shape = [shape(s, BF16) for s in full_shapes]
     out_shape += [
-        shape((tokens, 2 * D), BF16), shape((tokens, D), F32), shape((tokens, 3 * D), BF16),
-        shape((tokens, D), BF16), shape((tokens, D), F32), shape((tokens, FF), F32),
-        shape((tokens, FF), BF16), shape((tokens, D), BF16), shape((tokens, D), BF16),
+        shape((tokens, 2 * D), BF16), shape((tokens, 3 * D), BF16), shape((tokens, D), BF16),
+        shape((tokens, FF), BF16), shape((tokens, FF), BF16),
+        shape((tokens, D), BF16), shape((tokens, D), BF16),
+        shape((tokens, D), BF16), shape((tokens, D), BF16),
+        shape((tokens, 128), F32),
         shape((tokens, D), BF16), shape((n_fsdp,) + gains.shape, F32),
     ]
     anywhere = pl.BlockSpec(memory_space=pl.ANY)
@@ -508,8 +533,12 @@
             pltpu.VMEM((tokens, D), BF16),
             pltpu.VMEM((tokens, D), F32),
             pltpu.VMEM((tokens, D), BF16),
-            pltpu.VMEM((2, tokens, 512), F32),
+            pltpu.VMEM((tokens, 512), F32),
             pltpu.VMEM((tokens, D), BF16),
+            pltpu.VMEM((tokens, D), BF16),
+            pltpu.VMEM((tokens, D), BF16),
+            pltpu.VMEM((tokens, 128), F32),
+            pltpu.VMEM((2, tokens, 512), BF16),
             pltpu.SemaphoreType.DMA((total,)),
             pltpu.SemaphoreType.DMA((total,)),
             pltpu.SemaphoreType.DMA((64,)),
@@ -525,118 +554,90 @@
     return results
 
 
-def move(value, axis, shift):
-    n_y, n_c, n_a, n_b = sizes()
-    dims = {"y": n_y, "c": n_c, "a": n_a, "b": n_b}
-    pairs = []
-    for source in range(n_y * n_c * n_a * n_b):
-        at = {
-            "y": source // (n_c * n_a * n_b),
-            "c": source // (n_a * n_b) % n_c,
-            "a": source // n_b % n_a,
-            "b": source % n_b,
-        }
-        at[axis] = (at[axis] + shift) % dims[axis]
-        target = ((at["y"] * n_c + at["c"]) * n_a + at["a"]) * n_b + at["b"]
-        pairs.append((source, target))
-    return lax.ppermute(value, ("dp", "fsdp"), pairs)
-
-
-def swap(value, axis, mask):
-    n_y, n_c, n_a, n_b = sizes()
-    pairs = []
-    for source in range(n_y * n_c * n_a * n_b):
-        at = {
-            "y": source // (n_c * n_a * n_b),
-            "c": source // (n_a * n_b) % n_c,
-            "a": source // n_b % n_a,
-            "b": source % n_b,
-        }
-        at[axis] = at[axis] ^ mask
-        target = ((at["y"] * n_c + at["c"]) * n_a + at["a"]) * n_b + at["b"]
-        pairs.append((source, target))
-    return lax.ppermute(value, ("dp", "fsdp"), pairs)
-
-
-def pick(value, index, axis):
-    return lax.dynamic_index_in_dim(value, index, axis, keepdims=False)
-
-
-def add_all(values):
-    total = values[0].astype(F32)
-    for value in values[1:]:
-        total = total + value.astype(F32)
-    return total.astype(BF16)
-
-
-def reduce_kernel(dims, shapes, *refs):
+def norm_back(hat, scale, gain_row, gradient):
+    scaled = gradient * gain_row
+    back = scale * (
+        scaled
+        - jnp.mean(scaled, axis=-1, keepdims=True)
+        - hat * jnp.mean(scaled * hat, axis=-1, keepdims=True)
+    )
+    return back, jnp.sum(gradient * hat, axis=0, keepdims=True)
+
+
+RING = 4
+
+
+def backward_kernel(dims, shapes, *refs):
     n_y, n_c, n_a, n_b = dims
-    count = 5
-    lefts, rights, returning = refs[:count], refs[count : 2 * count], refs[2 * count]
-    outs = refs[2 * count + 1 : 3 * count + 1]
-    returned = refs[3 * count + 1]
-    scratch = refs[3 * count + 2 :]
-    sums, finals = scratch[:count], scratch[count : 2 * count]
-    left_bufs, right_bufs = scratch[2 * count : 2 * count + 3], scratch[2 * count + 3 : 2 * count + 6]
-    rest = scratch[2 * count + 6 :]
-    landing = rest[: 3 * len(REDUCE_UNITS)]
-    send_sem, recv_sem, local_sem, credit = rest[3 * len(REDUCE_UNITS) :]
+    fulls, refs = refs[:5], refs[5:]
+    (packed, qkv, mixed, slope, act, one, two, hat_one, hat_two, scales,
+     cotangent, frame_weight, gains_all, back_hot, ids_down, ids_across, slopes) = refs[:17]
+    refs = refs[17:]
+    outs, returned, gains_out, squares_out = refs[:5], refs[5], refs[6], refs[7]
+    refs = refs[8:]
+    sums, finals, refs = refs[:5], refs[5:10], refs[10:]
+    (pool, low_far, wide, wide_far, left_far, ring, slope_buf, acc, hidden,
+     cot, low, hat, gain_buf, gain_land, square_buf, square_land) = refs[:16]
+    refs = refs[16:]
+    landing, refs = refs[: 3 * len(REDUCE_UNITS)], refs[3 * len(REDUCE_UNITS) :]
+    send_sem, recv_sem, local_sem, credit = refs
     dp, fsdp = lax.axis_index("dp"), lax.axis_index("fsdp")
     y, c, a, b = dp // n_c, lax.rem(dp, n_c), fsdp // n_b, lax.rem(fsdp, n_b)
-    n_dp = n_y * n_c
-    used = [0, 0]
-    sent = []
+    n_dp, n_fsdp = n_y * n_c, n_a * n_b
     other_core = (y * n_c + 1 - c, fsdp)
-    slot_of = {4: 0, 0: 0, 3: 1, 1: 1, 2: 2}
-
-    def remote(src, dst, land, device):
-        index = used[0]
-        used[0] += 1
-        sems = dict(send_sem=send_sem.at[index], recv_sem=recv_sem.at[index])
-        copy = pltpu.make_async_remote_copy(
-            src_ref=src, dst_ref=dst, device_id=device, device_id_type=MESH, **sems
-        )
-        copy.start()
-        sent.append(copy)
-        return pltpu.make_async_remote_copy(
-            src_ref=src, dst_ref=land, device_id=device, device_id_type=MESH, **sems
-        )
-
-    def local(src, dst):
-        index = used[1]
-        used[1] += 1
-        copy = pltpu.make_async_copy(src, dst, local_sem.at[index])
-        copy.start()
-        return copy
-
-    def turn(value, step, size):
-        return lax.rem(value + (step + size) % size, size)
-
-    tokens = lefts[0].shape[0]
-    acts = {}
-
-    def send_acts(m):
-        depth, width = lefts[m].shape[1], rights[m].shape[1] // n_c
-        left, right = left_bufs[slot_of[m]], right_bufs[slot_of[m]]
-        mine = pl.ds(pl.multiple_of(c * width, 128), width)
-        others = pl.ds(pl.multiple_of((1 - c) * width, 128), width)
-        low, high = pl.ds(0, tokens), pl.ds(tokens, tokens)
-        here = [
-            local(rights[m].at[:, mine], right.at[low, pl.ds(0, width)]),
-            local(lefts[m], left.at[low, pl.ds(0, depth)]),
-        ]
-        there = right.at[high, pl.ds(0, width)]
-        away = [remote(rights[m].at[:, others], there, there, other_core)]
-        there = left.at[high, pl.ds(0, depth)]
-        away.append(remote(lefts[m], there, there, other_core))
-        acts[m] = (here, away)
-
-    def wait_acts(m):
-        here, away = acts[m]
-        for copy in here:
-            copy.wait()
-        for copy in away:
-            copy.wait_recv()
+    copies = Copies(send_sem, recv_sem, local_sem)
+    remote, local = copies.remote, copies.local
+    tokens = cot.shape[0]
+    micro = ids_down.shape[0]
+    per_pack = tokens // micro
+    near, far = pl.ds(0, tokens), pl.ds(tokens, tokens)
+
+    order = []
+    for block in range(4):
+        order += [(4, block * 1024, 0), (4, block * 1024, 512)]
+        order += [(3, 0, block * 1024), (3, 0, block * 1024 + 512)]
+    order += [(2, 0, 0), (2, 0, 512)]
+    order += [(1, 0, first) for first in range(0, 3 * D, 512)]
+    order += [(0, first, second) for first in (0, 1024) for second in (0, 512)]
+    ring_copies = {}
+    ring_state = [0, 0]
+
+    def ring_load():
+        index = ring_state[0]
+        if index < len(order):
+            m, first, second = order[index]
+            ring_copies[index] = local(
+                fulls[m].at[pl.ds(first, 1024), pl.ds(second, 512)], ring.at[index % RING]
+            )
+            ring_state[0] += 1
+
+    def ring_next():
+        index = ring_state[1]
+        ring_state[1] += 1
+        ring_copies.pop(index).wait()
+        return ring.at[index % RING]
+
+    def far_half(width):
+        return pl.ds(pl.multiple_of((1 - c) * width, 128), width)
+
+    cot_copy = local(cotangent, cot)
+    for _ in range(RING):
+        ring_load()
+    half_ff = FF // 2
+    slope_copies = {}
+
+    def slope_load(j):
+        slope_copies[j] = local(slope.at[:, pl.ds(j * 512, 512)], slope_buf.at[j % 2])
+
+    slope_load(0)
+    slope_load(1)
+    act_here, act_away = [], []
+    for half in range(2):
+        view = act.at[:, pl.ds(half * half_ff, half_ff)]
+        act_away.append(remote(view, pool.at[half, far], pool.at[half, far], other_core))
+        act_here.append(local(view, pool.at[half, near]))
+    hat_copy = local(hat_two, hat)
+    two_away = remote(two, left_far, left_far, other_core)
 
     units = []
     for m, part, parts, shared in REDUCE_UNITS:
@@ -651,23 +652,40 @@
             return pl.ds(pl.multiple_of(first + of_y * step, 128), step), step
         return pl.ds(first, width), width
 
-    def product(u):
+    def product(u, left_near, left_other, right_near, right_far):
         m, first, width, shared = units[u]
         rows = sums[m].shape[2]
-        left, right, total = left_bufs[slot_of[m]], right_bufs[slot_of[m]], sums[m]
         group = max(1, 512 // (n_b * rows))
         tile = group * n_b * rows
+        half = shapes[m][1] // n_c
+        mine = pl.ds(pl.multiple_of(c * half + first, 128), width)
 
         @pl.loop(0, n_a // group)
         def _(i):
-            at = pl.ds(pl.multiple_of(i * tile, 128), tile)
+            contract = (((0,), (0,)), ((), ()))
             value = lax.dot_general(
-                left[:, at], right[:, pl.ds(first, width)], (((0,), (0,)), ((), ())),
+                left_near(i, tile), right_near[:, mine], contract, preferred_element_type=F32
+            )
+            value += lax.dot_general(
+                left_other(i, tile), right_far[:, pl.ds(first, width)], contract,
                 preferred_element_type=F32,
-            ).astype(BF16)
-            total[pl.ds(i * group, group), :, :, pl.ds(first, width)] = value.reshape(
+            )
+            sums[m][pl.ds(i * group, group), :, :, pl.ds(first, width)] = value.astype(BF16).reshape(
                 group, n_b, rows, width
             )
+
+    def tiles(ref, rows, first):
+        def pick_tile(i, tile):
+            return ref[rows, pl.ds(pl.multiple_of(first + i * tile, 128), tile)]
+
+        return pick_tile
+
+    def pool_tiles(rows):
+        def pick_tile(i, tile):
+            per = half_ff // tile
+            return pool[i // per, rows, pl.ds(pl.multiple_of(lax.rem(i, per) * tile, 128), tile)]
+
+        return pick_tile
 
     def chunks(outer, rows, body):
         chunk = min(64, rows)
@@ -676,6 +694,7 @@
         @pl.loop(0, outer * per)
         def _(i):
             body(i // per, pl.ds(pl.multiple_of(lax.rem(i, per) * chunk, 16), chunk))
+
 
     def y_send(u):
         m, first, width, shared = units[u]
@@ -757,6 +776,8 @@
             if shared:
                 at = pl.ds(pl.multiple_of(c * half + first + y * step, 128), step)
                 finals[m][rows, at] = value.astype(BF16)
+            elif n_y == 2:
+                sums[m][a, b, rows, cols] = value.astype(BF16)
             else:
                 landing[3 * u + 2][y, rows, :] = value.astype(BF16)
 
@@ -775,6 +796,9 @@
                 theirs = pl.ds(pl.multiple_of(c * half + first + from_y * step, 128), step)
                 view = finals[m].at[:, mine]
                 state[u]["last"].append(remote(view, view, finals[m].at[:, theirs], device))
+            elif n_y == 2:
+                view, there = sums[m].at[a, b, :, piece(units[u], y)[0]], landing[3 * u + 2].at[0]
+                state[u]["last"].append(remote(view, there, there, device))
             else:
                 view = landing[3 * u + 2].at[y]
                 state[u]["last"].append(remote(view, view, landing[3 * u + 2].at[from_y], device))
@@ -789,7 +813,9 @@
 
             def body(outer, rows):
                 value = landing[3 * u + 2][0, rows, :].astype(F32)
-                for k in range(1, n_y):
+                if n_y == 2:
+                    value += sums[m][a, b, rows, pl.ds(first, width)].astype(F32)
+                for k in range(1, n_y if n_y > 2 else 0):
                     value += landing[3 * u + 2][k, rows, :].astype(F32)
                 finals[m][rows, at] = value.astype(BF16)
 
@@ -798,46 +824,6 @@
         theirs = pl.ds(pl.multiple_of((1 - c) * half + first, 128), width)
         state[u]["core"] = remote(view, view, finals[m].at[:, theirs], other_core)
 
-    def give_credit(index):
-        pl.semaphore_signal(credit.at[index], inc=1, device_id=other_core, device_id_type=MESH)
-
-    for m in (4, 3, 2):
-        send_acts(m)
-    wait_acts(4)
-    for u in (0, 1):
-        product(u)
-        x_send(u)
-    give_credit(0)
-    wait_acts(3)
-    for u in (2, 3):
-        product(u)
-        y_send(u)
-    give_credit(1)
-    frames = []
-    for k in range(1, n_dp):
-        to, back = turn(dp, k, n_dp), turn(dp, -k, n_dp)
-        frames.append(
-            remote(returning.at[:, to], returned.at[:, dp], returned.at[:, back], (to, fsdp))
-        )
-    own_frames = local(returning.at[:, dp], returned.at[:, dp])
-    wait_acts(2)
-    product(4)
-    x_send(4)
-    pl.semaphore_wait(credit.at[1], 1)
-    send_acts(1)
-    pl.semaphore_wait(credit.at[0], 1)
-    send_acts(0)
-    wait_acts(1)
-    for u in (5, 6):
-        product(u)
-        x_send(u)
-    x_add(0)
-    z_send(0)
-    wait_acts(0)
-    for u in (7, 8):
-        product(u)
-        x_send(u)
-
     def xz(u):
         x_add(u)
         z_send(u)
@@ -850,41 +836,353 @@
         z_add(u)
         last_send(u)
 
-    for do, u in (
-        (yx, 2), (xz, 1), (yx, 3), (zl, 0), (xz, 4), (zl, 1), (xz, 5), (zl, 4), (xz, 6), (zl, 5),
-        (xz, 7), (zl, 6), (xz, 8), (zl, 7), (xz, 2), (zl, 8), (xz, 3), (zl, 2), (last_add, 0),
-        (last_add, 1), (last_add, 4), (last_add, 5), (last_add, 6), (last_add, 7), (last_add, 8),
-        (zl, 3), (last_add, 2), (last_add, 3),
-    ):
+
+    def partners():
+        result = []
+        mask = 1
+        while mask < n_b:
+            result.append((dp, a * n_b + (b ^ mask)))
+            mask *= 2
+        mask = 1
+        while mask < n_a:
+            result.append((dp, (a ^ mask) * n_b + b))
+            mask *= 2
+        count = len(result)
+        mask = 1
+        while mask < n_y:
+            result.append(((y ^ mask) * n_c + c, fsdp))
+            mask *= 2
+        result.append(other_core)
+        return result, count
+
+    every_partner, fsdp_count = partners()
+    small = {}
+
+    def exchange(name, step, buf, land, device):
+        small[name, step] = remote(buf.at[step], land.at[step], land.at[step], device)
+
+    def absorb(name, step, buf, land):
+        small[name, step].wait_recv()
+        buf[step + 1] = buf[step] + land[step]
+
+    def gain_step(step):
+        if step > 0:
+            absorb("gains", step - 1, gain_buf, gain_land)
+        if step < len(every_partner):
+            exchange("gains", step, gain_buf, gain_land, every_partner[step])
+
+    def give_credit(index):
+        pl.semaphore_signal(credit.at[index], inc=1, device_id=other_core, device_id_type=MESH)
+
+
+    own = D // n_fsdp
+
+    def gain_row(row):
+        return jnp.concatenate(
+            [gains_all[f, pl.ds(row, 1), pl.ds(0, own)] for f in range(n_fsdp)], axis=1
+        )
+
+    cot_copy.wait()
+
+    def low_body(at):
+        low[at, :] = (frame_weight[at, :] * cot[at, :].astype(F32)).astype(BF16)
+
+    row_loop(tokens, 64, low_body)
+    low_away = remote(low.at[:, far_half(D // n_c)], low_far, low_far, other_core)
+
+    def dot_right(left, right):
+        return lax.dot_general(left, right, (((1,), (1,)), ((), ())), preferred_element_type=F32)
+
+    def add_product(left, weight, first):
+        for start in (0, 512):
+            cols = pl.ds(start, 512)
+            value = dot_right(left, weight[cols, :])
+            acc[:, cols] = value if first else acc[:, cols] + value
+
+    def feed_forward(block):
+        down = (ring_next(), ring_next())
+        for part in range(2):
+            j = 2 * block + part
+            slope_copies[j].wait()
+            rows = pl.ds(part * 512, 512)
+            d_act = dot_right(low[:, :512], down[0][rows, :])
+            d_act += dot_right(low[:, 512:], down[1][rows, :])
+            wide[:, pl.ds(j * 512, 512)] = (d_act * slope_buf[j % 2].astype(F32)).astype(BF16)
+            if j + 2 < 8:
+                slope_load(j + 2)
+        ring_load()
+        ring_load()
+        for part in range(2):
+            j = 2 * block + part
+            add_product(wide[:, pl.ds(j * 512, 512)], ring_next(), j == 0)
+            ring_load()
+
+    feed_forward(0)
+    feed_forward(1)
+    for copy in act_here:
+        copy.wait()
+    for copy in act_away:
+        copy.wait_recv()
+    low_away.wait_recv()
+    for u in (0, 1):
+        product(u, pool_tiles(near), pool_tiles(far), low, low_far)
+        x_send(u)
+    give_credit(0)
+    left_here = [
+        local(two, pool.at[0, near, pl.ds(0, D)]),
+        local(one, pool.at[0, near, pl.ds(D, D)]),
+    ]
+    qkv_here = [
+        local(qkv.at[:, pl.ds(0, D)], pool.at[1, near, pl.ds(0, D)]),
+        local(qkv.at[:, pl.ds(D, D)], pool.at[1, near, pl.ds(D, D)]),
+        local(qkv.at[:, pl.ds(2 * D, D)], pool.at[1, far, pl.ds(0, D)]),
+        local(mixed, pool.at[1, far, pl.ds(D, D)]),
+    ]
+    feed_forward(2)
+    feed_forward(3)
+    pl.semaphore_wait(credit.at[0], 1)
+    there = pool.at[0, far, pl.ds(0, D)]
+    mixed_away = remote(mixed, there, there, other_core)
+    wide_away = remote(wide.at[:, far_half(half_ff)], wide_far, wide_far, other_core)
+    hat_copy.wait()
+    low_away.wait_send()
+    gain_buf[0] = jnp.zeros_like(gain_buf[0])
+    gain_two = gain_row(1)
+
+    def after_body(at):
+        back, grad_gain = norm_back(
+            hat[at, :].astype(F32), scales[at, pl.ds(64, 1)], gain_two, acc[at, :]
+        )
+        d_after = frame_weight[at, :] * cot[at, :].astype(F32) + back
+        hidden[at, :] = d_after
+        low[at, :] = d_after.astype(BF16)
+        gain_buf[0, pl.ds(1, 1), :] += grad_gain
+
+    row_loop(tokens, 64, after_body)
+    after_away = remote(low.at[:, far_half(D // n_c)], low_far, low_far, other_core)
+    hat_copy = local(hat_one, hat)
+    pair = (ring_next(), ring_next())
+    for start in (0, 512):
+        cols = pl.ds(start, 512)
+        value = dot_right(low[:, :512], pair[0][cols, :]) + dot_right(low[:, 512:], pair[1][cols, :])
+        cot[:, cols] = value.astype(BF16)
+    ring_load()
+    ring_load()
+    for copy in left_here + qkv_here:
+        copy.wait()
+    two_away.wait_recv()
+    wide_away.wait_recv()
+    for u in (2, 3):
+        product(u, tiles(pool.at[0], near, 0), tiles(left_far, near, 0), wide, wide_far)
+        y_send(u)
+    mixed_away.wait_recv()
+    after_away.wait_recv()
+    product(4, tiles(pool.at[1], far, D), tiles(pool.at[0], far, 0), low, low_far)
+    give_credit(1)
+    x_send(4)
+    wide_away.wait_send()
+    pl.semaphore_wait(credit.at[1], 1)
+    packed_away = remote(packed, pool.at[0, far], pool.at[0, far], other_core)
+    one_away = remote(one, left_far, left_far, other_core)
+
+    def attend_back(i):
+        rows = pl.ds(i * per_pack, per_pack)
+        rows_far = pl.ds(tokens + i * per_pack, per_pack)
+        position = lax.broadcasted_iota(jnp.int32, (per_pack, per_pack), 0)
+        distance = jnp.abs(
+            position - lax.broadcasted_iota(jnp.int32, (per_pack, per_pack), 1)
+        ).astype(F32)
+        first_head = pair_mask(per_pack)
+
+        @pl.loop(0, HEADS // 2)
+        def _(pair):
+            def cols(first):
+                return pl.ds(pl.multiple_of(first + pair * 2 * HD, 128), 2 * HD)
+
+            same = ids_down[i] == ids_across[i]
+            queries, keys_all = pool[1, rows, cols(0)], pool[1, rows, cols(D)]
+            values_all = pool[1, rows_far, cols(0)]
+            d_mixed = cot[rows, cols(0)]
+            zero = jnp.zeros_like(queries)
+            total = [None, None, None]
+            for head in range(2):
+                mine = first_head if head == 0 else jnp.logical_not(first_head)
+                query, key, d_head = (
+                    jnp.where(mine, value, zero) for value in (queries, keys_all, d_mixed)
+                )
+                probs = head_probs(
+                    query, keys_all, distance, same, slopes[pl.ds(2 * pair + head, 1), :]
+                )
+                d_probs = dot_right(d_head, values_all)
+                carried = jnp.sum(probs * d_probs, axis=-1, keepdims=True)
+                d_scores = (probs * (d_probs - carried)).astype(BF16)
+                contract = (((0,), (0,)), ((), ()))
+                parts = (
+                    jnp.dot(d_scores, key, preferred_element_type=F32),
+                    lax.dot_general(d_scores, query, contract, preferred_element_type=F32),
+                    lax.dot_general(
+                        probs.astype(BF16), d_head, contract, preferred_element_type=F32
+                    ),
+                )
+                total = [p if t is None else t + p for t, p in zip(total, parts)]
+            wide[rows, cols(0)] = (total[0] * HD ** (-0.5)).astype(BF16)
+            wide[rows, cols(D)] = (total[1] * HD ** (-0.5)).astype(BF16)
+            wide[rows, cols(2 * D)] = total[2].astype(BF16)
+
+    attend_back(0)
+    xz(0)
+    attend_back(1)
+    qkv_half = 3 * D // n_c
+    qkv_view = wide_far.at[:, pl.ds(0, qkv_half)]
+    qkv_away = remote(wide.at[:, far_half(qkv_half)], qkv_view, qkv_view, other_core)
+    for part in range(6):
+        add_product(wide[:, pl.ds(part * 512, 512)], ring_next(), part == 0)
+        ring_load()
+    one_away.wait_recv()
+    qkv_away.wait_recv()
+    for u in (5, 6):
+        product(u, tiles(pool.at[0], near, D), tiles(left_far, near, 0), wide, wide_far)
+        x_send(u)
+    packed_here = local(packed, pool.at[0, near])
+    hat_copy.wait()
+    after_away.wait_send()
+    gain_one = gain_row(0)
+
+    def base_body(at):
+        back, grad_gain = norm_back(
+            hat[at, :].astype(F32), scales[at, pl.ds(0, 1)], gain_one, acc[at, :]
+        )
+        low[at, :] = (hidden[at, :] + back).astype(BF16)
+        gain_buf[0, pl.ds(0, 1), :] += grad_gain
+
+    row_loop(tokens, 64, base_body)
+    base_away = remote(low.at[:, far_half(D // n_c)], low_far, low_far, other_core)
+    gain_step(0)
+    qkv_away.wait_send()
+    for half in range(2):
+        pair = (ring_next(), ring_next())
+        for start in (0, 512):
+            cols = pl.ds(start, 512)
+            value = dot_right(low[:, :512], pair[0][cols, :])
+            value += dot_right(low[:, 512:], pair[1][cols, :])
+            wide[:, pl.ds(half * 1024 + start, 512)] = value.astype(BF16)
+        ring_load()
+        ring_load()
+    packed_here.wait()
+    packed_away.wait_recv()
+    base_away.wait_recv()
+    for u in (7, 8):
+        product(u, tiles(pool.at[0], near, 0), tiles(pool.at[0], far, 0), low, low_far)
+    xz(1)
+    slots = back_hot.shape[1] // n_dp
+    slab = n_dp * slots
+    for i in range(micro):
+        for half in range(2):
+            cols = pl.ds(half * 1024, 1024)
+            pool[1, pl.ds(i * slab, slab), cols] = jnp.dot(
+                back_hot[i], wide[pl.ds(i * per_pack, per_pack), cols], preferred_element_type=F32
+            ).astype(BF16)
+    frames = []
+
+    def slot(group, base=0):
+        return pl.ds(pl.multiple_of(base + group * slots, 16), slots)
+
+    for k in range(1, n_dp):
+        to, back = turn(dp, k, n_dp), turn(dp, -k, n_dp)
+        for i in range(micro):
+            frames.append(
+                remote(
+                    pool.at[1, slot(to, i * slab)], returned.at[i, slot(dp)],
+                    returned.at[i, slot(back)], (to, fsdp),
+                )
+            )
+    own_frames = [local(pool.at[1, slot(dp, i * slab)], returned.at[i, slot(dp)]) for i in range(micro)]
+    gain_step(1)
+    yx(2)
+    xz(4)
+    yx(3)
+    x_send(7)
+    x_send(8)
+    steps = [
+        (zl, 0), (zl, 1), (zl, 4), (xz, 5), (last_add, 0), (last_add, 1), (xz, 6), (zl, 5),
+        (last_add, 4), (xz, 2), (zl, 6), (last_add, 5), (xz, 3), (zl, 2), (xz, 7), (zl, 3),
+        (last_add, 6), (last_add, 2), (xz, 8), (zl, 7), (last_add, 3), (last_add, 7), (zl, 8),
+        (last_add, 8),
+    ]
+    step_gain = 2
+    for index, (do, u) in enumerate(steps):
         do(u)
-    for u in range(len(units)):
-        state[u]["core"].wait_recv()
-    final_copies = [local(finals[m], outs[m]) for m in range(count)]
+        if index % 2 == 0 and step_gain <= len(every_partner):
+            gain_step(step_gain)
+            step_gain += 1
+    while step_gain <= len(every_partner):
+        gain_step(step_gain)
+        step_gain += 1
+    outgoing = []
+    square_buf[0] = jnp.zeros_like(square_buf[0])
+
+    def add_squares(m):
+        rows, columns = finals[m].shape
+        chunk = min(32, rows)
+
+        @pl.loop(0, rows // chunk)
+        def _(i):
+            at = pl.ds(pl.multiple_of(i * chunk, chunk), chunk)
+            for first in range(0, columns, 1024):
+                value = finals[m][at, pl.ds(first, 1024)].astype(F32)
+                value = (value * value).reshape(chunk // 8, 8, 8, 128)
+                square_buf[0] += jnp.sum(value, axis=(0, 2))
+
+    for m in (4, 3, 2, 1, 0):
+        for u in range(len(units)):
+            if units[u][0] == m:
+                state[u]["core"].wait_recv()
+        outgoing.append(local(finals[m], outs[m]))
+        add_squares(m)
+    for step in range(fsdp_count):
+        exchange("squares", step, square_buf, square_land, every_partner[step])
+        absorb("squares", step, square_buf, square_land)
+    last = len(every_partner)
+    outgoing.append(local(gain_buf.at[last], gains_out))
+    outgoing.append(local(square_buf.at[fsdp_count], squares_out))
     for copy in frames:
         copy.wait_recv()
-    own_frames.wait()
-    for copy in sent:
+    for copy in own_frames + outgoing:
+        copy.wait()
+    for copy in copies.sent:
         copy.wait_send()
-    for copy in final_copies:
-        copy.wait()
-
-
-def reduce_all(lefts, rights, returning):
+
+
+def backward_all(fulls, saved, cotangent, frame_weight, gains_all, back_hot, source):
     dims = sizes()
     n_y, n_c, n_a, n_b = dims
     n_fsdp = n_a * n_b
-    tokens = lefts[0].shape[0]
-    shapes = [(left.shape[1], right.shape[1]) for left, right in zip(lefts, rights)]
+    tokens = cotangent.shape[0]
+    micro, slab, per_pack = back_hot.shape
+    shapes = [full.shape for full in fulls]
+    shape = jax.ShapeDtypeStruct
     anywhere = pl.BlockSpec(memory_space=pl.ANY)
+    inside = pl.BlockSpec(memory_space=pltpu.VMEM)
+    steps = (n_y * n_c * n_a * n_b).bit_length() - 1
     scratch = [pltpu.VMEM((n_a, n_b, r // n_fsdp, w // n_c), BF16) for r, w in shapes]
     scratch += [pltpu.VMEM((r // n_fsdp, w), BF16) for r, w in shapes]
     scratch += [
-        pltpu.VMEM((2 * tokens, max(shapes[m][0] for m in group)), BF16)
-        for group in ((4, 0), (3, 1), (2,))
-    ]
-    scratch += [
-        pltpu.VMEM((2 * tokens, max(shapes[m][1] // n_c for m in group)), BF16)
-        for group in ((4, 0), (3, 1), (2,))
+        pltpu.VMEM((2, 2 * tokens, FF // 2), BF16),
+        pltpu.VMEM((tokens, D // n_c), BF16),
+        pltpu.VMEM((tokens, FF), BF16),
+        pltpu.VMEM((tokens, FF // n_c), BF16),
+        pltpu.VMEM((tokens, D), BF16),
+        pltpu.VMEM((RING, 1024, 512), BF16),
+        pltpu.VMEM((2, tokens, 512), BF16),
+        pltpu.VMEM((tokens, D), F32),
+        pltpu.VMEM((tokens, D), F32),
+        pltpu.VMEM((tokens, D), BF16),
+        pltpu.VMEM((tokens, D), BF16),
+        pltpu.VMEM((tokens, D), BF16),
+        pltpu.VMEM((steps + 1, 8, D), F32),
+        pltpu.VMEM((steps, 8, D), F32),
+        pltpu.VMEM((steps + 1, 8, 128), F32),
+        pltpu.VMEM((steps, 8, 128), F32),
     ]
     for m, part, parts, shared in REDUCE_UNITS:
         rows, width = shapes[m][0] // n_fsdp, shapes[m][1] // n_c // parts
@@ -899,80 +1197,42 @@
             scratch += [
                 pltpu.VMEM((n_b - 1, n_a, rows, width), BF16),
                 pltpu.VMEM((n_a - 1, rows, width), BF16),
-                pltpu.VMEM((n_y, rows, width), BF16),
+                pltpu.VMEM((1 if n_y == 2 else n_y, rows, width), BF16),
             ]
-    total = 10 + n_y * n_c - 1
+    total = 10 + micro * (n_y * n_c - 1) + 2 * steps
     for _, _, _, shared in REDUCE_UNITS:
         total += (n_b - 1) + (n_a - 1) + (n_y - 1) + 1 + (n_y - 1 if shared else 0)
     scratch += [
         pltpu.SemaphoreType.DMA((total,)),
         pltpu.SemaphoreType.DMA((total,)),
-        pltpu.SemaphoreType.DMA((16,)),
+        pltpu.SemaphoreType.DMA((72,)),
         pltpu.SemaphoreType.REGULAR((2,)),
     ]
-    out_shape = [jax.ShapeDtypeStruct((r // n_fsdp, w), BF16) for r, w in shapes]
-    out_shape.append(jax.ShapeDtypeStruct(returning.shape, returning.dtype))
+    out_shape = [shape((r // n_fsdp, w), BF16) for r, w in shapes]
+    out_shape += [
+        shape((micro, slab, 2 * D), BF16), shape((8, D), F32), shape((8, 128), F32),
+    ]
+    slopes = jnp.exp2(-8.0 * (jnp.arange(HEADS, dtype=F32) + 1.0) / HEADS)
+    slopes = jnp.broadcast_to(slopes[:, None], (HEADS, per_pack))
     results = pl.pallas_call(
-        partial(reduce_kernel, dims, shapes),
+        partial(backward_kernel, dims, shapes),
         out_shape=out_shape,
-        in_specs=[anywhere] * 11,
-        out_specs=[anywhere] * 6,
+        in_specs=[anywhere] * 14 + [inside] + [anywhere] + [inside] * 6,
+        out_specs=[anywhere] * len(out_shape),
         scratch_shapes=scratch,
         compiler_params=pltpu.CompilerParams(
-            has_side_effects=True, vmem_limit_bytes=60 * 2**20
+            has_side_effects=True, vmem_limit_bytes=VMEM_LIMIT
         ),
-        name="reduce_gradients",
-    )(*lefts, *rights, returning)
-    return results[:5], results[5]
-
-
-def sum_over(value, axis, count):
-    mask = 1
-    while mask < count:
-        value = value + swap(value, axis, mask)
-        mask *= 2
-    return value
-
-
-def dot_rows(left, right):
-    return jnp.dot(left, right, preferred_element_type=F32)
-
-
-def dot_right(left, right):
-    return lax.dot_general(left, right, (((1,), (1,)), ((), ())), preferred_element_type=F32)
-
-
-def norm_parts(hidden):
-    centre = hidden - jnp.mean(hidden, axis=-1, keepdims=True)
-    spread = jnp.mean(centre * centre, axis=-1, keepdims=True)
-    scale = lax.rsqrt(spread + NORM_EPSILON)
-    return centre * scale, scale
-
-
-def norm_back(normal, scale, gain_row, gradient):
-    scaled = gradient * gain_row
-    grad_gain = jnp.sum(gradient * normal, axis=0)
-    back = scale * (
-        scaled
-        - jnp.mean(scaled, axis=-1, keepdims=True)
-        - normal * jnp.mean(scaled * normal, axis=-1, keepdims=True)
+        name="backward_and_reduce",
+    )(
+        *fulls, *saved, cotangent, frame_weight, gains_all, back_hot,
+        source[:, :, None], source[:, None, :], slopes,
     )
-    return back, grad_gain
-
-
-def alibi_bias(length):
-    position = jnp.arange(length, dtype=F32)
-    distance = jnp.abs(position[:, None] - position[None, :])
-    slopes = jnp.exp2(-8.0 * (jnp.arange(HEADS, dtype=F32) + 1.0) / HEADS)
-    return -slopes[:, None, None] * distance[None]
-
-
-def attention_scores(queries, keys_all, alibi_terms, same_item):
-    scores = (
-        jnp.einsum("nqhe,nkhe->nhqk", queries, keys_all, preferred_element_type=F32) * HD ** (-0.5)
-        + alibi_terms[None]
-    )
-    return jnp.where(same_item[:, None], scores, -1e30)
+    return results
+
+
+def pick(value, index, axis):
+    return lax.dynamic_index_in_dim(value, index, axis, keepdims=False)
 
 
 def adam_update(master, first, second, gradient, rate, decay):
@@ -1053,73 +1313,23 @@
         (w_skip, w_qkv, w_out, w_up, w_down), payload, low_gains,
         jnp.moveaxis(back.reshape(micro, n_dp * capacity, row_count), 1, 2), source,
     )
-    fulls, results = results[:5], results[5:]
-    used_skip, used_qkv, used_out, used_up, used_down = (
-        full.reshape(-1, full.shape[-1]) for full in fulls
+    fulls, saved, out_frames, gains_all = results[:5], results[5:15], results[15], results[16]
+    fulls = [full.reshape(-1, full.shape[-1]) for full in fulls]
+    results = backward_all(
+        fulls, saved, out_cotangent.reshape(rows, width), weight.reshape(rows, 1), gains_all,
+        back.reshape(micro, n_dp * capacity, row_count), source,
     )
-    packed, base_rows, qkv_rows, mixed, after_attn, up_rows, activated = results[:7]
-    normed_one, normed_two, out_frames, gains_all = results[7:]
-    used_gains = jnp.moveaxis(gains_all[:, :2, :own_gains], 0, 1).reshape(2, width)
-    normal_one, scale_one = norm_parts(base_rows)
-    normal_two, scale_two = norm_parts(after_attn)
-    heads_shape = (micro, row_count, HEADS, HD)
-    queries = qkv_rows[:, :width].reshape(heads_shape)
-    keys_all = qkv_rows[:, width : 2 * width].reshape(heads_shape)
-    values_all = qkv_rows[:, 2 * width :].reshape(heads_shape)
-    alibi_terms = alibi_bias(row_count)
-    same_item = source[:, :, None] == source[:, None, :]
-    gelu_back = jax.vjp(partial(jax.nn.gelu, approximate=True), up_rows)[1]
-
-    d_out = weight.reshape(rows, 1) * out_cotangent.reshape(rows, width).astype(F32)
-    d_out_low = d_out.astype(BF16)
-    d_up = gelu_back(dot_right(d_out_low, used_down))[0].astype(BF16)
-    d_after_norm, grad_gain_two = norm_back(
-        normal_two, scale_two, used_gains[1], dot_right(d_up, used_up)
-    )
-    d_after = d_out + d_after_norm
-    d_after_low = d_after.astype(BF16)
-    d_mixed = dot_right(d_after_low, used_out).astype(BF16).reshape(heads_shape)
-    scores = attention_scores(queries, keys_all, alibi_terms, same_item)
-    probs = jax.nn.softmax(scores, axis=-1)
-    probs_low = probs.astype(BF16)
-    d_probs = jnp.einsum("nqhe,nkhe->nhqk", d_mixed, values_all, preferred_element_type=F32)
-    d_values = jnp.einsum("nhqk,nqhe->nkhe", probs_low, d_mixed, preferred_element_type=F32)
-    d_scores = (probs * (d_probs - jnp.sum(probs * d_probs, axis=-1, keepdims=True))).astype(BF16)
-    d_queries = jnp.einsum("nhqk,nkhe->nqhe", d_scores, keys_all, preferred_element_type=F32)
-    d_keys = jnp.einsum("nhqk,nqhe->nkhe", d_scores, queries, preferred_element_type=F32)
-    d_qkv = jnp.concatenate(
-        [
-            (d_queries * HD ** (-0.5)).reshape(rows, width),
-            (d_keys * HD ** (-0.5)).reshape(rows, width),
-            d_values.reshape(rows, width),
-        ],
-        axis=1,
+    gradients, returned, grad_gains, squares = results[:5], results[5], results[6], results[7]
+    in_gradient = jnp.einsum(
+        "bsr,bsw->brw", send.reshape(micro, n_dp * capacity, source_rows), returned,
+        preferred_element_type=F32,
     ).astype(BF16)
-    d_base_norm, grad_gain_one = norm_back(
-        normal_one, scale_one, used_gains[0], dot_right(d_qkv, used_qkv)
-    )
-    d_base_low = (d_after + d_base_norm).astype(BF16)
-    d_packed = dot_right(d_base_low, used_skip).astype(BF16).reshape(micro, row_count, 2 * width)
-    returning = jnp.einsum("bpst,btw->bpsw", back, d_packed, preferred_element_type=F32).astype(BF16)
-    (grad_skip, grad_qkv, grad_out, grad_up, grad_down), returned = reduce_all(
-        (packed, normed_one, mixed, normed_two, activated),
-        (d_base_low, d_qkv, d_after_low, d_up, d_out_low),
-        returning,
-    )
-    in_gradient = jnp.einsum("bpsr,bpsw->brw", send, returned, preferred_element_type=F32)
-    in_gradient = in_gradient.astype(BF16)
     input_gradient, skip_gradient = in_gradient[..., :width], in_gradient[..., width:]
-
-    grad_gains = lax.psum(jnp.stack([grad_gain_one, grad_gain_two]), ("dp", "fsdp"))
+    grad_gains = grad_gains[:2]
+    total_squares = jnp.sum(squares) + jnp.sum(grad_gains * grad_gains)
+    gradient_norm = jnp.sqrt(total_squares)
     grad_gains = pick(grad_gains.reshape(2, n_fsdp, own_gains), fsdp, 1)
-
-    gradients = [g.astype(F32) for g in (grad_skip, grad_qkv, grad_out, grad_up, grad_down)]
-    gradients.append(grad_gains)
-    squares = jnp.float32(0.0)
-    for gradient in gradients:
-        squares = squares + jnp.sum(gradient * gradient)
-    squares = sum_over(sum_over(jnp.full((8, 128), squares), "b", n_b), "a", n_a)
-    gradient_norm = jnp.sqrt(squares[0, 0])
+    gradients = [gradient.astype(F32) for gradient in gradients] + [grad_gains]
     param_count = 6 * D * D + 2 * D * FF + 2 * D
     clip = jnp.minimum(1.0, 0.02 * math.sqrt(param_count) / gradient_norm)
     grad_skip, grad_qkv, grad_out, grad_up, grad_down, grad_gains = [clip * g for g in gradients]

time: 595 us -> 454 us (0.76)
  matrix products: 64.2 us -> 9.41 us
  local copies, waits for them, and re-layouts: 64.9 us -> 11.2 us
  Pallas kernels: 358 us -> 399 us
  blocking collectives: 40.4 us -> 0 us
  other arithmetic: 48.5 us -> 28.4 us
    dot_general x11 -> x1, matrix products: 51.3 us -> 4.52 us  [on_device(): jnp.einsum('bsr,bsw->brw', send.reshape(micro, n_dp * capacity, source_ro...]
    reshape x13 -> x0, local copies, waits for them, and re-layouts: 43.5 us -> none  [the longest x2 8.1 us: on_device(): d_values.reshape(rows, width)]
    pallas_call x1, Pallas kernels: 190 us -> 231 us  [backward_all(): pl.pallas_call(partial(backward_kernel, dims, shapes), out_shape=out_shap...]
    psum x1 -> x0, blocking collectives: 40.4 us -> none  [on_device(): lax.psum(jnp.stack([grad_gain_one, grad_gain_two]), ('dp', 'fsdp'))]
    reduce_sum x10 -> x1, other arithmetic: 12.7 us -> 1.28 us  [on_device(): total_squares = jnp.sum(squares) + jnp.sum(grad_gains * grad_gains)]
    sub x1 -> x0, matrix products: 7.19 us -> none  [on_device(): probs = jax.nn.softmax(scores, axis=-1)]
    convert_element_type x4 -> x0, other arithmetic: 6.55 us -> none  [the longest x1 3.86 us: on_device(): d_after_low = d_after.astype(BF16)]
    unnamed x115 -> x53, local copies, waits for them, and re-layouts: 12.1 us -> 5.84 us
  transfers between devices with their start and end apart: 3 -> 0, of which waited for: 2 -> 0; matrix products, arithmetic and copies ran while one was open for 1% -> 0% of each run, Pallas kernels for 0% -> 0%
where the time goes in v3:
time: 454 us; the launch traced here: 451 us
  Pallas kernels  399 us (88%)
  other arithmetic  28.4 us (6%)
  local copies, waits for them, and re-layouts  11.2 us (2%)
  matrix products  9.41 us (2%)
    pallas_call x1, Pallas kernels, backward_all(): pl.pallas_call(partial(backward_kernel, dims, shapes), out_shape=out_shap...  231 us
    pallas_call x1, Pallas kernels, forward_all(): pl.pallas_call(partial(forward_kernel, dims), out_shape=out_shape, in_spe...  168 us
    convert_element_type x5, other arithmetic, on_device(): results.append(new[0].astype(BF16))  17.7 us

profile of v3, /device:TPU:0, one launch (start us, length us, event | category | flops | bytes accessed | tf_op | source)
XLA Modules:
  0.0 451.3 jit_solution(15498454517423009609)
XLA Ops:
  1.4 0.7 constant_dynamic-slice_fusion
  2.5 0.9 select_reduce_fusion.3
  5.6 0.9 copy.72
  6.5 0.9 copy.61.refs_8_.refs_19_
  7.4 1.1 fusion.29.refs_18_
  8.5 1.0 fusion.27.refs_7_
  9.5 3.3 fusion.16
  12.8 1.6 fusion.11
  14.4 2.4 pad_maximum_fusion.refs_5_
  16.8 167.7 %gather_and_forward.1 = (bf16[4,2,256,1024]{3,2,1,0:T(8,128)(2,1)}, bf16[4,2,128,3072]{3,2,1,0:T(8,128)(2,1)}, bf16[4,2,128,1024]{3,2,1,0:T(8,128)(2,1)}, bf16[4...) custom-call(f32[256,1024]{1,0:T(8,128)} %refs_0_.1, ...), custom_call_target="tpu_custom_call" | custom-call | tf_op jit(solution)/shard_map/gather_and_forward/pallas_call | solution.py:518
  184.5 230.9 %backward_and_reduce.1 = (bf16[256,1024]{1,0:T(8,128)(2,1)}, bf16[128,3072]{1,0:T(8,128)(2,1)}, bf16[128,1024]{1,0:T(8,128)(2,1)}, bf16[128,4096]{1,0:T(8,128)(2...) custom-call(bf16[2048,1024]{1,0:T(8,128)(2,1)} %bitcast.59, ...), custom_call_target="tpu_custom_call" | custom-call | tf_op jit(solution)/shard_map/backward_and_reduce/pallas_call | solution.py:1217
  415.4 1.3 reduce_sum.98
  416.7 4.5 %convolution_convert_fusion = bf16[2,512,2048]{2,1,0:T(8,128)(2,1)S(1)} fusion(bf16[2,512,2048]{2,1,0:T(8,128)(2,1)} %get-tuple-element.81, s32[2,512]{1,0:T(2,128)S(1)} %get-tuple-element.126, pred[2,512]{1,0:T(4,128)(4,1)S(1)} %get-tuple-element.124), kind=kOutput, calls=%fused_computation.1 | convolution fusion | flops 2150629376 | bytes 8393728 | tf_op jit(solution)/shard_map/bsr,bsw->brw/dot_general | solution.py:1323
  421.3 2.5 fusion.48
  423.8 1.5 slice_bitcast_fusion
  427.4 2.6 fusion.41
  430.0 2.5 fusion.45
  432.9 0.8 copy-done.10
  433.9 3.6 fusion.43
  437.4 1.3 copy-done.6
  438.9 4.7 %fusion.37 = (bf16[512,1024]{1,0:T(8,128)(2,1)}, f32[512,1024]{1,0:T(8,128)}, f32[512,1024]{1,0:T(8,128)}, f32[512,1024]{1,0:T(8,128)}) fusion(f32[512,1024]{1,0:T(8,128)S(1)} %copy-done, bf16[512,1024]{1,0:T(8,128)(2,1)S(1)} %copy-done.12, f32[]{:T(128)S(6)} %min.3, f32[512,1024]{1,0:T(8,128)S(1)} %copy-done.5, f32[512,1024]{1,0:T(8,128)S(1)} %copy-done.6), kind=kLoop, calls=%fused_computation.86 | loop fusion | flops 8912896 | bytes 14680068 | tf_op jit(solution)/shard_map/convert_element_type | solution.py:1348
  443.8 0.8 copy-done.11
  444.6 4.4 fusion.39
  449.0 1.0 copy.78
  (65 shorter events, 4.9 us)
Async XLA Ops:
  9.5 3.3 copy-start.23
  421.3 5.5 %copy-start.20 = (f32[2,128]{1,0:T(2,128)S(1)}, f32[2,128]{1,0:T(2,128)}, u32[]{:S(2)}) copy-start(f32[2,128]{1,0:T(2,128)} %param.34) | copy-start | bytes 3076
  421.3 5.5 %copy-start.21 = (f32[2,128]{1,0:T(2,128)S(1)}, f32[2,128]{1,0:T(2,128)}, u32[]{:S(2)}) copy-start(f32[2,128]{1,0:T(2,128)} %param.40) | copy-start | bytes 3076
  421.3 5.5 %copy-start.22 = (f32[2,128]{1,0:T(2,128)S(1)}, f32[2,128]{1,0:T(2,128)}, u32[]{:S(2)}) copy-start(f32[2,128]{1,0:T(2,128)} %param.46) | copy-start | bytes 3076
  421.3 6.1 %copy-start.4 = (f32[128,1024]{1,0:T(8,128)S(1)}, f32[128,1024]{1,0:T(8,128)}, u32[]{:S(2)}) copy-start(f32[128,1024]{1,0:T(8,128)} %refs_2_.1) | copy-start | bytes 1572868
  421.3 6.1 %copy-start.17 = (f32[128,1024]{1,0:T(8,128)S(1)}, f32[128,1024]{1,0:T(8,128)}, u32[]{:S(2)}) copy-start(f32[128,1024]{1,0:T(8,128)} %param.43) | copy-start | bytes 1572868
  421.3 6.1 %copy-start.19 = (bf16[128,1024]{1,0:T(8,128)(2,1)S(1)}, bf16[128,1024]{1,0:T(8,128)(2,1)}, u32[]{:S(2)}) copy-start(bf16[128,1024]{1,0:T(8,128)(2,1)} %get-tuple-element.86) | copy-start | bytes 786436
  423.8 6.2 %copy-start.3 = (f32[256,1024]{1,0:T(8,128)S(1)}, f32[256,1024]{1,0:T(8,128)}, u32[]{:S(2)}) copy-start(f32[256,1024]{1,0:T(8,128)} %refs_0_.1) | copy-start | bytes 3145732
  423.8 6.2 %copy-start.14 = (f32[256,1024]{1,0:T(8,128)S(1)}, f32[256,1024]{1,0:T(8,128)}, u32[]{:S(2)}) copy-start(f32[256,1024]{1,0:T(8,128)} %param.41) | copy-start | bytes 3145732
  426.7 3.3 copy-start.15
  426.7 3.3 copy-start.18
  430.0 2.6 copy-start.2
  430.0 2.8 copy-start.9
  430.0 3.7 copy-start.10
  430.0 3.8 copy-start.16
  433.9 3.6 copy-start
  433.9 3.6 copy-start.5
  433.9 4.8 %copy-start.6 = (f32[512,1024]{1,0:T(8,128)S(1)}, f32[512,1024]{1,0:T(8,128)}, u32[]{:S(2)}) copy-start(f32[512,1024]{1,0:T(8,128)} %param.51) | copy-start | bytes 6291460
  433.9 5.0 %copy-start.12 = (bf16[512,1024]{1,0:T(8,128)(2,1)S(1)}, bf16[512,1024]{1,0:T(8,128)(2,1)}, u32[]{:S(2)}) copy-start(bf16[512,1024]{1,0:T(8,128)(2,1)} %get-tuple-element.88) | copy-start | bytes 3145732
  438.9 4.7 %copy-start.1 = (f32[128,4096]{1,0:T(8,128)S(1)}, f32[128,4096]{1,0:T(8,128)}, u32[]{:S(2)}) copy-start(f32[128,4096]{1,0:T(8,128)} %refs_3_.1) | copy-start | bytes 6291460
  438.9 4.7 %copy-start.7 = (f32[128,4096]{1,0:T(8,128)S(1)}, f32[128,4096]{1,0:T(8,128)}, u32[]{:S(2)}) copy-start(f32[128,4096]{1,0:T(8,128)} %param.44) | copy-start | bytes 6291460
  438.9 4.9 %copy-start.8 = (f32[128,4096]{1,0:T(8,128)S(1)}, f32[128,4096]{1,0:T(8,128)}, u32[]{:S(2)}) copy-start(f32[128,4096]{1,0:T(8,128)} %param.50) | copy-start | bytes 6291460
  438.9 5.6 %copy-start.11 = (bf16[128,4096]{1,0:T(8,128)(2,1)S(1)}, bf16[128,4096]{1,0:T(8,128)(2,1)}, u32[]{:S(2)}) copy-start(bf16[128,4096]{1,0:T(8,128)(2,1)} %get-tuple-element.87) | copy-start | bytes 3145732
  444.6 4.4 copy-start.13
